TPU v7x, 32 devices: a whole 2x2x4 slice. The times are simulated.
32 devices in a mesh: seq: 8 (over z, x), head: 4 (over y, core).
Axes of the slice: x: 2, y: 2, z: 4, core: 2. Of those that a mesh axis runs over, the one named last changes fastest.
Arguments:
- queries: bfloat16 [8192, 1024], P('seq', 'head'), may hold values from -6 to 6
- keys: bfloat16 [8192, 512], P('seq', 'head'), may hold values from -6 to 6
- values: bfloat16 [8192, 512], P('seq', 'head'), may hold values from -6 to 6
- grad_out: bfloat16 [8192, 1024], P('seq', 'head'), may hold values from -6 to 6
- starts: int32 [64], P('seq'), may hold values 0 or 1
Outputs:
- grad_queries: bfloat16 [8192, 1024], P('seq', 'head')
- grad_keys: bfloat16 [8192, 512], P('seq', 'head')
- grad_values: bfloat16 [8192, 512], P('seq', 'head')
Inputs may be any that keep to these rules, and one draw needn't show every extreme that they name: `starts`: blocks of 128 tokens, in storage order.
All inputs are finite; a program needn't handle non-finite values.
Results may differ from a plain program's by a relative error of at most 0.0087.
Values may be sent and summed in bfloat16 or wider, within the bound.
No kernel may reach another device: no remote copies, remote signals or barrier semaphores. Data moves between devices by JAX's collectives and lax.ppermute only.
A program may use at most 64 MiB of HBM per device.

v0:
```python
import jax
import jax.numpy as jnp
from jax import lax
from jax.sharding import PartitionSpec as P

HEAD_SIZE = 128
WINDOW = 1024
QUERY_PER_KEY = 2
BLOCK = 128


query_scaling = 168.0 ** (-0.5)


def padded_2(shard, sides, width):
    for axis, dim in sides:
        count, length = (lax.axis_size(axis), shard.shape[dim])
        up = [(i, (i + 1) % count) for i in range(count - 1)]
        down = [(j, i) for i, j in up]
        last = lax.slice_in_dim(shard, length - width, length, axis=dim)
        first = lax.slice_in_dim(shard, 0, width, axis=dim)
        before = lax.ppermute(last, axis, up)
        after = lax.ppermute(first, axis, down)
        shard = jnp.concatenate([before, shard, after], axis=dim)
    return shard


def pack_piece(key_rows, value_rows, block_starts):
    joined = jnp.concatenate([key_rows, value_rows], axis=1)
    filler = jnp.zeros((joined.shape[1] - block_starts.shape[0],), jnp.bfloat16)
    marker = jnp.concatenate([block_starts.astype(jnp.bfloat16), filler])
    return jnp.concatenate([joined, marker[None, :]], axis=0)


def preceding_pieces(front_half, back_half, at_fold):
    stacked = jnp.stack([back_half, front_half])
    padded = padded_2(stacked, (("seq", 0),), 1)
    from_left = padded[0]
    from_right = padded[3]
    before_back = jnp.where(at_fold, front_half, from_right)
    return (from_left, before_back)


def return_grads(grad_front, grad_back, at_fold):
    fold_part = jnp.where(at_fold, grad_back, 0.0)
    sent_back = jnp.where(at_fold, 0.0, grad_back)
    stacked = jnp.stack([grad_front, sent_back])
    padded = padded_2(stacked, (("seq", 0),), 1)
    to_front = padded[3] + fold_part
    to_back = padded[0]
    return (to_front, to_back)


def piece_mask(piece_id, block_starts, length):
    counts = jnp.cumsum(block_starts)
    key_doc = jnp.repeat(counts, BLOCK)
    query_doc = key_doc[2 * length :]
    key_pos = (piece_id - 2) * length + jnp.arange(3 * length, dtype=jnp.int32)
    query_pos = piece_id * length + jnp.arange(length, dtype=jnp.int32)
    offset = query_pos[:, None] - key_pos[None, :]
    return (
        (offset >= 0)
        & (offset < WINDOW)
        & (key_pos[None, :] >= 0)
        & (query_doc[:, None] == key_doc[None, :])
    )


def half_grads(
    piece_id, query_rows_local, gradient_rows, older_piece, nearer_piece, own_piece, width
):
    length = query_rows_local.shape[0]
    blocks = length // BLOCK
    pieces = [older_piece, nearer_piece, own_piece]
    key_all = jnp.concatenate([p[:length, :width] for p in pieces])
    val_all = jnp.concatenate([p[:length, width:] for p in pieces])
    block_starts = jnp.concatenate([p[length, :blocks].astype(jnp.int32) for p in pieces])
    allowed = piece_mask(piece_id, block_starts, length)
    dq_parts = []
    dk_sum = jnp.zeros(key_all.shape, jnp.float32)
    dv_sum = jnp.zeros(val_all.shape, jnp.float32)
    for member in range(QUERY_PER_KEY):
        query_h = query_rows_local[:, member * HEAD_SIZE : (member + 1) * HEAD_SIZE]
        gradout_h = gradient_rows[:, member * HEAD_SIZE : (member + 1) * HEAD_SIZE]
        scores = (
            jnp.einsum("qd,kd->qk", query_h, key_all, preferred_element_type=jnp.float32)
            * query_scaling
        )
        masked = jnp.where(allowed, scores, -jnp.inf)
        row_max = jnp.max(masked, axis=1, keepdims=True)
        exp_terms = jnp.where(allowed, jnp.exp(scores - row_max), 0.0)
        weights = exp_terms / jnp.sum(exp_terms, axis=1, keepdims=True)
        weights_bfloat = weights.astype(jnp.bfloat16)
        dweights = jnp.einsum("qd,kd->qk", gradout_h, val_all, preferred_element_type=jnp.float32)
        row_dot = jnp.sum(weights * dweights, axis=1, keepdims=True)
        score_gradient = (weights * (dweights - row_dot)).astype(jnp.bfloat16)
        dq_parts.append(
            (
                jnp.dot(score_gradient, key_all, preferred_element_type=jnp.float32) * query_scaling
            ).astype(jnp.bfloat16)
        )
        dk_sum = (
            dk_sum
            + jnp.einsum("qk,qd->kd", score_gradient, query_h, preferred_element_type=jnp.float32)
            * query_scaling
        )
        dv_sum = dv_sum + jnp.einsum(
            "qk,qd->kd", weights_bfloat, gradout_h, preferred_element_type=jnp.float32
        )
    dk_cols = [dk_sum]
    dv_cols = [dv_sum]
    grad_q = jnp.concatenate(dq_parts, axis=1)
    grad_all = jnp.concatenate(dk_cols + dv_cols, axis=1)
    return (grad_q, grad_all[:length], grad_all[length : 2 * length], grad_all[2 * length :])


def on_device(queries, keys, values, grad_out, starts):
    length = keys.shape[0] // 2
    blocks = starts.shape[0] // 2
    width = keys.shape[1]
    seq_index = lax.axis_index("seq")
    seq_total = lax.axis_size("seq")
    at_fold = seq_index == seq_total - 1
    front_half = pack_piece(keys[:length], values[:length], starts[:blocks])
    back_half = pack_piece(keys[length:], values[length:], starts[blocks:])
    near_front, near_back = preceding_pieces(front_half, back_half, at_fold)
    far_front, far_back = preceding_pieces(near_front, near_back, at_fold)
    front_dq, front_far, front_near, front_own = half_grads(
        seq_index, queries[:length], grad_out[:length], far_front, near_front, front_half, width
    )
    back_dq, back_far, back_near, back_own = half_grads(
        2 * seq_total - 1 - seq_index,
        queries[length:],
        grad_out[length:],
        far_back,
        near_back,
        back_half,
        width,
    )
    grad_q = jnp.concatenate([front_dq, back_dq])
    up_front, up_back = return_grads(front_far, back_far, at_fold)
    to_front, to_back = return_grads(front_near + up_front, back_near + up_back, at_fold)
    total_front = front_own + to_front
    total_back = back_own + to_back
    key_gradient = jnp.concatenate([total_front[:, :width], total_back[:, :width]]).astype(
        jnp.bfloat16
    )
    value_gradient = jnp.concatenate([total_front[:, width:], total_back[:, width:]]).astype(
        jnp.bfloat16
    )
    return (grad_q, key_gradient, value_gradient)


def solution(mesh):
    in_specs = (P("seq", "head"), P("seq", "head"), P("seq", "head"), P("seq", "head"), P("seq"))
    out_specs = (P("seq", "head"), P("seq", "head"), P("seq", "head"))
    return jax.shard_map(
        on_device, mesh=mesh, in_specs=in_specs, out_specs=out_specs, check_vma=False
    )
```

profile of v0, /device:TPU:0, one launch (start us, length us, event | category | flops | bytes accessed | tf_op | source)
XLA Modules:
  0.0 147.0 jit_solution(14405805594431324461)
XLA Ops:
  7.4 7.0 %collective-permute-done.2 = bf16[1,513,256]{2,1,0:T(8,128)(2,1)S(1)} collective-permute-done((bf16[1,513,256]{2,1,0:T(8,128)(2,1)S(1)}, bf16[1,513,256]{2,1,0:T(8,128)(2,1)S(1)}, u32[]{:S(2)}, u32[]{:S(2)}) %collective-permute-start.2) | collective-permute-done | bytes 262688 | tf_op jit(solution)/shard_map/ppermute | solution.py:23
  14.5 4.6 %collective-permute-start = (bf16[1,513,256]{2,1,0:T(8,128)(2,1)S(1)}, bf16[1,513,256]{2,1,0:T(8,128)(2,1)S(1)}, u32[]{:S(2)}, u32[]{:S(2)}) collective-permute-start(bf16[1,513,256]{2,1,0:T(8,128)(2,1)S(1)} %get-tuple-element.22), channel_id=1, source_target_pairs={{0,4},{4,8},{8,12},{12,16},{16,20},{20,24},{24,28},{1,5},{5,9},{9,... | collective-permute-start | bytes 787976 | tf_op jit(solution)/shard_map/ppermute | solution.py:22
  21.2 8.3 %collective-permute-done = bf16[1,513,256]{2,1,0:T(8,128)(2,1)S(1)} collective-permute-done((bf16[1,513,256]{2,1,0:T(8,128)(2,1)S(1)}, bf16[1,513,256]{2,1,0:T(8,128)(2,1)S(1)}, u32[]{:S(2)}, u32[]{:S(2)}) %collective-permute-start) | collective-permute-done | bytes 262688 | tf_op jit(solution)/shard_map/ppermute | solution.py:22
  32.1 1.6 %fusion.3 = f32[512,1536]{0,1:T(8,128)S(1)} fusion(bf16[1024,256]{1,0:T(8,128)(2,1)} %param.5, bf16[512,128]{1,0:T(8,128)(2,1)S(1)} %get-tuple-element.29, bf16[512,128]{1,0:T(8,128)(2,1)} %get-tuple-element.20, bf16[512,128]{1,0:T(8,128)(2,1)} %get-tuple-element.18), kind=kOutput, calls=%fused_computation.11 | convolution fusion | flops 203292672 | bytes 3670016 | tf_op jit(solution)/shard_map/qd,kd->qk/dot_general | solution.py:86
  33.8 2.4 %select_reduce_fusion.1 = (f32[512]{0:T(512)S(1)}, f32[512,1536]{0,1:T(8,128)S(1)}) fusion(s32[1536]{0:T(1024)S(1)} %broadcast_bitcast_fusion, s32[512]{0:T(512)S(1)} %broadcast_bitcast_fusion.2, pred[1536]{0:T(1024)(128)(4,1)} %broadcast_compare_fusion, s32[1536]{0:T(1024)S(1)} %iota_add_fusion, s32[512]{0:T(512)} %iota_add_fusion.2, ...), kind=kOutput, calls=%fused_computation.23 | convolution fusion | flops 210370048 | bytes 3690496 | tf_op jit(solution)/shard_map/qd,kd->qk/dot_general | solution.py:86
  36.2 2.0 %fusion.17 = f32[512]{0:T(512)S(1)} fusion(f32[512,1536]{0,1:T(8,128)S(1)} %get-tuple-element.39, f32[512]{0:T(512)S(1)} %get-tuple-element.38, s32[1536]{0:T(1024)S(1)} %broadcast_bitcast_fusion, s32[512]{0:T(512)S(1)} %broadcast_bitcast_fusion.2, pred[1536]{0:T(1024)(128)(4,1)S(1)} %copy-done.25, s32[1536]{0:T(1024)S(1)} %iota_add_fusion, s32[512]{0:T(512)S(1)} %copy-done.28), kind=kLoop, calls=%fused_computation.49 | loop fusion | flops 7863808 | bytes 3167744 | tf_op jit(solution)/shard_map/reduce_sum | solution.py:92
  38.2 3.4 %fusion.21 = f32[1536,128]{0,1:T(8,128)} fusion(bf16[1024,256]{1,0:T(8,128)(2,1)S(1)} %copy-done.39, f32[512,1536]{0,1:T(8,128)S(1)} %get-tuple-element.39, f32[512]{0:T(512)S(1)} %fusion.17, f32[512]{0:T(512)S(1)} %get-tuple-element.38, s32[512]{0:T(512)S(1)} %broadcast_bitcast_fusion.2, s32[1536]{0:T(1024)S(1)} %iota_add_fusion, s32[512]{0:T(512)S(1)} %copy-done.28, ...), kind=kOutput, calls=%fused_computation.61 | convolution fusion | flops 209977344 | bytes 4089856 | tf_op jit(solution)/shard_map/qk,qd->kd/dot_general | solution.py:107
  41.6 2.2 %multiply_reduce_fusion.1 = (f32[512]{0:T(512)S(1)}, f32[512]{0:T(512)S(1)}, f32[512,1536]{0,1:T(8,128)S(1)}) fusion(f32[512]{0:T(512)S(1)} %fusion.17, f32[512,1536]{0,1:T(8,128)S(1)} %get-tuple-element.39, f32[512]{0:T(512)S(1)} %get-tuple-element.38, s32[1536]{0:T(1024)S(1)} %broadcast_bitcast_fusion, s32[512]{0:T(512)S(1)} %broadcast_bitcast_fusion.2, ...), kind=kOutput, calls=%fused_computation.21 | convolution fusion | flops 213515264 | bytes 9992192 | tf_op jit(solution)/shard_map/qd,kd->qk/dot_general | solution.py:94
  43.8 2.8 %multiply_convert_fusion.1 = (bf16[512,1536]{0,1:T(8,128)(2,1)S(1)}, f32[512]{0:T(512)S(1)}) fusion(f32[512,1536]{0,1:T(8,128)S(1)} %get-tuple-element.40, f32[512]{0:T(512)S(1)} %get-tuple-element.8, f32[512]{0:T(512)S(1)} %fusion.17, f32[512,1536]{0,1:T(8,128)S(1)} %get-tuple-element.39, f32[512]{0:T(512)S(1)} %get-tuple-element.38, ...), kind=kLoop, calls=%fused_computation.20 | loop fusion | flops 12582400 | bytes 11038208 | tf_op jit(solution)/shard_map/convert_element_type | solution.py:96
  46.7 1.9 %multiply_reduce_fusion = (f32[512]{0:T(512)S(1)}, f32[512,1536]{0,1:T(8,128)S(1)}) fusion(f32[512]{0:T(512)S(1)} %get-tuple-element.35, f32[512,1536]{0,1:T(8,128)S(1)} %fusion.3, f32[512]{0:T(512)S(1)} %get-tuple-element.9, s32[1536]{0:T(1024)S(1)} %broadcast_bitcast_fusion, s32[512]{0:T(512)S(1)} %broadcast_bitcast_fusion.2, ...), kind=kOutput, calls=%fused_computation.17 | convolution fusion | flops 211942912 | bytes 6844416 | tf_op jit(solution)/shard_map/qd,kd->qk/dot_general | solution.py:94
  49.3 2.4 %multiply_convert_fusion = bf16[512,1536]{0,1:T(8,128)(2,1)S(1)} fusion(f32[512,1536]{0,1:T(8,128)S(1)} %get-tuple-element.42, f32[512]{0:T(512)S(1)} %get-tuple-element.41, f32[512]{0:T(512)S(1)} %get-tuple-element.35, f32[512,1536]{0,1:T(8,128)S(1)} %fusion.3, f32[512]{0:T(512)S(1)} %get-tuple-element.9, s32[1536]{0:T(1024)S(1)} %broadcast_bitcast_fusion, ...), kind=kLoop, calls=%fused_computation.16 | loop fusion | flops 10223616 | bytes 7888384 | tf_op jit(solution)/shard_map/convert_element_type | solution.py:96
  51.7 1.6 %fusion.11 = f32[1536,128]{0,1:T(8,128)} fusion(f32[1536,128]{0,1:T(8,128)S(1)} %fusion.48, bf16[512,1536]{0,1:T(8,128)(2,1)S(1)} %multiply_convert_fusion, bf16[1024,256]{1,0:T(8,128)(2,1)S(1)} %copy-done.6), kind=kOutput, calls=%fused_computation.43 | convolution fusion | flops 201719808 | bytes 3276800 | tf_op jit(solution)/shard_map/qk,qd->kd/dot_general | solution.py:104
  53.3 4.6 %collective-permute-start.1 = (bf16[1,513,256]{2,1,0:T(8,128)(2,1)S(1)}, bf16[1,513,256]{2,1,0:T(8,128)(2,1)S(1)}, u32[]{:S(2)}, u32[]{:S(2)}) collective-permute-start(bf16[1,513,256]{2,1,0:T(8,128)(2,1)S(1)} %copy-done.9), channel_id=1, source_target_pairs={{0,4},{4,8},{8,12},{12,16},{16,20},{20,24},{24,28},{1,5},{5,9},{9,... | collective-permute-start | bytes 787976 | tf_op jit(solution)/shard_map/ppermute | solution.py:22
  59.0 2.6 %collective-permute-done.1 = bf16[1,513,256]{2,1,0:T(8,128)(2,1)S(1)} collective-permute-done((bf16[1,513,256]{2,1,0:T(8,128)(2,1)S(1)}, bf16[1,513,256]{2,1,0:T(8,128)(2,1)S(1)}, u32[]{:S(2)}, u32[]{:S(2)}) %collective-permute-start.1) | collective-permute-done | bytes 262688 | tf_op jit(solution)/shard_map/ppermute | solution.py:22
  62.9 1.3 reduce-window.12
  65.9 1.6 %fusion.1 = f32[512,1536]{0,1:T(8,128)S(1)} fusion(bf16[1024,256]{1,0:T(8,128)(2,1)} %param.5, bf16[512,128]{1,0:T(8,128)(2,1)S(1)} %get-tuple-element.28, bf16[512,128]{1,0:T(8,128)(2,1)} %get-tuple-element.16, bf16[512,128]{1,0:T(8,128)(2,1)} %get-tuple-element.14), kind=kOutput, calls=%fused_computation.9 | convolution fusion | flops 203292672 | bytes 3670016 | tf_op jit(solution)/shard_map/qd,kd->qk/dot_general | solution.py:86
  67.5 1.5 %select_reduce_fusion.3 = (f32[512]{0:T(512)S(1)}, f32[512,1536]{0,1:T(8,128)S(1)}) fusion(s32[1536]{0:T(1024)S(1)} %broadcast_bitcast_fusion.1, s32[512]{0:T(512)S(1)} %broadcast_bitcast_fusion.3, pred[1536]{0:T(1024)(128)(4,1)S(1)} %copy-done.27, s32[1536]{0:T(1024)S(1)} %iota_add_fusion.1, s32[512]{0:T(512)S(1)} %copy-done.30, ...), kind=kOutput, calls=%fused_computation.31 | convolution fusion | flops 210370048 | bytes 3694592 | tf_op jit(solution)/shard_map/qd,kd->qk/dot_general | solution.py:86
  69.0 2.0 %fusion.13 = f32[512]{0:T(512)S(1)} fusion(f32[512,1536]{0,1:T(8,128)S(1)} %get-tuple-element.44, f32[512]{0:T(512)S(1)} %get-tuple-element.43, s32[1536]{0:T(1024)S(1)} %broadcast_bitcast_fusion.1, s32[512]{0:T(512)S(1)} %broadcast_bitcast_fusion.3, pred[1536]{0:T(1024)(128)(4,1)S(1)} %copy-done.27, s32[1536]{0:T(1024)S(1)} %iota_add_fusion.1, ...), kind=kLoop, calls=%fused_computation.45 | loop fusion | flops 7863808 | bytes 3167744 | tf_op jit(solution)/shard_map/reduce_sum | solution.py:92
  71.0 2.0 %fusion.24 = f32[1536,128]{0,1:T(8,128)S(1)} fusion(bf16[1024,256]{1,0:T(8,128)(2,1)S(1)} %copy-done.40, f32[512,1536]{0,1:T(8,128)S(1)} %get-tuple-element.44, f32[512]{0:T(512)S(1)} %fusion.13, f32[512]{0:T(512)S(1)} %get-tuple-element.43, s32[512]{0:T(512)S(1)} %broadcast_bitcast_fusion.3, s32[1536]{0:T(1024)S(1)} %iota_add_fusion.1, ...), kind=kOutput, calls=%fused_computation.64 | convolution fusion | flops 209977344 | bytes 4089856 | tf_op jit(solution)/shard_map/qk,qd->kd/dot_general | solution.py:107
  73.0 2.2 %multiply_reduce_fusion.3 = (f32[512]{0:T(512)S(1)}, f32[512]{0:T(512)S(1)}, f32[512,1536]{0,1:T(8,128)S(1)}) fusion(f32[512]{0:T(512)S(1)} %fusion.13, f32[512,1536]{0,1:T(8,128)S(1)} %get-tuple-element.44, f32[512]{0:T(512)S(1)} %get-tuple-element.43, s32[1536]{0:T(1024)S(1)} %broadcast_bitcast_fusion.1, s32[512]{0:T(512)S(1)} %broadcast_bitcast_fusion.3, ...), kind=kOutput, calls=%fused_computation.29 | convolution fusion | flops 213515264 | bytes 9992192 | tf_op jit(solution)/shard_map/qd,kd->qk/dot_general | solution.py:94
  75.2 2.8 %multiply_convert_fusion.3 = (bf16[512,1536]{0,1:T(8,128)(2,1)S(1)}, f32[512]{0:T(512)S(1)}) fusion(f32[512,1536]{0,1:T(8,128)S(1)} %get-tuple-element.45, f32[512]{0:T(512)S(1)} %get-tuple-element.6, f32[512]{0:T(512)S(1)} %fusion.13, f32[512,1536]{0,1:T(8,128)S(1)} %get-tuple-element.44, f32[512]{0:T(512)S(1)} %get-tuple-element.43, ...), kind=kLoop, calls=%fused_computation.28 | loop fusion | flops 12582400 | bytes 11038208 | tf_op jit(solution)/shard_map/convert_element_type | solution.py:96
  78.0 1.9 %multiply_reduce_fusion.2 = (f32[512]{0:T(512)S(1)}, f32[512,1536]{0,1:T(8,128)S(1)}) fusion(f32[512]{0:T(512)S(1)} %get-tuple-element.33, f32[512,1536]{0,1:T(8,128)S(1)} %fusion.1, f32[512]{0:T(512)S(1)} %get-tuple-element.7, s32[1536]{0:T(1024)S(1)} %broadcast_bitcast_fusion.1, s32[512]{0:T(512)S(1)} %broadcast_bitcast_fusion.3, ...), kind=kOutput, calls=%fused_computation.25 | convolution fusion | flops 211942912 | bytes 6844416 | tf_op jit(solution)/shard_map/qd,kd->qk/dot_general | solution.py:94
  79.9 2.0 %convolution_add_fusion.2 = f32[1536,128]{0,1:T(8,128)S(1)} fusion(f32[1536,128]{0,1:T(8,128)S(1)} %fusion.24, bf16[1024,256]{1,0:T(8,128)(2,1)S(1)} %copy-done.40, f32[512,1536]{0,1:T(8,128)S(1)} %fusion.1, f32[512]{0:T(512)S(1)} %get-tuple-element.33, f32[512]{0:T(512)S(1)} %get-tuple-element.7, s32[512]{0:T(512)S(1)} %broadcast_bitcast_fusion.3, ...), kind=kOutput, calls=%fused_computation.40 | convolution fusion | flops 210173952 | bytes 4876288 | tf_op jit(solution)/shard_map/qk,qd->kd/dot_general | solution.py:107
  82.6 2.4 %multiply_convert_fusion.2 = bf16[512,1536]{0,1:T(8,128)(2,1)S(1)} fusion(f32[512,1536]{0,1:T(8,128)S(1)} %get-tuple-element.47, f32[512]{0:T(512)S(1)} %get-tuple-element.46, f32[512]{0:T(512)S(1)} %get-tuple-element.33, f32[512,1536]{0,1:T(8,128)S(1)} %fusion.1, f32[512]{0:T(512)S(1)} %get-tuple-element.7, s32[1536]{0:T(1024)S(1)} %broadcast_bitcast_fusion.1, ...), kind=kLoop, calls=%fused_computation.24 | loop fusion | flops 10223616 | bytes 7888384 | tf_op jit(solution)/shard_map/convert_element_type | solution.py:96
  85.7 1.6 %collective-permute-start.4 = (f32[1,512,256]{1,2,0:T(8,128)S(1)}, f32[1,512,256]{1,2,0:T(8,128)S(1)}, u32[]{:S(2)}, u32[]{:S(2)}) collective-permute-start(f32[1,512,256]{1,2,0:T(8,128)S(1)} %fusion.41), channel_id=1, source_target_pairs={{4,0},{8,4},{12,8},{16,12},{20,16},{24,20},{28,24},{5,1},{9,5},{13... | collective-permute-start | bytes 1572872 | tf_op jit(solution)/shard_map/ppermute | solution.py:23
  87.5 2.0 %convolution_add_fusion = f32[1536,128]{0,1:T(8,128)S(1)} fusion(f32[1536,128]{0,1:T(8,128)S(1)} %copy-done.41, bf16[1024,256]{1,0:T(8,128)(2,1)S(1)} %copy-done.40, f32[512,1536]{0,1:T(8,128)S(1)} %fusion.3, f32[512]{0:T(512)S(1)} %copy-done.36, f32[512]{0:T(512)S(1)} %copy-done.34, s32[512]{0:T(512)S(1)} %copy-done.32, s32[1536]{0:T(1024)S(1)} %iota_add_fusion, ...), kind=kOutput, calls=%fused_computation.38 | convolution fusion | flops 210173952 | bytes 4876288 | tf_op jit(solution)/shard_map/qk,qd->kd/dot_general | solution.py:107
  89.5 11.3 %collective-permute-done.4 = f32[1,512,256]{1,2,0:T(8,128)S(1)} collective-permute-done((f32[1,512,256]{1,2,0:T(8,128)S(1)}, f32[1,512,256]{1,2,0:T(8,128)S(1)}, u32[]{:S(2)}, u32[]{:S(2)}) %collective-permute-start.4) | collective-permute-done | bytes 524320 | tf_op jit(solution)/shard_map/ppermute | solution.py:23
  102.2 6.0 %collective-permute-start.6 = (f32[1,512,256]{1,2,0:T(8,128)S(1)}, f32[1,512,256]{1,2,0:T(8,128)S(1)}, u32[]{:S(2)}, u32[]{:S(2)}) collective-permute-start(f32[1,512,256]{1,2,0:T(8,128)S(1)} %get-tuple-element.13), channel_id=1, source_target_pairs={{0,4},{4,8},{8,12},{12,16},{16,20},{20,24},{24,28},{1,5},{5,9},{9,... | collective-permute-start | bytes 1572872 | tf_op jit(solution)/shard_map/ppermute | solution.py:22
  109.1 7.4 %collective-permute-done.5 = f32[1,512,256]{1,2,0:T(8,128)S(1)} collective-permute-done((f32[1,512,256]{1,2,0:T(8,128)S(1)}, f32[1,512,256]{1,2,0:T(8,128)S(1)}, u32[]{:S(2)}, u32[]{:S(2)}) %collective-permute-start.5) | collective-permute-done | bytes 524320 | tf_op jit(solution)/shard_map/ppermute | solution.py:23
  116.5 11.4 %collective-permute-done.6 = f32[1,512,256]{1,2,0:T(8,128)S(1)} collective-permute-done((f32[1,512,256]{1,2,0:T(8,128)S(1)}, f32[1,512,256]{1,2,0:T(8,128)S(1)}, u32[]{:S(2)}, u32[]{:S(2)}) %collective-permute-start.6) | collective-permute-done | bytes 524320 | tf_op jit(solution)/shard_map/ppermute | solution.py:22
  128.9 4.5 %collective-permute-start.7 = (f32[1,512,256]{1,2,0:T(8,128)}, f32[1,512,256]{1,2,0:T(8,128)S(1)}, u32[]{:S(2)}, u32[]{:S(2)}) collective-permute-start(f32[1,512,256]{1,2,0:T(8,128)} %get-tuple-element.11), channel_id=1, source_target_pairs={{0,4},{4,8},{8,12},{12,16},{16,20},{20,24},{24,28},{1,5},{5,9},{9,... | collective-permute-start | bytes 1572872 | tf_op jit(solution)/shard_map/ppermute | solution.py:22
  135.0 10.1 %collective-permute-done.7 = f32[1,512,256]{1,2,0:T(8,128)S(1)} collective-permute-done((f32[1,512,256]{1,2,0:T(8,128)}, f32[1,512,256]{1,2,0:T(8,128)S(1)}, u32[]{:S(2)}, u32[]{:S(2)}) %collective-permute-start.7) | collective-permute-done | bytes 524320 | tf_op jit(solution)/shard_map/ppermute | solution.py:22
  (145 shorter events, 24.4 us)
Async XLA Ops:
  3.2 11.2 %collective-permute-start.2 = (bf16[1,513,256]{2,1,0:T(8,128)(2,1)S(1)}, bf16[1,513,256]{2,1,0:T(8,128)(2,1)S(1)}, u32[]{:S(2)}, u32[]{:S(2)}) collective-permute-start(bf16[1,513,256]{2,1,0:T(8,128)(2,1)S(1)} %maximum_bitcast_fusion), channel_id=1, source_target_pairs={{4,0},{8,4},{12,8},{16,12},{20,16},{24,20},{28,24},{5,1},{9,5},{13... | collective-permute-start | bytes 787976 | tf_op jit(solution)/shard_map/ppermute | solution.py:23
  14.5 15.0 %collective-permute-start = (bf16[1,513,256]{2,1,0:T(8,128)(2,1)S(1)}, bf16[1,513,256]{2,1,0:T(8,128)(2,1)S(1)}, u32[]{:S(2)}, u32[]{:S(2)}) collective-permute-start(bf16[1,513,256]{2,1,0:T(8,128)(2,1)S(1)} %get-tuple-element.22), channel_id=1, source_target_pairs={{0,4},{4,8},{8,12},{12,16},{16,20},{20,24},{24,28},{1,5},{5,9},{9,... | collective-permute-start | bytes 787976 | tf_op jit(solution)/shard_map/ppermute | solution.py:22
  19.2 11.7 %collective-permute-start.3 = (bf16[1,513,256]{2,1,0:T(8,128)(2,1)S(1)}, bf16[1,513,256]{2,1,0:T(8,128)(2,1)S(1)}, u32[]{:S(2)}, u32[]{:S(2)}) collective-permute-start(bf16[1,513,256]{2,1,0:T(8,128)(2,1)S(1)} %maximum_select_fusion), channel_id=1, source_target_pairs={{4,0},{8,4},{12,8},{16,12},{20,16},{24,20},{28,24},{5,1},{9,5},{13... | collective-permute-start | bytes 787976 | tf_op jit(solution)/shard_map/ppermute | solution.py:23
  29.5 2.6 %copy-start.8 = (bf16[1,513,256]{2,1,0:T(8,128)(2,1)}, bf16[1,513,256]{2,1,0:T(8,128)(2,1)S(1)}, u32[]{:S(2)}) copy-start(bf16[1,513,256]{2,1,0:T(8,128)(2,1)S(1)} %collective-permute-done) | copy-start | bytes 787972
  32.0 17.2 %copy-start.23 = (s32[1536]{0:T(1024)}, s32[1536]{0:T(1024)S(1)}, u32[]{:S(2)}) copy-start(s32[1536]{0:T(1024)S(1)} %broadcast_bitcast_fusion) | copy-start | bytes 18436
  32.1 17.1 %copy-start.31 = (s32[512]{0:T(512)}, s32[512]{0:T(512)S(1)}, u32[]{:S(2)}) copy-start(s32[512]{0:T(512)S(1)} %broadcast_bitcast_fusion.2) | copy-start | bytes 6148
  38.2 3.4 %copy-start.17 = (bf16[512,128]{1,0:T(8,128)(2,1)S(1)}, bf16[512,128]{1,0:T(8,128)(2,1)}, u32[]{:S(2)}) copy-start(bf16[512,128]{1,0:T(8,128)(2,1)} %copy-done.16) | copy-start | bytes 393220
  38.2 3.4 %copy-start.19 = (bf16[512,128]{1,0:T(8,128)(2,1)S(1)}, bf16[512,128]{1,0:T(8,128)(2,1)}, u32[]{:S(2)}) copy-start(bf16[512,128]{1,0:T(8,128)(2,1)} %get-tuple-element.21) | copy-start | bytes 393220
  38.2 3.4 %copy-start.21 = (bf16[512,128]{1,0:T(8,128)(2,1)S(1)}, bf16[512,128]{1,0:T(8,128)(2,1)}, u32[]{:S(2)}) copy-start(bf16[512,128]{1,0:T(8,128)(2,1)} %get-tuple-element.19) | copy-start | bytes 393220
  43.8 5.5 %copy-start.33 = (f32[512]{0:T(512)}, f32[512]{0:T(512)S(1)}, u32[]{:S(2)}) copy-start(f32[512]{0:T(512)S(1)} %get-tuple-element.9) | copy-start | bytes 6148
  46.7 2.6 %copy-start.35 = (f32[512]{0:T(512)}, f32[512]{0:T(512)S(1)}, u32[]{:S(2)}) copy-start(f32[512]{0:T(512)S(1)} %get-tuple-element.35) | copy-start | bytes 6148
  51.7 7.3 %copy-start.4 = (bf16[512,1536]{0,1:T(8,128)(2,1)}, bf16[512,1536]{0,1:T(8,128)(2,1)S(1)}, u32[]{:S(2)}) copy-start(bf16[512,1536]{0,1:T(8,128)(2,1)S(1)} %multiply_convert_fusion) | copy-start | bytes 4718596
  51.7 10.6 %copy-start.37 = (bf16[4]{0:T(256)(128)(2,1)S(1)}, bf16[4]{0:T(256)(128)(2,1)}, u32[]{:S(2)}) copy-start(bf16[4]{0:T(256)(128)(2,1)} %slice_bitcast_fusion.3) | copy-start | bytes 28
  51.7 10.6 %copy-start.38 = (bf16[4]{0:T(256)(128)(2,1)S(1)}, bf16[4]{0:T(256)(128)(2,1)}, u32[]{:S(2)}) copy-start(bf16[4]{0:T(256)(128)(2,1)} %slice_bitcast_fusion.4) | copy-start | bytes 28
  53.3 8.3 %collective-permute-start.1 = (bf16[1,513,256]{2,1,0:T(8,128)(2,1)S(1)}, bf16[1,513,256]{2,1,0:T(8,128)(2,1)S(1)}, u32[]{:S(2)}, u32[]{:S(2)}) collective-permute-start(bf16[1,513,256]{2,1,0:T(8,128)(2,1)S(1)} %copy-done.9), channel_id=1, source_target_pairs={{0,4},{4,8},{8,12},{12,16},{16,20},{20,24},{24,28},{1,5},{5,9},{9,... | collective-permute-start | bytes 787976 | tf_op jit(solution)/shard_map/ppermute | solution.py:22
  64.2 3.2 %copy-start.7 = (bf16[1024,256]{1,0:T(8,128)(2,1)S(1)}, bf16[1024,256]{1,0:T(8,128)(2,1)}, u32[]{:S(2)}) copy-start(bf16[1024,256]{1,0:T(8,128)(2,1)} %param.5) | copy-start | bytes 1572868
  64.2 3.2 %copy-start.10 = (bf16[512,128]{1,0:T(8,128)(2,1)S(1)}, bf16[512,128]{1,0:T(8,128)(2,1)}, u32[]{:S(2)}) copy-start(bf16[512,128]{1,0:T(8,128)(2,1)} %get-tuple-element.16) | copy-start | bytes 393220
  64.2 3.2 %copy-start.15 = (bf16[512,128]{1,0:T(8,128)(2,1)S(1)}, bf16[512,128]{1,0:T(8,128)(2,1)}, u32[]{:S(2)}) copy-start(bf16[512,128]{1,0:T(8,128)(2,1)} %get-tuple-element.14) | copy-start | bytes 393220
  64.2 3.3 %copy-start.27 = (pred[1536]{0:T(1024)(128)(4,1)S(1)}, pred[1536]{0:T(1024)(128)(4,1)}, u32[]{:S(2)}) copy-start(pred[1536]{0:T(1024)(128)(4,1)} %broadcast_compare_fusion.1) | copy-start | bytes 4612
  64.3 3.3 %copy-start.30 = (s32[512]{0:T(512)S(1)}, s32[512]{0:T(512)}, u32[]{:S(2)}) copy-start(s32[512]{0:T(512)} %iota_add_fusion.3) | copy-start | bytes 6148
  85.7 15.0 %copy-start = (f32[1536,128]{0,1:T(8,128)S(1)}, f32[1536,128]{0,1:T(8,128)}, u32[]{:S(2)}) copy-start(f32[1536,128]{0,1:T(8,128)} %fusion.11) | copy-start | bytes 2359300
  85.7 15.0 %collective-permute-start.4 = (f32[1,512,256]{1,2,0:T(8,128)S(1)}, f32[1,512,256]{1,2,0:T(8,128)S(1)}, u32[]{:S(2)}, u32[]{:S(2)}) collective-permute-start(f32[1,512,256]{1,2,0:T(8,128)S(1)} %fusion.41), channel_id=1, source_target_pairs={{4,0},{8,4},{12,8},{16,12},{20,16},{24,20},{28,24},{5,1},{9,5},{13... | collective-permute-start | bytes 1572872 | tf_op jit(solution)/shard_map/ppermute | solution.py:23
  89.4 38.4 %copy-start.2 = (f32[1536,128]{0,1:T(8,128)}, f32[1536,128]{0,1:T(8,128)S(1)}, u32[]{:S(2)}) copy-start(f32[1536,128]{0,1:T(8,128)S(1)} %convolution_add_fusion) | copy-start | bytes 2359300
  89.5 18.7 %copy-start.5 = (bf16[512,1536]{0,1:T(8,128)(2,1)S(1)}, bf16[512,1536]{0,1:T(8,128)(2,1)}, u32[]{:S(2)}) copy-start(bf16[512,1536]{0,1:T(8,128)(2,1)} %copy-done.4) | copy-start | bytes 4718596
  89.5 18.7 %copy-start.12 = (bf16[512,128]{1,0:T(8,128)(2,1)S(1)}, bf16[512,128]{1,0:T(8,128)(2,1)}, u32[]{:S(2)}) copy-start(bf16[512,128]{1,0:T(8,128)(2,1)} %get-tuple-element.20) | copy-start | bytes 393220
  89.5 18.7 %copy-start.14 = (bf16[512,128]{1,0:T(8,128)(2,1)S(1)}, bf16[512,128]{1,0:T(8,128)(2,1)}, u32[]{:S(2)}) copy-start(bf16[512,128]{1,0:T(8,128)(2,1)} %get-tuple-element.18) | copy-start | bytes 393220
  100.9 15.5 %collective-permute-start.5 = (f32[1,512,256]{1,2,0:T(8,128)S(1)}, f32[1,512,256]{1,2,0:T(8,128)S(1)}, u32[]{:S(2)}, u32[]{:S(2)}) collective-permute-start(f32[1,512,256]{1,2,0:T(8,128)S(1)} %get-tuple-element.12), channel_id=1, source_target_pairs={{4,0},{8,4},{12,8},{16,12},{20,16},{24,20},{28,24},{5,1},{9,5},{13... | collective-permute-start | bytes 1572872 | tf_op jit(solution)/shard_map/ppermute | solution.py:23
  102.2 25.6 %collective-permute-start.6 = (f32[1,512,256]{1,2,0:T(8,128)S(1)}, f32[1,512,256]{1,2,0:T(8,128)S(1)}, u32[]{:S(2)}, u32[]{:S(2)}) collective-permute-start(f32[1,512,256]{1,2,0:T(8,128)S(1)} %get-tuple-element.13), channel_id=1, source_target_pairs={{0,4},{4,8},{8,12},{12,16},{16,20},{20,24},{24,28},{1,5},{5,9},{9,... | collective-permute-start | bytes 1572872 | tf_op jit(solution)/shard_map/ppermute | solution.py:22
  128.9 5.0 %copy-start.22 = (bf16[512,128]{0,1:T(8,128)(2,1)S(1)}, bf16[512,128]{0,1:T(8,128)(2,1)}, u32[]{:S(2)}) copy-start(bf16[512,128]{0,1:T(8,128)(2,1)} %fusion.28) | copy-start | bytes 393220
  128.9 16.2 %copy-start.1 = (f32[1536,128]{0,1:T(8,128)S(1)}, f32[1536,128]{0,1:T(8,128)}, u32[]{:S(2)}) copy-start(f32[1536,128]{0,1:T(8,128)} %fusion.11) | copy-start | bytes 2359300
  128.9 16.2 %copy-start.3 = (f32[1536,128]{0,1:T(8,128)S(1)}, f32[1536,128]{0,1:T(8,128)}, u32[]{:S(2)}) copy-start(f32[1536,128]{0,1:T(8,128)} %copy-done.2) | copy-start | bytes 2359300
  128.9 16.2 %collective-permute-start.7 = (f32[1,512,256]{1,2,0:T(8,128)}, f32[1,512,256]{1,2,0:T(8,128)S(1)}, u32[]{:S(2)}, u32[]{:S(2)}) collective-permute-start(f32[1,512,256]{1,2,0:T(8,128)} %get-tuple-element.11), channel_id=1, source_target_pairs={{0,4},{4,8},{8,12},{12,16},{16,20},{20,24},{24,28},{1,5},{5,9},{9,... | collective-permute-start | bytes 1572872 | tf_op jit(solution)/shard_map/ppermute | solution.py:22
  (18 other events, 37.9 us)
where the time goes:
time: 148 us; the launch traced here: 147 us
  waiting for transfers between devices  58.1 us (39%)
  matrix products  30.5 us (21%)
  starting transfers between devices  25.1 us (17%)
  other arithmetic  21.2 us (14%)
  local copies, waits for them, and re-layouts  10.6 us (7%)
    ppermute x4, waiting for transfers between devices, padded_2(): before = lax.ppermute(last, axis, up)  32.5 us
    ppermute x4, waiting for transfers between devices, padded_2(): after = lax.ppermute(first, axis, down)  25.7 us
    ppermute x4, starting transfers between devices, padded_2(): before = lax.ppermute(last, axis, up)  19.6 us
    convert_element_type x4, other arithmetic, half_grads(): score_gradient = (weights * (dweights - row_dot)).astype(jnp.bfloat16)  10.4 us
    dot_general x4, matrix products, half_grads(): jnp.einsum('qk,qd->kd', weights_bfloat, gradout_h, preferred_element_type...  9.34 us
    dot_general x4, matrix products, half_grads(): jnp.einsum('qd,kd->qk', gradout_h, val_all, preferred_element_type=jnp.fl...  8.13 us
    dot_general x4, matrix products, half_grads(): jnp.einsum('qd,kd->qk', query_h, key_all, preferred_element_type=jnp.floa...  7.09 us
    ppermute x4, starting transfers between devices, padded_2(): after = lax.ppermute(first, axis, down)  5.52 us
  transfers between devices with their start and end apart: 8, of which 7 were waited for; matrix products, arithmetic and copies ran while one was open for 7% of the time, Pallas kernels for 0%

commit v1 on v0

v1 whole, which is shorter than its diff:
```python
import math

import jax
import jax.numpy as jnp
from jax import lax
from jax.experimental import pallas as pl
from jax.experimental.pallas import tpu as pltpu
from jax.sharding import PartitionSpec as P

HEAD_SIZE = 128
WINDOW = 1024
QUERY_PER_KEY = 2
BLOCK = 128
TILE = 256
MARK = 16
NEG = -1e30

query_scaling = 168.0 ** (-0.5)
exponent_scale = query_scaling * math.log2(math.e)


def dot(a, b, ca, cb):
    return lax.dot_general(a, b, (((ca,), (cb,)), ((), ())), preferred_element_type=jnp.float32)


def pack_kernel(index_ref, starts_ref, keys_ref, values_ref, inner_ref, outer_ref):
    length = keys_ref.shape[0] // 2
    width = keys_ref.shape[1]
    blocks = length // BLOCK
    index = index_ref[0]
    parity = lax.rem(index, 2)
    for out_ref, half in ((inner_ref, 1 - parity), (outer_ref, parity)):
        rows = pl.ds(pl.multiple_of(half * length, length), length)
        out_ref[:length, :width] = keys_ref[rows, :]
        out_ref[:length, width:] = values_ref[rows, :]
        row = lax.broadcasted_iota(jnp.int32, (MARK, 2 * width), 0)
        marks = jnp.zeros((MARK, 2 * width), jnp.float32)
        for j in range(blocks):
            begin = starts_ref[half * blocks + j]
            if j == 0:
                begin = jnp.where((index == 0) & (half == 0), 1, begin)
            marks = jnp.where(row == j, begin.astype(jnp.float32), marks)
        out_ref[length:, :] = marks.astype(jnp.bfloat16)


def stage_kernel(with_half, index_ref, q_ref, g_ref, own_ref, near_ref, far_ref, *refs):
    dq_ref, own_out, near_out, far_out, acc_ref = refs[-5:]
    length = q_ref.shape[0] // 2
    width = own_ref.shape[1] // 2
    blocks = length // BLOCK
    tiles = length // TILE
    per = TILE // BLOCK
    chunks = WINDOW // TILE + 1
    index = index_ref[0]
    parity = lax.rem(index, 2)
    half = 1 - parity if with_half == "inner" else parity
    base = half * length
    pieces = (far_ref, near_ref, own_ref)

    docs = []
    count = jnp.zeros((1, TILE), jnp.float32)
    for piece in pieces:
        marks = piece[length:, :TILE].astype(jnp.float32)
        for j in range(blocks):
            count = count + marks[j : j + 1, :]
            docs.append(count)
    lane = lax.broadcasted_iota(jnp.int32, (1, TILE), 1)
    row2 = lax.broadcasted_iota(jnp.int32, (TILE, TILE), 0)
    col2 = lax.broadcasted_iota(jnp.int32, (TILE, TILE), 1)
    after = row2 > col2

    key_t = [jnp.transpose(p[:length, :width]) for p in pieces]

    started = [False] * (3 * length // TILE)
    for i in range(tiles):
        own_docs = docs[2 * blocks + i * per]
        for b in range(1, per):
            own_docs = jnp.where(lane >= b * BLOCK, docs[2 * blocks + i * per + b], own_docs)
        bias = []
        for c in range(chunks):
            bias.append(
                [jnp.where(docs[(i + c) * per + b] == own_docs, 0.0, NEG) for b in range(per)]
            )
        rows = pl.ds(pl.multiple_of(base + i * TILE, TILE), TILE)
        members = []
        for h in range(QUERY_PER_KEY):
            cols = slice(h * HEAD_SIZE, (h + 1) * HEAD_SIZE)
            qt = q_ref[rows, cols]
            gt = g_ref[rows, cols]
            scores, dweights = [], []
            top = None
            for c in range(chunks):
                p, r = divmod((i + c) * TILE, length)
                s = dot(pieces[p][r : r + TILE, :width], qt, 1, 1)
                if c == 0:
                    s = jnp.where(after, s, NEG)
                if c == chunks - 1:
                    s = jnp.where(after, NEG, s)
                scores.append(s)
                dweights.append(dot(pieces[p][r : r + TILE, width:], gt, 1, 1))
                for b in range(per):
                    t = jnp.max(s[b * BLOCK : (b + 1) * BLOCK], axis=0, keepdims=True) + bias[c][b]
                    top = t if top is None else jnp.maximum(top, t)
            shift = top * exponent_scale
            total = jnp.zeros((1, TILE), jnp.float32)
            row_dot = jnp.zeros((1, TILE), jnp.float32)
            terms = []
            for c in range(chunks):
                parts = [
                    jnp.exp2(
                        scores[c][b * BLOCK : (b + 1) * BLOCK] * exponent_scale
                        + (bias[c][b] - shift)
                    )
                    for b in range(per)
                ]
                e = jnp.concatenate(parts, axis=0)
                terms.append(e)
                total = total + jnp.sum(e, axis=0, keepdims=True)
                row_dot = row_dot + jnp.sum(e * dweights[c], axis=0, keepdims=True)
            inverse = 1.0 / total
            row_dot = row_dot * inverse
            weights, dscores = [], []
            dq_t = jnp.zeros((width, TILE), jnp.float32)
            for c in range(chunks):
                w = terms[c] * inverse
                ds = (w * (dweights[c] - row_dot)).astype(jnp.bfloat16)
                weights.append(w.astype(jnp.bfloat16))
                dscores.append(ds)
                p, r = divmod((i + c) * TILE, length)
                dq_t = dq_t + dot(key_t[p][:, r : r + TILE], ds, 1, 0)
            dq_ref[rows, cols] = jnp.transpose(dq_t * query_scaling).astype(jnp.bfloat16)
            members.append((qt, gt, weights, dscores))
        q_all = jnp.concatenate([m[0] for m in members], axis=0)
        g_all = jnp.concatenate([m[1] for m in members], axis=0)
        for c in range(chunks):
            w_all = jnp.concatenate([m[2][c] for m in members], axis=1)
            d_all = jnp.concatenate([m[3][c] for m in members], axis=1)
            dk = dot(d_all, q_all, 1, 0) * query_scaling
            dv = dot(w_all, g_all, 1, 0)
            slot = i + c
            at = slice(slot * TILE, (slot + 1) * TILE)
            if started[slot]:
                dk = dk + acc_ref[at, :width]
                dv = dv + acc_ref[at, width:]
            started[slot] = True
            acc_ref[at, :width] = dk
            acc_ref[at, width:] = dv
    if len(refs) == 6:
        other = pl.ds(pl.multiple_of(length - base, length), length)
        dq_ref[other, :] = refs[0][other, :]
    far_out[...] = acc_ref[:length].astype(jnp.bfloat16)
    near_out[...] = acc_ref[length : 2 * length].astype(jnp.bfloat16)
    own_out[...] = acc_ref[2 * length :]


def sum_kernel(index_ref, inner_own, inner_a, inner_b, outer_own, outer_a, outer_b, dk_ref, dv_ref):
    length = inner_own.shape[0]
    width = dk_ref.shape[1]
    parity = lax.rem(index_ref[0], 2)
    f32 = jnp.float32
    for half, own, a, b in (
        (1 - parity, inner_own, inner_a, inner_b),
        (parity, outer_own, outer_a, outer_b),
    ):
        rows = pl.ds(pl.multiple_of(half * length, length), length)
        total = own[...] + (a[...].astype(f32) + b[...].astype(f32))
        dk_ref[rows, :] = total[:, :width].astype(jnp.bfloat16)
        dv_ref[rows, :] = total[:, width:].astype(jnp.bfloat16)


def smem():
    return pl.BlockSpec(memory_space=pltpu.SMEM)


def vmem():
    return pl.BlockSpec(memory_space=pltpu.VMEM)


LIMIT = pltpu.CompilerParams(vmem_limit_bytes=48 * 1024 * 1024)


def on_device(queries, keys, values, grad_out, starts):
    length = keys.shape[0] // 2
    width = keys.shape[1]
    count = lax.axis_size("seq")
    index = lax.axis_index("seq").astype(jnp.int32).reshape(1)
    order = list(range(0, count, 2)) + list(range(count - 1, 0, -2))
    clockwise = [(order[k], order[(k + 1) % count]) for k in range(count)]
    counter = [(b, a) for a, b in clockwise]
    pairs = [(d, d ^ 1) for d in range(count)]
    follow = dict(clockwise)
    across = [(d, follow[d ^ 1]) for d in range(count)]

    packed = jax.ShapeDtypeStruct((length + MARK, 2 * width), jnp.bfloat16)
    inner, outer = pl.pallas_call(
        pack_kernel,
        out_shape=(packed, packed),
        in_specs=[smem(), smem(), vmem(), vmem()],
        out_specs=(vmem(), vmem()),
    )(index, starts, keys, values)

    inner_far = lax.ppermute(inner, "seq", counter)
    outer_far = lax.ppermute(outer, "seq", clockwise)
    inner_near = lax.ppermute(outer, "seq", pairs)
    outer_near = lax.ppermute(inner_far, "seq", pairs)

    def stage(which, own, near, far, dq):
        wide = jax.ShapeDtypeStruct((length, 2 * width), jnp.float32)
        narrow = jax.ShapeDtypeStruct((length, 2 * width), jnp.bfloat16)
        operands = [index, queries, grad_out, own, near, far]
        specs = [smem()] + [vmem()] * 5
        aliases = {}
        if dq is not None:
            aliases = {len(operands): 0}
            operands.append(dq)
            specs.append(pl.BlockSpec(memory_space=pltpu.VMEM))
        flops = 10 * QUERY_PER_KEY * length * (WINDOW + TILE) * width
        return pl.pallas_call(
            lambda *refs: stage_kernel(which, *refs),
            out_shape=(jax.ShapeDtypeStruct(queries.shape, jnp.bfloat16), wide, narrow, narrow),
            in_specs=specs,
            out_specs=(vmem(),) * 4,
            scratch_shapes=[pltpu.VMEM((3 * length, 2 * width), jnp.float32)],
            input_output_aliases=aliases,
            compiler_params=LIMIT,
            cost_estimate=pl.CostEstimate(
                flops=flops, bytes_accessed=4 * 1024 * 1024, transcendentals=0
            ),
            name=which + "_stage",
        )(*operands)

    dq, inner_own, inner_g1, inner_g2 = stage("inner", inner, inner_near, inner_far, None)
    outer_b = lax.ppermute(inner_g1, "seq", pairs)
    inner_b = lax.ppermute(inner_g2, "seq", clockwise)
    dq, outer_own, outer_g1, outer_g2 = stage("outer", outer, outer_near, outer_far, dq)
    inner_a = lax.ppermute(outer_g1, "seq", across)
    outer_a = lax.ppermute(outer_g2, "seq", counter)

    half = jax.ShapeDtypeStruct(keys.shape, jnp.bfloat16)
    dk, dv = pl.pallas_call(
        sum_kernel,
        out_shape=(half, half),
        in_specs=[smem()] + [vmem()] * 6,
        out_specs=(vmem(), vmem()),
    )(index, inner_own, inner_a, inner_b, outer_own, outer_a, outer_b)
    return dq, dk, dv


def solution(mesh):
    in_specs = (P("seq", "head"), P("seq", "head"), P("seq", "head"), P("seq", "head"), P("seq"))
    out_specs = (P("seq", "head"), P("seq", "head"), P("seq", "head"))
    return jax.shard_map(
        on_device, mesh=mesh, in_specs=in_specs, out_specs=out_specs, check_vma=False
    )
```

time: 148 us -> 54.1 us (0.37)
  waiting for transfers between devices: 58.1 us -> 15.3 us
  matrix products: 30.5 us -> 0 us
  other arithmetic: 21.2 us -> 0 us
  Pallas kernels: 0 us -> 17.2 us
  starting transfers between devices: 25.1 us -> 16.3 us
  local copies, waits for them, and re-layouts: 10.6 us -> 4.28 us
    ppermute x8, waiting for transfers between devices: 58.1 us -> 15.3 us  [the longest x1 7.77 us: on_device(): outer_a = lax.ppermute(outer_g2, 'seq', counter)]
    dot_general x20 -> x0, matrix products: 30.5 us -> none  [the longest x4 9.34 us: half_grads(): jnp.einsum('qk,qd->kd', weights_bfloat, gradout_h, preferred_element_type...]
    pallas_call x0 -> x4, Pallas kernels: none -> 17.2 us  [the longest x2 12.8 us: stage(): pl.pallas_call(lambda *refs: stage_kernel(which, *refs), out_shape=(jax.S...]
    convert_element_type x4 -> x0, other arithmetic: 10.4 us -> none  [half_grads(): score_gradient = (weights * (dweights - row_dot)).astype(jnp.bfloat16)]
    ppermute x8, starting transfers between devices: 25.1 us -> 16.3 us  [the longest x1 4.77 us: on_device(): outer_a = lax.ppermute(outer_g2, 'seq', counter)]
    slice x10 -> x0, local copies, waits for them, and re-layouts: 5 us -> none  [the longest x4 2.88 us: half_grads(): key_all = jnp.concatenate([p[:length, :width] for p in pieces])]
    another operation x11 -> x0, other arithmetic: 4.32 us -> none
    reduce_sum x2 -> x0, other arithmetic: 3.94 us -> none  [half_grads(): weights = exp_terms / jnp.sum(exp_terms, axis=1, keepdims=True)]
  transfers between devices with their start and end apart: 8 -> 8, of which waited for: 7 -> 3; matrix products, arithmetic and copies ran while one was open for 7% -> 0% of each run, Pallas kernels for 0% -> 24%
where the time goes in v1:
time: 54.1 us; the launch traced here: 53.8 us
  Pallas kernels  17.2 us (32%)
  starting transfers between devices  16.3 us (30%)
  waiting for transfers between devices  15.3 us (28%)
  local copies, waits for them, and re-layouts  4.28 us (8%)
  between operations  0.7 us (1%)
    pallas_call x2, Pallas kernels, stage(): pl.pallas_call(lambda *refs: stage_kernel(which, *refs), out_shape=(jax.S...  12.8 us
    ppermute x1, waiting for transfers between devices, on_device(): outer_a = lax.ppermute(outer_g2, 'seq', counter)  7.77 us
    ppermute x1, starting transfers between devices, on_device(): outer_a = lax.ppermute(outer_g2, 'seq', counter)  4.77 us
    unnamed x20, local copies, waits for them, and re-layouts  4.28 us
    ppermute x1, waiting for transfers between devices, on_device(): inner_far = lax.ppermute(inner, 'seq', counter)  4.05 us
    ppermute x1, waiting for transfers between devices, on_device(): inner_near = lax.ppermute(outer, 'seq', pairs)  3.42 us
    ppermute x1, starting transfers between devices, on_device(): inner_far = lax.ppermute(inner, 'seq', counter)  2.94 us
    pallas_call x1, Pallas kernels, on_device(): pl.pallas_call(sum_kernel, out_shape=(half, half), in_specs=[smem()] + [v...  2.42 us
  transfers between devices with their start and end apart: 8, of which 3 were waited for; matrix products, arithmetic and copies ran while one was open for 0% of the time, Pallas kernels for 24%

profile of v1, /device:TPU:0, one launch (start us, length us, event | category | flops | bytes accessed | tf_op | source)
XLA Modules:
  0.0 53.8 jit_solution(8955989074486711877)
XLA Ops:
  0.6 0.0 copy-start.2
  0.6 2.0 %shard_map.76 = (bf16[528,256]{1,0:T(8,128)(2,1)}, bf16[528,256]{1,0:T(8,128)(2,1)}) custom-call(s32[1]{0:T(128)} %bitcast.index_ref.refs_0_, s32[8]{0:T(128)} %starts_ref.1, bf16[1024,128]{1,0:T(8,128)(2,1)} %keys_ref.1, bf16[1024,128]{1,0:T(8,128)(2,1)} %values_ref.1), custom_call_target="tpu_custom_call" | custom-call | tf_op jit(solution)/shard_map/pallas_call | solution.py:195
  2.6 2.9 %collective-permute-start = (bf16[528,256]{1,0:T(8,128)(2,1)}, bf16[528,256]{1,0:T(8,128)(2,1)S(1)}, u32[]{:S(2)}, u32[]{:S(2)}) collective-permute-start(bf16[528,256]{1,0:T(8,128)(2,1)} %get-tuple-element.16.refs_3_), channel_id=1, source_target_pairs={{8,0},{16,8},{24,16},{28,24},{20,28},{12,20},{4,12},{0,4},{9,1},{1... | collective-permute-start | bytes 811016 | tf_op jit(solution)/shard_map/ppermute | solution.py:202
  5.6 1.6 %collective-permute-start.3 = (bf16[528,256]{1,0:T(8,128)(2,1)}, bf16[528,256]{1,0:T(8,128)(2,1)S(1)}, u32[]{:S(2)}, u32[]{:S(2)}) collective-permute-start(bf16[528,256]{1,0:T(8,128)(2,1)} %get-tuple-element.15.refs_3_), channel_id=1, source_target_pairs={{0,4},{4,0},{8,12},{12,8},{16,20},{20,16},{24,28},{28,24},{1,5},{5... | collective-permute-start | bytes 811016 | tf_op jit(solution)/shard_map/ppermute | solution.py:204
  7.1 1.6 %collective-permute-start.2 = (bf16[528,256]{1,0:T(8,128)(2,1)}, bf16[528,256]{1,0:T(8,128)(2,1)S(1)}, u32[]{:S(2)}, u32[]{:S(2)}) collective-permute-start(bf16[528,256]{1,0:T(8,128)(2,1)} %get-tuple-element.15.refs_3_), channel_id=1, source_target_pairs={{0,8},{8,16},{16,24},{24,28},{28,20},{20,12},{12,4},{4,0},{1,9},{9... | collective-permute-start | bytes 811016 | tf_op jit(solution)/shard_map/ppermute | solution.py:203
  8.7 4.0 %collective-permute-done.refs_5_ = bf16[528,256]{1,0:T(8,128)(2,1)S(1)} collective-permute-done((bf16[528,256]{1,0:T(8,128)(2,1)}, bf16[528,256]{1,0:T(8,128)(2,1)S(1)}, u32[]{:S(2)}, u32[]{:S(2)}) %collective-permute-start) | collective-permute-done | bytes 270368 | tf_op jit(solution)/shard_map/ppermute | solution.py:202
  12.8 2.4 %collective-permute-start.1 = (bf16[528,256]{1,0:T(8,128)(2,1)S(1)}, bf16[528,256]{1,0:T(8,128)(2,1)S(1)}, u32[]{:S(2)}, u32[]{:S(2)}) collective-permute-start(bf16[528,256]{1,0:T(8,128)(2,1)S(1)} %collective-permute-done.refs_5_), channel_id=1, source_target_pairs={{0,4},{4,0},{8,12},{12,8},{16,20},{20,16},{24,28},{28,24},{1,5},{5... | collective-permute-start | bytes 811016 | tf_op jit(solution)/shard_map/ppermute | solution.py:205
  15.2 3.4 %collective-permute-done.3.refs_4_ = bf16[528,256]{1,0:T(8,128)(2,1)S(1)} collective-permute-done((bf16[528,256]{1,0:T(8,128)(2,1)}, bf16[528,256]{1,0:T(8,128)(2,1)S(1)}, u32[]{:S(2)}, u32[]{:S(2)}) %collective-permute-start.3) | collective-permute-done | bytes 270368 | tf_op jit(solution)/shard_map/ppermute | solution.py:204
  18.6 0.0 copy-done.2
  18.6 1.0 %copy-done.3 = bf16[1024,256]{1,0:T(8,128)(2,1)S(1)} copy-done((bf16[1024,256]{1,0:T(8,128)(2,1)S(1)}, bf16[1024,256]{1,0:T(8,128)(2,1)}, u32[]{:S(2)}) %copy-start.3) | copy-done | bytes 524312
  19.6 1.0 %copy-done.5 = bf16[528,256]{1,0:T(8,128)(2,1)S(1)} copy-done((bf16[528,256]{1,0:T(8,128)(2,1)S(1)}, bf16[528,256]{1,0:T(8,128)(2,1)}, u32[]{:S(2)}) %copy-start.5) | copy-done | bytes 270360
  20.6 5.9 %inner_stage.1 = (bf16[1024,256]{1,0:T(8,128)(2,1)}, f32[512,256]{1,0:T(8,128)S(1)}, bf16[512,256]{1,0:T(8,128)(2,1)S(1)}, bf16[512,256]{1,0:T(8,128)(2,1)S(1)}) custom-call(s32[1]{0:T(128)} %bitcast.index_ref.refs_0_, bf16[1024,256]{1,0:T(8,128)(2,1)S(1)} %copy-done.2, bf16[1024,256]{1,0:T(8,128)(2,1)S(1)} %copy-done.3, bf16[528,256]{1,0:T(8,128)(2,1)S(1)} %copy-done.5, ...), custom_call_target="tpu_custom_call" | custom-call | flops 1677721600 | bytes 4194304 | tf_op jit(solution)/shard_map/inner_stage/pallas_call | solution.py:218
  26.5 0.8 %copy-done = f32[512,256]{1,0:T(8,128)} copy-done((f32[512,256]{1,0:T(8,128)}, f32[512,256]{1,0:T(8,128)S(1)}, u32[]{:S(2)}) %copy-start) | copy-done | bytes 524312
  27.3 0.0 collective-permute-start.5
  27.3 2.4 %collective-permute-start.7 = (bf16[512,256]{1,0:T(8,128)(2,1)S(1)}, bf16[512,256]{1,0:T(8,128)(2,1)S(1)}, u32[]{:S(2)}, u32[]{:S(2)}) collective-permute-start(bf16[512,256]{1,0:T(8,128)(2,1)S(1)} %get-tuple-element.24), channel_id=1, source_target_pairs={{0,4},{4,0},{8,12},{12,8},{16,20},{20,16},{24,28},{28,24},{1,5},{5... | collective-permute-start | bytes 786440 | tf_op jit(solution)/shard_map/ppermute | solution.py:233
  29.6 0.0 collective-permute-done.2.refs_5_
  29.6 0.0 collective-permute-done.1.refs_4_
  29.6 0.0 copy-done.4
  29.7 6.9 %outer_stage.1 = (bf16[1024,256]{1,0:T(8,128)(2,1)}, f32[512,256]{1,0:T(8,128)S(1)}, bf16[512,256]{1,0:T(8,128)(2,1)S(1)}, bf16[512,256]{1,0:T(8,128)(2,1)S(1)}) custom-call(s32[1]{0:T(128)} %bitcast.index_ref.refs_0_, bf16[1024,256]{1,0:T(8,128)(2,1)S(1)} %copy-done.2, bf16[1024,256]{1,0:T(8,128)(2,1)S(1)} %copy-done.3, ...), custom_call_target="tpu_custom_call", output_to_operand_aliasing={{0}: (6, {})} | custom-call | flops 1677721600 | bytes 4194304 | tf_op jit(solution)/shard_map/outer_stage/pallas_call | solution.py:218
  36.6 0.8 %copy-done.1 = f32[512,256]{1,0:T(8,128)} copy-done((f32[512,256]{1,0:T(8,128)}, f32[512,256]{1,0:T(8,128)S(1)}, u32[]{:S(2)}) %copy-start.1) | copy-done | bytes 524312
  37.4 0.7 %collective-permute-start.4 = (bf16[512,256]{1,0:T(8,128)(2,1)S(1)}, bf16[512,256]{1,0:T(8,128)(2,1)S(1)}, u32[]{:S(2)}, u32[]{:S(2)}) collective-permute-start(bf16[512,256]{1,0:T(8,128)(2,1)S(1)} %get-tuple-element.20), channel_id=1, source_target_pairs={{0,0},{4,8},{8,4},{12,16},{16,12},{20,24},{24,20},{28,28},{1,1},{5... | collective-permute-start | bytes 786440 | tf_op jit(solution)/shard_map/ppermute | solution.py:236
  38.1 4.8 %collective-permute-start.6 = (bf16[512,256]{1,0:T(8,128)(2,1)S(1)}, bf16[512,256]{1,0:T(8,128)(2,1)S(1)}, u32[]{:S(2)}, u32[]{:S(2)}) collective-permute-start(bf16[512,256]{1,0:T(8,128)(2,1)S(1)} %get-tuple-element.23), channel_id=1, source_target_pairs={{8,0},{16,8},{24,16},{28,24},{20,28},{12,20},{4,12},{0,4},{9,1},{1... | collective-permute-start | bytes 786440 | tf_op jit(solution)/shard_map/ppermute | solution.py:237
  42.8 0.0 collective-permute-done.5.inner_b
  42.8 0.0 collective-permute-done.7.outer_b
  42.8 0.0 copy-start.7
  42.8 0.0 collective-permute-done.4.inner_a
  42.9 0.0 copy-start.8
  42.9 7.8 %collective-permute-done.6.outer_a = bf16[512,256]{1,0:T(8,128)(2,1)S(1)} collective-permute-done((bf16[512,256]{1,0:T(8,128)(2,1)S(1)}, bf16[512,256]{1,0:T(8,128)(2,1)S(1)}, u32[]{:S(2)}, u32[]{:S(2)}) %collective-permute-start.6) | collective-permute-done | bytes 262176 | tf_op jit(solution)/shard_map/ppermute | solution.py:237
  50.6 0.0 copy-done.6
  50.6 0.0 copy-done.7
  50.7 0.7 %copy-done.9 = bf16[512,256]{1,0:T(8,128)(2,1)} copy-done((bf16[512,256]{1,0:T(8,128)(2,1)}, bf16[512,256]{1,0:T(8,128)(2,1)S(1)}, u32[]{:S(2)}) %copy-start.9) | copy-done | bytes 262168
  51.3 2.4 %shard_map.77 = (bf16[1024,128]{1,0:T(8,128)(2,1)}, bf16[1024,128]{1,0:T(8,128)(2,1)}) custom-call(s32[1]{0:T(128)} %bitcast.index_ref.refs_0_, f32[512,256]{1,0:T(8,128)} %copy-done, bf16[512,256]{1,0:T(8,128)(2,1)} %copy-done.8, bf16[512,256]{1,0:T(8,128)(2,1)} %copy-done.6, f32[512,256]{1,0:T(8,128)} %copy-done.1, bf16[512,256]{1,0:T(8,128)(2,1)} %copy-done.9, ...), custom_call_target="tpu_custom_call" | custom-call | tf_op jit(solution)/shard_map/pallas_call | solution.py:240
  (8 shorter events, 0.0 us)
Async XLA Ops:
  0.6 17.9 %copy-start.2 = (bf16[1024,256]{1,0:T(8,128)(2,1)S(1)}, bf16[1024,256]{1,0:T(8,128)(2,1)}, u32[]{:S(2)}) copy-start(bf16[1024,256]{1,0:T(8,128)(2,1)} %refs_1_.3) | copy-start | bytes 1572868
  2.6 10.1 %collective-permute-start = (bf16[528,256]{1,0:T(8,128)(2,1)}, bf16[528,256]{1,0:T(8,128)(2,1)S(1)}, u32[]{:S(2)}, u32[]{:S(2)}) collective-permute-start(bf16[528,256]{1,0:T(8,128)(2,1)} %get-tuple-element.16.refs_3_), channel_id=1, source_target_pairs={{8,0},{16,8},{24,16},{28,24},{20,28},{12,20},{4,12},{0,4},{9,1},{1... | collective-permute-start | bytes 811016 | tf_op jit(solution)/shard_map/ppermute | solution.py:202
  5.6 13.0 %collective-permute-start.3 = (bf16[528,256]{1,0:T(8,128)(2,1)}, bf16[528,256]{1,0:T(8,128)(2,1)S(1)}, u32[]{:S(2)}, u32[]{:S(2)}) collective-permute-start(bf16[528,256]{1,0:T(8,128)(2,1)} %get-tuple-element.15.refs_3_), channel_id=1, source_target_pairs={{0,4},{4,0},{8,12},{12,8},{16,20},{20,16},{24,28},{28,24},{1,5},{5... | collective-permute-start | bytes 811016 | tf_op jit(solution)/shard_map/ppermute | solution.py:204
  7.1 22.5 %collective-permute-start.2 = (bf16[528,256]{1,0:T(8,128)(2,1)}, bf16[528,256]{1,0:T(8,128)(2,1)S(1)}, u32[]{:S(2)}, u32[]{:S(2)}) collective-permute-start(bf16[528,256]{1,0:T(8,128)(2,1)} %get-tuple-element.15.refs_3_), channel_id=1, source_target_pairs={{0,8},{8,16},{16,24},{24,28},{28,20},{20,12},{12,4},{4,0},{1,9},{9... | collective-permute-start | bytes 811016 | tf_op jit(solution)/shard_map/ppermute | solution.py:203
  12.8 16.9 %collective-permute-start.1 = (bf16[528,256]{1,0:T(8,128)(2,1)S(1)}, bf16[528,256]{1,0:T(8,128)(2,1)S(1)}, u32[]{:S(2)}, u32[]{:S(2)}) collective-permute-start(bf16[528,256]{1,0:T(8,128)(2,1)S(1)} %collective-permute-done.refs_5_), channel_id=1, source_target_pairs={{0,4},{4,0},{8,12},{12,8},{16,20},{20,16},{24,28},{28,24},{1,5},{5... | collective-permute-start | bytes 811016 | tf_op jit(solution)/shard_map/ppermute | solution.py:205
  18.6 1.0 %copy-start.3 = (bf16[1024,256]{1,0:T(8,128)(2,1)S(1)}, bf16[1024,256]{1,0:T(8,128)(2,1)}, u32[]{:S(2)}) copy-start(bf16[1024,256]{1,0:T(8,128)(2,1)} %refs_2_.3) | copy-start | bytes 1572868
  19.6 1.0 %copy-start.5 = (bf16[528,256]{1,0:T(8,128)(2,1)S(1)}, bf16[528,256]{1,0:T(8,128)(2,1)}, u32[]{:S(2)}) copy-start(bf16[528,256]{1,0:T(8,128)(2,1)} %get-tuple-element.16.refs_3_) | copy-start | bytes 811012
  20.6 9.1 %copy-start.4 = (bf16[528,256]{1,0:T(8,128)(2,1)S(1)}, bf16[528,256]{1,0:T(8,128)(2,1)}, u32[]{:S(2)}) copy-start(bf16[528,256]{1,0:T(8,128)(2,1)} %get-tuple-element.15.refs_3_) | copy-start | bytes 811012
  26.5 0.8 %copy-start = (f32[512,256]{1,0:T(8,128)}, f32[512,256]{1,0:T(8,128)S(1)}, u32[]{:S(2)}) copy-start(f32[512,256]{1,0:T(8,128)S(1)} %get-tuple-element.19.inner_own) | copy-start | bytes 1572868
  27.3 15.6 %collective-permute-start.5 = (bf16[512,256]{1,0:T(8,128)(2,1)S(1)}, bf16[512,256]{1,0:T(8,128)(2,1)S(1)}, u32[]{:S(2)}, u32[]{:S(2)}) collective-permute-start(bf16[512,256]{1,0:T(8,128)(2,1)S(1)} %get-tuple-element.21), channel_id=1, source_target_pairs={{0,8},{8,16},{16,24},{24,28},{28,20},{20,12},{12,4},{4,0},{1,9},{9... | collective-permute-start | bytes 786440 | tf_op jit(solution)/shard_map/ppermute | solution.py:234
  27.3 15.6 %collective-permute-start.7 = (bf16[512,256]{1,0:T(8,128)(2,1)S(1)}, bf16[512,256]{1,0:T(8,128)(2,1)S(1)}, u32[]{:S(2)}, u32[]{:S(2)}) collective-permute-start(bf16[512,256]{1,0:T(8,128)(2,1)S(1)} %get-tuple-element.24), channel_id=1, source_target_pairs={{0,4},{4,0},{8,12},{12,8},{16,20},{20,16},{24,28},{28,24},{1,5},{5... | collective-permute-start | bytes 786440 | tf_op jit(solution)/shard_map/ppermute | solution.py:233
  36.6 0.8 %copy-start.1 = (f32[512,256]{1,0:T(8,128)}, f32[512,256]{1,0:T(8,128)S(1)}, u32[]{:S(2)}) copy-start(f32[512,256]{1,0:T(8,128)S(1)} %get-tuple-element.22.outer_own) | copy-start | bytes 1572868
  37.4 5.5 %collective-permute-start.4 = (bf16[512,256]{1,0:T(8,128)(2,1)S(1)}, bf16[512,256]{1,0:T(8,128)(2,1)S(1)}, u32[]{:S(2)}, u32[]{:S(2)}) collective-permute-start(bf16[512,256]{1,0:T(8,128)(2,1)S(1)} %get-tuple-element.20), channel_id=1, source_target_pairs={{0,0},{4,8},{8,4},{12,16},{16,12},{20,24},{24,20},{28,28},{1,1},{5... | collective-permute-start | bytes 786440 | tf_op jit(solution)/shard_map/ppermute | solution.py:236
  38.1 12.6 %collective-permute-start.6 = (bf16[512,256]{1,0:T(8,128)(2,1)S(1)}, bf16[512,256]{1,0:T(8,128)(2,1)S(1)}, u32[]{:S(2)}, u32[]{:S(2)}) collective-permute-start(bf16[512,256]{1,0:T(8,128)(2,1)S(1)} %get-tuple-element.23), channel_id=1, source_target_pairs={{8,0},{16,8},{24,16},{28,24},{20,28},{12,20},{4,12},{0,4},{9,1},{1... | collective-permute-start | bytes 786440 | tf_op jit(solution)/shard_map/ppermute | solution.py:237
  42.8 7.8 %copy-start.6 = (bf16[512,256]{1,0:T(8,128)(2,1)}, bf16[512,256]{1,0:T(8,128)(2,1)S(1)}, u32[]{:S(2)}) copy-start(bf16[512,256]{1,0:T(8,128)(2,1)S(1)} %collective-permute-done.5.inner_b) | copy-start | bytes 786436
  42.8 7.8 %copy-start.7 = (bf16[512,256]{1,0:T(8,128)(2,1)}, bf16[512,256]{1,0:T(8,128)(2,1)S(1)}, u32[]{:S(2)}) copy-start(bf16[512,256]{1,0:T(8,128)(2,1)S(1)} %collective-permute-done.7.outer_b) | copy-start | bytes 786436
  42.9 7.8 %copy-start.8 = (bf16[512,256]{1,0:T(8,128)(2,1)}, bf16[512,256]{1,0:T(8,128)(2,1)S(1)}, u32[]{:S(2)}) copy-start(bf16[512,256]{1,0:T(8,128)(2,1)S(1)} %collective-permute-done.4.inner_a) | copy-start | bytes 786436
  50.6 0.7 %copy-start.9 = (bf16[512,256]{1,0:T(8,128)(2,1)}, bf16[512,256]{1,0:T(8,128)(2,1)S(1)}, u32[]{:S(2)}) copy-start(bf16[512,256]{1,0:T(8,128)(2,1)S(1)} %collective-permute-done.6.outer_a) | copy-start | bytes 786436

commit v2 on v1

--- a/solution.py
+++ b/solution.py
@@ -23,24 +23,22 @@
     return lax.dot_general(a, b, (((ca,), (cb,)), ((), ())), preferred_element_type=jnp.float32)
 
 
-def pack_kernel(index_ref, starts_ref, keys_ref, values_ref, inner_ref, outer_ref):
-    length = keys_ref.shape[0] // 2
-    width = keys_ref.shape[1]
+def halves(index):
+    parity = lax.rem(index, 2)
+    even = lax.rem(parity + lax.div(index, 2), 2) == 0
+    return 1 - parity, parity, even
+
+
+def pack_half(keys, values, starts, half, place):
+    length = keys.shape[0] // 2
+    width = keys.shape[1]
     blocks = length // BLOCK
-    index = index_ref[0]
-    parity = lax.rem(index, 2)
-    for out_ref, half in ((inner_ref, 1 - parity), (outer_ref, parity)):
-        rows = pl.ds(pl.multiple_of(half * length, length), length)
-        out_ref[:length, :width] = keys_ref[rows, :]
-        out_ref[:length, width:] = values_ref[rows, :]
-        row = lax.broadcasted_iota(jnp.int32, (MARK, 2 * width), 0)
-        marks = jnp.zeros((MARK, 2 * width), jnp.float32)
-        for j in range(blocks):
-            begin = starts_ref[half * blocks + j]
-            if j == 0:
-                begin = jnp.where((index == 0) & (half == 0), 1, begin)
-            marks = jnp.where(row == j, begin.astype(jnp.float32), marks)
-        out_ref[length:, :] = marks.astype(jnp.bfloat16)
+    both = [lax.dynamic_slice_in_dim(x, half * length, length, 0) for x in (keys, values)]
+    begins = lax.dynamic_slice_in_dim(starts, half * blocks, blocks, 0)
+    first = (lax.iota(jnp.int32, blocks) == 0) & (place == 0) & (half == 0)
+    begins = jnp.pad(jnp.where(first, 1, begins).astype(jnp.bfloat16), (0, MARK - blocks))
+    marks = jnp.broadcast_to(begins[:, None], (MARK, 2 * width))
+    return jnp.concatenate([jnp.concatenate(both, axis=1), marks], axis=0)
 
 
 def stage_kernel(with_half, index_ref, q_ref, g_ref, own_ref, near_ref, far_ref, *refs):
@@ -153,17 +151,264 @@
     own_out[...] = acc_ref[2 * length :]
 
 
-def sum_kernel(index_ref, inner_own, inner_a, inner_b, outer_own, outer_a, outer_b, dk_ref, dv_ref):
+def block_docs(pieces, length):
+    docs = []
+    count = jnp.zeros((1, TILE), jnp.float32)
+    for piece in pieces:
+        marks = piece[length:, :TILE].astype(jnp.float32)
+        for j in range(length // BLOCK):
+            count = count + marks[j : j + 1, :]
+            docs.append(count)
+    return docs
+
+
+def tile_docs(docs, first):
+    lane = lax.broadcasted_iota(jnp.int32, (1, TILE), 1)
+    own = docs[first]
+    for b in range(1, TILE // BLOCK):
+        own = jnp.where(lane >= b * BLOCK, docs[first + b], own)
+    return own
+
+
+def chunk_list(tile, length, wanted):
+    found = []
+    for c in range(WINDOW // TILE + 1):
+        piece, row = divmod((tile + c) * TILE, length)
+        if piece in wanted:
+            found.append((c, piece, row))
+    return found
+
+
+def triangle():
+    row = lax.broadcasted_iota(jnp.int32, (TILE, TILE), 0)
+    return row > lax.broadcasted_iota(jnp.int32, (TILE, TILE), 1)
+
+
+def masked_scores(c, keys, qt, after):
+    s = dot(keys, qt, 1, 1)
+    if c == 0:
+        s = jnp.where(after, s, NEG)
+    if c == WINDOW // TILE:
+        s = jnp.where(after, NEG, s)
+    return s
+
+
+def bias_rows(docs, first, own):
+    return [jnp.where(docs[first + b] == own, 0.0, NEG) for b in range(TILE // BLOCK)]
+
+
+def chunk_top(s, bias, top):
+    for b, row in enumerate(bias):
+        t = jnp.max(s[b * BLOCK : (b + 1) * BLOCK], axis=0, keepdims=True) + row
+        top = t if top is None else jnp.maximum(top, t)
+    return top
+
+
+def chunk_terms(s, bias, shift):
+    return jnp.concatenate(
+        [
+            jnp.exp2(s[b * BLOCK : (b + 1) * BLOCK] * exponent_scale + (row - shift))
+            for b, row in enumerate(bias)
+        ],
+        axis=0,
+    )
+
+
+def softmax_part(parts):
+    top = None
+    for s, dw, bias in parts:
+        top = chunk_top(s, bias, top)
+    shift = top * exponent_scale
+    total = jnp.zeros((1, TILE), jnp.float32)
+    mixed = jnp.zeros((1, TILE), jnp.float32)
+    for s, dw, bias in parts:
+        e = chunk_terms(s, bias, shift)
+        total = total + jnp.sum(e, axis=0, keepdims=True)
+        mixed = mixed + jnp.sum(e * dw, axis=0, keepdims=True)
+    return top, total, mixed
+
+
+def outer_stats_kernel(index_ref, q_ref, g_ref, own_ref, far_ref, stats_ref):
+    length = q_ref.shape[0] // 2
+    width = own_ref.shape[1] // 2
+    blocks = length // BLOCK
+    base = lax.rem(index_ref[0], 2) * length
+    docs = block_docs((far_ref, own_ref), length)
+    after = triangle()
+    for i in range(length // TILE):
+        own_docs = tile_docs(docs, blocks + i * (TILE // BLOCK))
+        rows = pl.ds(pl.multiple_of(base + i * TILE, TILE), TILE)
+        for h in range(QUERY_PER_KEY):
+            cols = slice(h * HEAD_SIZE, (h + 1) * HEAD_SIZE)
+            qt, gt = q_ref[rows, cols], g_ref[rows, cols]
+            for n, (piece, ref, first) in enumerate(((2, own_ref, blocks), (0, far_ref, 0))):
+                parts = []
+                for c, _, r in chunk_list(i, length, (piece,)):
+                    s = masked_scores(c, ref[r : r + TILE, :width], qt, after)
+                    dw = dot(ref[r : r + TILE, width:], gt, 1, 1)
+                    parts.append((s, dw, bias_rows(docs, first + r // BLOCK, own_docs)))
+                for k, value in enumerate(softmax_part(parts)):
+                    at = (h * 2 + n) * 3 + k
+                    stats_ref[at : at + 1, i * TILE : (i + 1) * TILE] = value
+
+
+def outer_near_kernel(
+    index_ref, q_ref, g_ref, own_ref, near_ref, part_ref, near_out, dq_out, stats_ref, acc_ref
+):
+    length = q_ref.shape[0] // 2
+    width = own_ref.shape[1] // 2
+    blocks = length // BLOCK
+    base = lax.rem(index_ref[0], 2) * length
+    docs = block_docs((near_ref, own_ref), length)
+    far_bias = jnp.where(docs[blocks - 1] == 0.0, 0.0, NEG)
+    key_t = jnp.transpose(near_ref[:length, :width])
+    for i in range(length // TILE):
+        own_docs = tile_docs(docs, blocks + i * (TILE // BLOCK))
+        rows = pl.ds(pl.multiple_of(base + i * TILE, TILE), TILE)
+        lanes = slice(i * TILE, (i + 1) * TILE)
+        members = []
+        chunks = chunk_list(i, length, (1,))
+        for h in range(QUERY_PER_KEY):
+            cols = slice(h * HEAD_SIZE, (h + 1) * HEAD_SIZE)
+            qt, gt = q_ref[rows, cols], g_ref[rows, cols]
+            at = h * 6
+            own_top, own_total, own_mixed = [part_ref[at + k : at + k + 1, lanes] for k in range(3)]
+            far_top, far_total, far_mixed = [
+                part_ref[at + 3 + k : at + 4 + k, lanes] for k in range(3)
+            ]
+            top = jnp.maximum(own_top, far_top + far_bias)
+            parts = []
+            for c, _, r in chunks:
+                s = dot(near_ref[r : r + TILE, :width], qt, 1, 1)
+                dw = dot(near_ref[r : r + TILE, width:], gt, 1, 1)
+                bias = bias_rows(docs, r // BLOCK, own_docs)
+                top = chunk_top(s, bias, top)
+                parts.append((s, dw, bias))
+            shift = top * exponent_scale
+            own_scale = jnp.exp2(own_top * exponent_scale - shift)
+            far_scale = jnp.exp2(far_top * exponent_scale + (far_bias - shift))
+            total = own_total * own_scale + far_total * far_scale
+            mixed = own_mixed * own_scale + far_mixed * far_scale
+            terms = []
+            for s, dw, bias in parts:
+                e = chunk_terms(s, bias, shift)
+                terms.append(e)
+                total = total + jnp.sum(e, axis=0, keepdims=True)
+                mixed = mixed + jnp.sum(e * dw, axis=0, keepdims=True)
+            inverse = 1.0 / total
+            row_dot = mixed * inverse
+            for k, value in enumerate((shift, inverse, row_dot)):
+                stats_ref[h * 3 + k : h * 3 + k + 1, lanes] = value
+            weights, dscores = [], []
+            dq_t = jnp.zeros((width, TILE), jnp.float32)
+            for e, (s, dw, bias), (c, _, r) in zip(terms, parts, chunks):
+                w = e * inverse
+                ds = (w * (dw - row_dot)).astype(jnp.bfloat16)
+                weights.append(w.astype(jnp.bfloat16))
+                dscores.append(ds)
+                dq_t = dq_t + dot(key_t[:, r : r + TILE], ds, 1, 0)
+            dq_out[h * width : (h + 1) * width, lanes] = dq_t
+            members.append((qt, gt, weights, dscores))
+        add_key_grads(acc_ref, members, [r for _, _, r in chunks], i == 0)
+    near_out[...] = acc_ref[...].astype(jnp.bfloat16)
+
+
+def add_key_grads(acc_ref, members, slots, first):
+    width = acc_ref.shape[1] // 2
+    q_all = jnp.concatenate([m[0] for m in members], axis=0)
+    g_all = jnp.concatenate([m[1] for m in members], axis=0)
+    for n, slot in enumerate(slots):
+        w_all = jnp.concatenate([m[2][n] for m in members], axis=1)
+        d_all = jnp.concatenate([m[3][n] for m in members], axis=1)
+        dk = dot(d_all, q_all, 1, 0) * query_scaling
+        dv = dot(w_all, g_all, 1, 0)
+        at = slice(slot, slot + TILE)
+        fresh = first if isinstance(first, bool) else slot in first
+        if not fresh:
+            dk = dk + acc_ref[at, :width]
+            dv = dv + acc_ref[at, width:]
+        acc_ref[at, :width] = dk
+        acc_ref[at, width:] = dv
+
+
+def outer_share_kernel(
+    wanted, last, index_ref, q_ref, g_ref, own_ref, near_ref, far_ref, stats_ref, dq_part_ref, *refs
+):
+    length = q_ref.shape[0] // 2
+    width = own_ref.shape[1] // 2
+    blocks = length // BLOCK
+    base = lax.rem(index_ref[0], 2) * length
+    if wanted == 2:
+        dq_in, dq_ref, grad_out, acc_ref = refs
+    else:
+        inner_near_ref, inner_far_ref, dq_ref, pair_out, first_out, second_out, acc_ref = refs
+    docs = block_docs((far_ref, near_ref, own_ref), length)
+    after = triangle()
+    piece = own_ref if wanted == 2 else far_ref
+    key_t = jnp.transpose(piece[:length, :width])
+    seen = set()
+    for i in range(length // TILE):
+        own_docs = tile_docs(docs, 2 * blocks + i * (TILE // BLOCK))
+        rows = pl.ds(pl.multiple_of(base + i * TILE, TILE), TILE)
+        lanes = slice(i * TILE, (i + 1) * TILE)
+        members = []
+        chunks = chunk_list(i, length, (wanted,))
+        for h in range(QUERY_PER_KEY):
+            cols = slice(h * HEAD_SIZE, (h + 1) * HEAD_SIZE)
+            qt, gt = q_ref[rows, cols], g_ref[rows, cols]
+            shift, inverse, row_dot = [
+                stats_ref[h * 3 + k : h * 3 + k + 1, lanes] for k in range(3)
+            ]
+            weights, dscores = [], []
+            dq_t = dq_part_ref[h * width : (h + 1) * width, lanes]
+            for c, p, r in chunks:
+                s = masked_scores(c, piece[r : r + TILE, :width], qt, after)
+                dw = dot(piece[r : r + TILE, width:], gt, 1, 1)
+                bias = bias_rows(docs, p * blocks + r // BLOCK, own_docs)
+                w = chunk_terms(s, bias, shift) * inverse
+                ds = (w * (dw - row_dot)).astype(jnp.bfloat16)
+                weights.append(w.astype(jnp.bfloat16))
+                dscores.append(ds)
+                dq_t = dq_t + dot(key_t[:, r : r + TILE], ds, 1, 0)
+            if wanted == 2:
+                dq_ref[rows, cols] = jnp.transpose(dq_t * query_scaling).astype(jnp.bfloat16)
+            else:
+                dq_ref[h * width : (h + 1) * width, lanes] = dq_t
+            members.append((qt, gt, weights, dscores))
+        slots = [r for _, _, r in chunks]
+        add_key_grads(acc_ref, members, slots, [x for x in slots if x not in seen])
+        seen.update(slots)
+    if wanted == 2:
+        other = pl.ds(pl.multiple_of(length - base, length), length)
+        dq_ref[other, :] = dq_in[other, :]
+        grad_out[...] = acc_ref[...]
+    else:
+        index = index_ref[0]
+        _, _, even = halves(index)
+        grad = acc_ref[...]
+        pair = inner_near_ref[...].astype(jnp.float32) + jnp.where(index == last, grad, 0.0)
+        pair_out[...] = pair.astype(jnp.bfloat16)
+        grad = grad.astype(jnp.bfloat16)
+        other = inner_far_ref[...]
+        first_out[...] = jnp.where(even, other, grad)
+        second_out[...] = jnp.where(even, grad, other)
+
+
+def early_sum_kernel(own, across, out):
+    out[...] = own[...] + across[...].astype(jnp.float32)
+
+
+def sum_kernel(index_ref, inner_own, outer_own, pair, first, second, dk_ref, dv_ref):
     length = inner_own.shape[0]
     width = dk_ref.shape[1]
-    parity = lax.rem(index_ref[0], 2)
+    inner, outer, even = halves(index_ref[0])
     f32 = jnp.float32
-    for half, own, a, b in (
-        (1 - parity, inner_own, inner_a, inner_b),
-        (parity, outer_own, outer_a, outer_b),
+    one, two = first[...].astype(f32), second[...].astype(f32)
+    for half, total in (
+        (inner, inner_own[...] + jnp.where(even, two, one)),
+        (outer, outer_own[...] + (pair[...].astype(f32) + jnp.where(even, one, two))),
     ):
         rows = pl.ds(pl.multiple_of(half * length, length), length)
-        total = own[...] + (a[...].astype(f32) + b[...].astype(f32))
         dk_ref[rows, :] = total[:, :width].astype(jnp.bfloat16)
         dv_ref[rows, :] = total[:, width:].astype(jnp.bfloat16)
 
@@ -172,11 +417,16 @@
     return pl.BlockSpec(memory_space=pltpu.SMEM)
 
 
+def hbm():
+    return pl.BlockSpec(memory_space=pltpu.HBM)
+
+
 def vmem():
     return pl.BlockSpec(memory_space=pltpu.VMEM)
 
 
-LIMIT = pltpu.CompilerParams(vmem_limit_bytes=48 * 1024 * 1024)
+LIMIT = pltpu.CompilerParams(vmem_limit_bytes=16 * 1024 * 1024)
+SMALL = pltpu.CompilerParams(vmem_limit_bytes=4 * 1024 * 1024)
 
 
 def on_device(queries, keys, values, grad_out, starts):
@@ -184,65 +434,116 @@
     width = keys.shape[1]
     count = lax.axis_size("seq")
     index = lax.axis_index("seq").astype(jnp.int32).reshape(1)
-    order = list(range(0, count, 2)) + list(range(count - 1, 0, -2))
-    clockwise = [(order[k], order[(k + 1) % count]) for k in range(count)]
-    counter = [(b, a) for a, b in clockwise]
+    assert count % 4 == 0
+    last = count - 1
     pairs = [(d, d ^ 1) for d in range(count)]
-    follow = dict(clockwise)
-    across = [(d, follow[d ^ 1]) for d in range(count)]
-
-    packed = jax.ShapeDtypeStruct((length + MARK, 2 * width), jnp.bfloat16)
-    inner, outer = pl.pallas_call(
-        pack_kernel,
-        out_shape=(packed, packed),
-        in_specs=[smem(), smem(), vmem(), vmem()],
-        out_specs=(vmem(), vmem()),
-    )(index, starts, keys, values)
-
-    inner_far = lax.ppermute(inner, "seq", counter)
-    outer_far = lax.ppermute(outer, "seq", clockwise)
+    first = [(d, d ^ 2) for d in range(count)]
+    second = [(d, ((d - 2) ^ 2) + 2) for d in range(2, count - 2)]
+    across = [(d, d + 1 if d % 2 else d - 1) for d in range(1, last)] + [(last, last)]
+    _, _, even = halves(index[0])
+
+    bf16, f32 = jnp.bfloat16, jnp.float32
+    narrow = jax.ShapeDtypeStruct((length, 2 * width), bf16)
+    wide = jax.ShapeDtypeStruct((length, 2 * width), f32)
+    rows = jax.ShapeDtypeStruct((16, length), f32)
+    like_q = jax.ShapeDtypeStruct(queries.shape, bf16)
+    unit = 2 * QUERY_PER_KEY * TILE * TILE * width
+
+    def call(kernel, outs, operands, name, work, scratch=(), specs=None, limit=LIMIT, alias=None,
+             out_specs=None):
+        return pl.pallas_call(
+            kernel,
+            out_shape=outs,
+            in_specs=specs or [smem()] + [vmem()] * (len(operands) - 1),
+            out_specs=out_specs or (vmem(),) * len(outs),
+            scratch_shapes=list(scratch),
+            input_output_aliases=alias or {},
+            compiler_params=limit,
+            cost_estimate=pl.CostEstimate(
+                flops=unit * work, bytes_accessed=1024 * 1024, transcendentals=0
+            ),
+            name=name,
+        )(*operands)
+
+    place = index[0]
+    parity = lax.rem(place, 2)
+    inner = pack_half(keys, values, starts, 1 - parity, place)
+    outer = pack_half(keys, values, starts, parity, place)
+    give_1 = jnp.where(even, outer, inner)
+    give_2 = jnp.where(even, inner, outer)
+
+    take_1 = lax.ppermute(give_1, "seq", first)
+    take_2 = lax.ppermute(give_2, "seq", second + [(last - 1, last), (last, last - 1), (0, 1), (1, 0)])
     inner_near = lax.ppermute(outer, "seq", pairs)
+    inner_far = jnp.where(even, take_1, take_2)
+    outer_far = jnp.where(even, take_2, take_1)
+    q, g = queries, grad_out
     outer_near = lax.ppermute(inner_far, "seq", pairs)
 
-    def stage(which, own, near, far, dq):
-        wide = jax.ShapeDtypeStruct((length, 2 * width), jnp.float32)
-        narrow = jax.ShapeDtypeStruct((length, 2 * width), jnp.bfloat16)
-        operands = [index, queries, grad_out, own, near, far]
-        specs = [smem()] + [vmem()] * 5
-        aliases = {}
-        if dq is not None:
-            aliases = {len(operands): 0}
-            operands.append(dq)
-            specs.append(pl.BlockSpec(memory_space=pltpu.VMEM))
-        flops = 10 * QUERY_PER_KEY * length * (WINDOW + TILE) * width
-        return pl.pallas_call(
-            lambda *refs: stage_kernel(which, *refs),
-            out_shape=(jax.ShapeDtypeStruct(queries.shape, jnp.bfloat16), wide, narrow, narrow),
-            in_specs=specs,
-            out_specs=(vmem(),) * 4,
-            scratch_shapes=[pltpu.VMEM((3 * length, 2 * width), jnp.float32)],
-            input_output_aliases=aliases,
-            compiler_params=LIMIT,
-            cost_estimate=pl.CostEstimate(
-                flops=flops, bytes_accessed=4 * 1024 * 1024, transcendentals=0
-            ),
-            name=which + "_stage",
-        )(*operands)
-
-    dq, inner_own, inner_g1, inner_g2 = stage("inner", inner, inner_near, inner_far, None)
-    outer_b = lax.ppermute(inner_g1, "seq", pairs)
-    inner_b = lax.ppermute(inner_g2, "seq", clockwise)
-    dq, outer_own, outer_g1, outer_g2 = stage("outer", outer, outer_near, outer_far, dq)
+    def after(value, *others):
+        return lax.optimization_barrier((value,) + others)[0]
+
+    grads = pltpu.VMEM((length, 2 * width), f32)
+    dq_rows = jax.ShapeDtypeStruct((QUERY_PER_KEY * width, length), f32)
+
+    (part,) = call(
+        outer_stats_kernel, (rows,), (index, q, g, outer, outer_far), "outer_stats", 12
+    )
+    dq, inner_own, inner_g1, inner_g2 = call(
+        lambda *refs: stage_kernel("inner", *refs),
+        (like_q, wide, narrow, narrow),
+        (index, after(q, part), g, inner, inner_near, inner_far),
+        "inner_stage",
+        50,
+        [pltpu.VMEM((3 * length, 2 * width), f32)],
+    )
+    outer_g1, dq_part, stats = call(
+        outer_near_kernel,
+        (narrow, dq_rows, rows),
+        (index, after(q, dq), g, outer, outer_near, part),
+        "outer_near",
+        20,
+        [grads],
+    )
     inner_a = lax.ppermute(outer_g1, "seq", across)
-    outer_a = lax.ppermute(outer_g2, "seq", counter)
-
-    half = jax.ShapeDtypeStruct(keys.shape, jnp.bfloat16)
-    dk, dv = pl.pallas_call(
+    dq_part, pair_give, give_1, give_2 = call(
+        lambda *refs: outer_share_kernel(0, last, *refs),
+        (dq_rows, narrow, narrow, narrow),
+        (index, q, g, outer, outer_near, outer_far, stats, dq_part, inner_g1, inner_g2),
+        "outer_far",
+        15,
+        [grads],
+    )
+    pair_take = lax.ppermute(pair_give, "seq", pairs)
+    take_1 = lax.ppermute(give_1, "seq", first)
+    take_2 = lax.ppermute(give_2, "seq", second + [(last - 1, last)])
+    dq, outer_own = call(
+        lambda *refs: outer_share_kernel(2, last, *refs),
+        (like_q, wide),
+        (index, q, g, outer, outer_near, outer_far, stats, dq_part, dq),
+        "outer_own",
+        15,
+        [grads],
+        alias={8: 0},
+    )
+    (inner_own,) = call(
+        early_sum_kernel,
+        (wide,),
+        (inner_own, inner_a),
+        "early_sum",
+        0,
+        specs=[vmem(), vmem()],
+        limit=SMALL,
+    )
+    half = jax.ShapeDtypeStruct(keys.shape, bf16)
+    dk, dv = call(
         sum_kernel,
-        out_shape=(half, half),
-        in_specs=[smem()] + [vmem()] * 6,
-        out_specs=(vmem(), vmem()),
-    )(index, inner_own, inner_a, inner_b, outer_own, outer_a, outer_b)
+        (half, half),
+        (index, inner_own, outer_own, pair_take, take_1, take_2),
+        "sum",
+        1,
+        limit=SMALL,
+    )
     return dq, dk, dv
 
 

time: 54.1 us -> 44.8 us (0.83)
  starting transfers between devices: 16.3 us -> 12.3 us
  waiting for transfers between devices: 15.3 us -> 12.7 us
  local copies, waits for them, and re-layouts: 4.28 us -> 1.79 us
  Pallas kernels: 17.2 us -> 16.6 us
    unnamed x20 -> x6, local copies, waits for them, and re-layouts: 4.28 us -> 0.66 us
    ppermute x5, starting transfers between devices: 11.7 us -> 9.57 us  [the longest x2 4.62 us: on_device(): take_1 = lax.ppermute(give_1, 'seq', first)]
    ppermute x5, waiting for transfers between devices: 11.8 us -> 9.85 us  [the longest x2 5.53 us: on_device(): take_1 = lax.ppermute(give_1, 'seq', first)]
    dynamic_slice x0 -> x1, local copies, waits for them, and re-layouts: none -> 1.14 us  [pack_half(): lax.dynamic_slice_in_dim(x, half * length, length, 0)]
    ppermute x1, starting transfers between devices: 1.58 us -> 0.53 us  [on_device(): inner_near = lax.ppermute(outer, 'seq', pairs)]
    ppermute x1, starting transfers between devices: 2.38 us -> 1.56 us  [on_device(): outer_near = lax.ppermute(inner_far, 'seq', pairs)]
    pallas_call x4 -> x7, Pallas kernels: 17.2 us -> 16.6 us  [call(): pl.pallas_call(kernel, out_shape=outs, in_specs=specs or [smem()] + [vmem...]
    ppermute x1, waiting for transfers between devices: 3.42 us -> 2.86 us  [on_device(): inner_near = lax.ppermute(outer, 'seq', pairs)]
  transfers between devices with their start and end apart: 8 -> 8, of which waited for: 3 -> 5; matrix products, arithmetic and copies ran while one was open for 0% -> 0% of each run, Pallas kernels for 24% -> 29%
where the time goes in v2:
time: 44.8 us; the launch traced here: 44.6 us
  Pallas kernels  16.6 us (37%)
  waiting for transfers between devices  12.7 us (28%)
  starting transfers between devices  12.3 us (27%)
  local copies, waits for them, and re-layouts  1.79 us (4%)
  between operations  0.74 us (2%)
    pallas_call x7, Pallas kernels, call(): pl.pallas_call(kernel, out_shape=outs, in_specs=specs or [smem()] + [vmem...  16.6 us
    ppermute x2, waiting for transfers between devices, on_device(): take_1 = lax.ppermute(give_1, 'seq', first)  5.53 us
    ppermute x2, starting transfers between devices, on_device(): take_1 = lax.ppermute(give_1, 'seq', first)  4.62 us
    ppermute x1, waiting for transfers between devices, on_device(): lax.ppermute(give_2, 'seq', second + [(last - 1, last), (last, last - 1),...  2.92 us
    ppermute x1, waiting for transfers between devices, on_device(): inner_near = lax.ppermute(outer, 'seq', pairs)  2.86 us
    ppermute x1, starting transfers between devices, on_device(): pair_take = lax.ppermute(pair_give, 'seq', pairs)  2.8 us
    ppermute x1, starting transfers between devices, on_device(): outer_near = lax.ppermute(inner_far, 'seq', pairs)  1.56 us
    ppermute x1, starting transfers between devices, on_device(): lax.ppermute(give_2, 'seq', second + [(last - 1, last), (last, last - 1),...  1.49 us
  transfers between devices with their start and end apart: 8, of which 5 were waited for; matrix products, arithmetic and copies ran while one was open for 0% of the time, Pallas kernels for 29%

profile of v2, /device:TPU:0, one launch (start us, length us, event | category | flops | bytes accessed | tf_op | source)
XLA Modules:
  0.0 44.6 jit_solution(6196470659759174844)
XLA Ops:
  0.7 0.0 copy-start.2
  0.7 0.6 %copy-done.2 = s32[8]{0:T(128)S(1)} copy-done((s32[8]{0:T(128)S(1)}, s32[8]{0:T(128)}, u32[]{:S(2)}) %copy-start.2) | copy-done | bytes 56
  1.3 0.1 fusion.3
  1.4 1.1 %constant_dynamic-slice_fusion = (bf16[512,128]{1,0:T(8,128)(2,1)S(1)}, bf16[512,128]{1,0:T(8,128)(2,1)S(1)}, bf16[512,128]{1,0:T(8,128)(2,1)S(1)}, bf16[512,128]{1,0:T(8,128)(2,1)S(1)}) fusion(bf16[1024,128]{1,0:T(8,128)(2,1)} %param.7, s32[]{:T(128)S(6)} %select_n.45, s32[]{:T(128)S(6)} %select_n.41, bf16[1024,128]{1,0:T(8,128)(2,1)} %param.6), kind=kLoop, calls=%fused_computation.12 | loop fusion | bytes 1048584 | tf_op jit(solution)/shard_map/dynamic_slice | solution.py:36
  2.6 0.2 broadcast_select_fusion.2
  2.8 3.1 %collective-permute-start = (bf16[528,256]{1,0:T(8,128)(2,1)S(1)}, bf16[528,256]{1,0:T(8,128)(2,1)S(1)}, u32[]{:S(2)}, u32[]{:S(2)}) collective-permute-start(bf16[528,256]{1,0:T(8,128)(2,1)S(1)} %get-tuple-element.40), channel_id=1, source_target_pairs={{0,8},{4,12},{8,0},{12,4},{16,24},{20,28},{24,16},{28,20},{1,9},{5... | collective-permute-start | bytes 811016 | tf_op jit(solution)/shard_map/ppermute | solution.py:475
  5.9 1.5 %collective-permute-start.1 = (bf16[528,256]{1,0:T(8,128)(2,1)S(1)}, bf16[528,256]{1,0:T(8,128)(2,1)S(1)}, u32[]{:S(2)}, u32[]{:S(2)}) collective-permute-start(bf16[528,256]{1,0:T(8,128)(2,1)S(1)} %get-tuple-element.39), channel_id=1, source_target_pairs={{8,16},{12,20},{16,8},{20,12},{24,28},{28,24},{0,4},{4,0},{9,17},{... | collective-permute-start | bytes 811016 | tf_op jit(solution)/shard_map/ppermute | solution.py:476
  7.4 0.0 copy-start
  7.4 0.0 copy-start.1
  7.4 0.5 %collective-permute-start.3 = (bf16[528,256]{1,0:T(8,128)(2,1)S(1)}, bf16[528,256]{1,0:T(8,128)(2,1)S(1)}, u32[]{:S(2)}, u32[]{:S(2)}) collective-permute-start(bf16[528,256]{1,0:T(8,128)(2,1)S(1)} %get-tuple-element.42.own_ref.refs_3_), channel_id=1, source_target_pairs={{0,4},{4,0},{8,12},{12,8},{16,20},{20,16},{24,28},{28,24},{1,5},{5... | collective-permute-start | bytes 811016 | tf_op jit(solution)/shard_map/ppermute | solution.py:477
  7.9 4.5 %collective-permute-done = bf16[528,256]{1,0:T(8,128)(2,1)S(1)} collective-permute-done((bf16[528,256]{1,0:T(8,128)(2,1)S(1)}, bf16[528,256]{1,0:T(8,128)(2,1)S(1)}, u32[]{:S(2)}, u32[]{:S(2)}) %collective-permute-start) | collective-permute-done | bytes 270368 | tf_op jit(solution)/shard_map/ppermute | solution.py:475
  12.3 2.9 %collective-permute-done.1 = bf16[528,256]{1,0:T(8,128)(2,1)S(1)} collective-permute-done((bf16[528,256]{1,0:T(8,128)(2,1)S(1)}, bf16[528,256]{1,0:T(8,128)(2,1)S(1)}, u32[]{:S(2)}, u32[]{:S(2)}) %collective-permute-start.1) | collective-permute-done | bytes 270368 | tf_op jit(solution)/shard_map/ppermute | solution.py:476
  15.3 1.6 %collective-permute-start.2 = (bf16[528,256]{1,0:T(8,128)(2,1)S(1)}, bf16[528,256]{1,0:T(8,128)(2,1)S(1)}, u32[]{:S(2)}, u32[]{:S(2)}) collective-permute-start(bf16[528,256]{1,0:T(8,128)(2,1)S(1)} %get-tuple-element.38.refs_5_), channel_id=1, source_target_pairs={{0,4},{4,0},{8,12},{12,8},{16,20},{20,16},{24,28},{28,24},{1,5},{5... | collective-permute-start | bytes 811016 | tf_op jit(solution)/shard_map/ppermute | solution.py:481
  16.9 0.0 copy-done
  16.9 0.0 copy-done.1
  16.9 1.3 %outer_stats.1.part_ref = f32[16,512]{1,0:T(8,128)S(1)} custom-call(s32[1]{0:T(128)} %bitcast.index_ref.refs_0_, bf16[1024,256]{1,0:T(8,128)(2,1)S(1)} %copy-done, bf16[1024,256]{1,0:T(8,128)(2,1)S(1)} %copy-done.1, bf16[528,256]{1,0:T(8,128)(2,1)S(1)} %get-tuple-element.42.own_ref.refs_3_, bf16[528,256]{1,0:T(8,128)(2,1)S(1)} %get-tuple-element.37.far_ref.refs_5_), custom_call_target="tpu_custom_call" | custom-call | flops 402653184 | bytes 1048576 | tf_op jit(solution)/shard_map/outer_stats/pallas_call | solution.py:454
  18.2 2.9 %collective-permute-done.3.refs_4_ = bf16[528,256]{1,0:T(8,128)(2,1)S(1)} collective-permute-done((bf16[528,256]{1,0:T(8,128)(2,1)S(1)}, bf16[528,256]{1,0:T(8,128)(2,1)S(1)}, u32[]{:S(2)}, u32[]{:S(2)}) %collective-permute-start.3) | collective-permute-done | bytes 270368 | tf_op jit(solution)/shard_map/ppermute | solution.py:477
  21.1 6.0 %inner_stage.1 = (bf16[1024,256]{1,0:T(8,128)(2,1)}, f32[512,256]{1,0:T(8,128)S(1)}, bf16[512,256]{1,0:T(8,128)(2,1)S(1)}, bf16[512,256]{1,0:T(8,128)(2,1)S(1)}) custom-call(s32[1]{0:T(128)} %bitcast.index_ref.refs_0_, bf16[1024,256]{1,0:T(8,128)(2,1)S(1)} %copy-done, bf16[1024,256]{1,0:T(8,128)(2,1)S(1)} %copy-done.1, ...), custom_call_target="tpu_custom_call" | custom-call | flops 1677721600 | bytes 1048576 | tf_op jit(solution)/shard_map/inner_stage/pallas_call | solution.py:454
  27.0 0.0 collective-permute-done.2.near_ref.refs_4_
  27.0 2.7 %outer_near.1 = (bf16[512,256]{1,0:T(8,128)(2,1)S(1)}, f32[256,512]{1,0:T(8,128)S(1)}, f32[16,512]{1,0:T(8,128)S(1)}) custom-call(s32[1]{0:T(128)} %bitcast.index_ref.refs_0_, bf16[1024,256]{1,0:T(8,128)(2,1)S(1)} %copy-done, bf16[1024,256]{1,0:T(8,128)(2,1)S(1)} %copy-done.1, bf16[528,256]{1,0:T(8,128)(2,1)S(1)} %get-tuple-element.42.own_ref.refs_3_, ...), custom_call_target="tpu_custom_call" | custom-call | flops 671088640 | bytes 1048576 | tf_op jit(solution)/shard_map/outer_near/pallas_call | solution.py:454
  29.7 0.7 %collective-permute-start.4 = (bf16[512,256]{1,0:T(8,128)(2,1)S(1)}, bf16[512,256]{1,0:T(8,128)(2,1)S(1)}, u32[]{:S(2)}, u32[]{:S(2)}) collective-permute-start(bf16[512,256]{1,0:T(8,128)(2,1)S(1)} %get-tuple-element.30), channel_id=1, source_target_pairs={{4,8},{8,4},{12,16},{16,12},{20,24},{24,20},{28,28},{5,9},{9,5},{1... | collective-permute-start | bytes 786440 | tf_op jit(solution)/shard_map/ppermute | solution.py:508
  30.4 2.0 %outer_far.1 = (f32[256,512]{1,0:T(8,128)S(1)}, bf16[512,256]{1,0:T(8,128)(2,1)S(1)}, bf16[512,256]{1,0:T(8,128)(2,1)S(1)}, bf16[512,256]{1,0:T(8,128)(2,1)S(1)}) custom-call(s32[1]{0:T(128)} %bitcast.index_ref.refs_0_, bf16[1024,256]{1,0:T(8,128)(2,1)S(1)} %copy-done, bf16[1024,256]{1,0:T(8,128)(2,1)S(1)} %copy-done.1, ...), custom_call_target="tpu_custom_call" | custom-call | flops 503316480 | bytes 1048576 | tf_op jit(solution)/shard_map/outer_far/pallas_call | solution.py:454
  32.3 2.8 %collective-permute-start.5 = (bf16[512,256]{1,0:T(8,128)(2,1)S(1)}, bf16[512,256]{1,0:T(8,128)(2,1)S(1)}, u32[]{:S(2)}, u32[]{:S(2)}) collective-permute-start(bf16[512,256]{1,0:T(8,128)(2,1)S(1)} %get-tuple-element.32), channel_id=1, source_target_pairs={{0,4},{4,0},{8,12},{12,8},{16,20},{20,16},{24,28},{28,24},{1,5},{5... | collective-permute-start | bytes 786440 | tf_op jit(solution)/shard_map/ppermute | solution.py:517
  35.1 1.5 %collective-permute-start.6 = (bf16[512,256]{1,0:T(8,128)(2,1)S(1)}, bf16[512,256]{1,0:T(8,128)(2,1)S(1)}, u32[]{:S(2)}, u32[]{:S(2)}) collective-permute-start(bf16[512,256]{1,0:T(8,128)(2,1)S(1)} %get-tuple-element.33), channel_id=1, source_target_pairs={{0,8},{4,12},{8,0},{12,4},{16,24},{20,28},{24,16},{28,20},{1,9},{5... | collective-permute-start | bytes 786440 | tf_op jit(solution)/shard_map/ppermute | solution.py:518
  36.7 0.7 %collective-permute-start.7 = (bf16[512,256]{1,0:T(8,128)(2,1)S(1)}, bf16[512,256]{1,0:T(8,128)(2,1)S(1)}, u32[]{:S(2)}, u32[]{:S(2)}) collective-permute-start(bf16[512,256]{1,0:T(8,128)(2,1)S(1)} %get-tuple-element.34), channel_id=1, source_target_pairs={{8,16},{12,20},{16,8},{20,12},{24,28},{9,17},{13,21},{17,9},{21,13... | collective-permute-start | bytes 786440 | tf_op jit(solution)/shard_map/ppermute | solution.py:519
  37.3 3.7 %outer_own.1 = (bf16[1024,256]{1,0:T(8,128)(2,1)}, f32[512,256]{1,0:T(8,128)S(1)}) custom-call(s32[1]{0:T(128)} %bitcast.index_ref.refs_0_, bf16[1024,256]{1,0:T(8,128)(2,1)S(1)} %copy-done, bf16[1024,256]{1,0:T(8,128)(2,1)S(1)} %copy-done.1, bf16[528,256]{1,0:T(8,128)(2,1)S(1)} %get-tuple-element.42.own_ref.refs_3_, ...), custom_call_target="tpu_custom_call", output_to_operand_aliasing={{0}: (8, {})} | custom-call | flops 503316480 | bytes 1048576 | tf_op jit(solution)/shard_map/outer_own/pallas_call | solution.py:454
  41.1 0.0 collective-permute-done.4.across
  41.1 1.4 %collective-permute-done.5.pair = bf16[512,256]{1,0:T(8,128)(2,1)S(1)} collective-permute-done((bf16[512,256]{1,0:T(8,128)(2,1)S(1)}, bf16[512,256]{1,0:T(8,128)(2,1)S(1)}, u32[]{:S(2)}, u32[]{:S(2)}) %collective-permute-start.5) | collective-permute-done | bytes 262176 | tf_op jit(solution)/shard_map/ppermute | solution.py:517
  42.5 1.1 %collective-permute-done.6.first = bf16[512,256]{1,0:T(8,128)(2,1)S(1)} collective-permute-done((bf16[512,256]{1,0:T(8,128)(2,1)S(1)}, bf16[512,256]{1,0:T(8,128)(2,1)S(1)}, u32[]{:S(2)}, u32[]{:S(2)}) %collective-permute-start.6) | collective-permute-done | bytes 262176 | tf_op jit(solution)/shard_map/ppermute | solution.py:518
  43.6 0.0 collective-permute-done.7.second
  43.6 1.0 %sum.1 = (bf16[1024,128]{1,0:T(8,128)(2,1)}, bf16[1024,128]{1,0:T(8,128)(2,1)}) custom-call(s32[1]{0:T(128)} %bitcast.index_ref.refs_0_, f32[512,256]{1,0:T(8,128)S(1)} %early_sum.1.inner_own, f32[512,256]{1,0:T(8,128)S(1)} %get-tuple-element.31.outer_own, bf16[512,256]{1,0:T(8,128)(2,1)S(1)} %collective-permute-done.5.pair, ...), custom_call_target="tpu_custom_call" | custom-call | flops 33554432 | bytes 1048576 | tf_op jit(solution)/shard_map/sum/pallas_call | solution.py:454
  (3 shorter events, 0.1 us)
Async XLA Ops:
  0.7 0.7 %copy-start.2 = (s32[8]{0:T(128)S(1)}, s32[8]{0:T(128)}, u32[]{:S(2)}) copy-start(s32[8]{0:T(128)} %param.9) | copy-start | bytes 100
  2.8 9.6 %collective-permute-start = (bf16[528,256]{1,0:T(8,128)(2,1)S(1)}, bf16[528,256]{1,0:T(8,128)(2,1)S(1)}, u32[]{:S(2)}, u32[]{:S(2)}) collective-permute-start(bf16[528,256]{1,0:T(8,128)(2,1)S(1)} %get-tuple-element.40), channel_id=1, source_target_pairs={{0,8},{4,12},{8,0},{12,4},{16,24},{20,28},{24,16},{28,20},{1,9},{5... | collective-permute-start | bytes 811016 | tf_op jit(solution)/shard_map/ppermute | solution.py:475
  5.9 9.4 %collective-permute-start.1 = (bf16[528,256]{1,0:T(8,128)(2,1)S(1)}, bf16[528,256]{1,0:T(8,128)(2,1)S(1)}, u32[]{:S(2)}, u32[]{:S(2)}) collective-permute-start(bf16[528,256]{1,0:T(8,128)(2,1)S(1)} %get-tuple-element.39), channel_id=1, source_target_pairs={{8,16},{12,20},{16,8},{20,12},{24,28},{28,24},{0,4},{4,0},{9,17},{... | collective-permute-start | bytes 811016 | tf_op jit(solution)/shard_map/ppermute | solution.py:476
  7.4 9.5 %copy-start = (bf16[1024,256]{1,0:T(8,128)(2,1)S(1)}, bf16[1024,256]{1,0:T(8,128)(2,1)}, u32[]{:S(2)}) copy-start(bf16[1024,256]{1,0:T(8,128)(2,1)} %refs_1_.4) | copy-start | bytes 1572868
  7.4 9.5 %copy-start.1 = (bf16[1024,256]{1,0:T(8,128)(2,1)S(1)}, bf16[1024,256]{1,0:T(8,128)(2,1)}, u32[]{:S(2)}) copy-start(bf16[1024,256]{1,0:T(8,128)(2,1)} %refs_2_.5) | copy-start | bytes 1572868
  7.4 13.7 %collective-permute-start.3 = (bf16[528,256]{1,0:T(8,128)(2,1)S(1)}, bf16[528,256]{1,0:T(8,128)(2,1)S(1)}, u32[]{:S(2)}, u32[]{:S(2)}) collective-permute-start(bf16[528,256]{1,0:T(8,128)(2,1)S(1)} %get-tuple-element.42.own_ref.refs_3_), channel_id=1, source_target_pairs={{0,4},{4,0},{8,12},{12,8},{16,20},{20,16},{24,28},{28,24},{1,5},{5... | collective-permute-start | bytes 811016 | tf_op jit(solution)/shard_map/ppermute | solution.py:477
  15.3 11.7 %collective-permute-start.2 = (bf16[528,256]{1,0:T(8,128)(2,1)S(1)}, bf16[528,256]{1,0:T(8,128)(2,1)S(1)}, u32[]{:S(2)}, u32[]{:S(2)}) collective-permute-start(bf16[528,256]{1,0:T(8,128)(2,1)S(1)} %get-tuple-element.38.refs_5_), channel_id=1, source_target_pairs={{0,4},{4,0},{8,12},{12,8},{16,20},{20,16},{24,28},{28,24},{1,5},{5... | collective-permute-start | bytes 811016 | tf_op jit(solution)/shard_map/ppermute | solution.py:481
  29.7 11.4 %collective-permute-start.4 = (bf16[512,256]{1,0:T(8,128)(2,1)S(1)}, bf16[512,256]{1,0:T(8,128)(2,1)S(1)}, u32[]{:S(2)}, u32[]{:S(2)}) collective-permute-start(bf16[512,256]{1,0:T(8,128)(2,1)S(1)} %get-tuple-element.30), channel_id=1, source_target_pairs={{4,8},{8,4},{12,16},{16,12},{20,24},{24,20},{28,28},{5,9},{9,5},{1... | collective-permute-start | bytes 786440 | tf_op jit(solution)/shard_map/ppermute | solution.py:508
  32.3 10.2 %collective-permute-start.5 = (bf16[512,256]{1,0:T(8,128)(2,1)S(1)}, bf16[512,256]{1,0:T(8,128)(2,1)S(1)}, u32[]{:S(2)}, u32[]{:S(2)}) collective-permute-start(bf16[512,256]{1,0:T(8,128)(2,1)S(1)} %get-tuple-element.32), channel_id=1, source_target_pairs={{0,4},{4,0},{8,12},{12,8},{16,20},{20,16},{24,28},{28,24},{1,5},{5... | collective-permute-start | bytes 786440 | tf_op jit(solution)/shard_map/ppermute | solution.py:517
  35.1 8.4 %collective-permute-start.6 = (bf16[512,256]{1,0:T(8,128)(2,1)S(1)}, bf16[512,256]{1,0:T(8,128)(2,1)S(1)}, u32[]{:S(2)}, u32[]{:S(2)}) collective-permute-start(bf16[512,256]{1,0:T(8,128)(2,1)S(1)} %get-tuple-element.33), channel_id=1, source_target_pairs={{0,8},{4,12},{8,0},{12,4},{16,24},{20,28},{24,16},{28,20},{1,9},{5... | collective-permute-start | bytes 786440 | tf_op jit(solution)/shard_map/ppermute | solution.py:518
  36.7 6.9 %collective-permute-start.7 = (bf16[512,256]{1,0:T(8,128)(2,1)S(1)}, bf16[512,256]{1,0:T(8,128)(2,1)S(1)}, u32[]{:S(2)}, u32[]{:S(2)}) collective-permute-start(bf16[512,256]{1,0:T(8,128)(2,1)S(1)} %get-tuple-element.34), channel_id=1, source_target_pairs={{8,16},{12,20},{16,8},{20,12},{24,28},{9,17},{13,21},{17,9},{21,13... | collective-permute-start | bytes 786440 | tf_op jit(solution)/shard_map/ppermute | solution.py:519

commit v3 on v2

--- a/solution.py
+++ b/solution.py
@@ -34,6 +34,7 @@
     width = keys.shape[1]
     blocks = length // BLOCK
     both = [lax.dynamic_slice_in_dim(x, half * length, length, 0) for x in (keys, values)]
+    starts = lax.optimization_barrier((starts, *both))[0]
     begins = lax.dynamic_slice_in_dim(starts, half * blocks, blocks, 0)
     first = (lax.iota(jnp.int32, blocks) == 0) & (place == 0) & (half == 0)
     begins = jnp.pad(jnp.where(first, 1, begins).astype(jnp.bfloat16), (0, MARK - blocks))
@@ -41,111 +42,75 @@
     return jnp.concatenate([jnp.concatenate(both, axis=1), marks], axis=0)
 
 
-def stage_kernel(with_half, index_ref, q_ref, g_ref, own_ref, near_ref, far_ref, *refs):
-    dq_ref, own_out, near_out, far_out, acc_ref = refs[-5:]
+def inner_stage_kernel(
+    index_ref, q_ref, g_ref, own_ref, near_ref, far_ref,
+    dq_ref, own_out, near_out, far_out, acc_ref,
+):
     length = q_ref.shape[0] // 2
     width = own_ref.shape[1] // 2
     blocks = length // BLOCK
-    tiles = length // TILE
-    per = TILE // BLOCK
-    chunks = WINDOW // TILE + 1
-    index = index_ref[0]
-    parity = lax.rem(index, 2)
-    half = 1 - parity if with_half == "inner" else parity
-    base = half * length
+    base = (1 - lax.rem(index_ref[0], 2)) * length
     pieces = (far_ref, near_ref, own_ref)
-
-    docs = []
-    count = jnp.zeros((1, TILE), jnp.float32)
-    for piece in pieces:
-        marks = piece[length:, :TILE].astype(jnp.float32)
-        for j in range(blocks):
-            count = count + marks[j : j + 1, :]
-            docs.append(count)
-    lane = lax.broadcasted_iota(jnp.int32, (1, TILE), 1)
-    row2 = lax.broadcasted_iota(jnp.int32, (TILE, TILE), 0)
-    col2 = lax.broadcasted_iota(jnp.int32, (TILE, TILE), 1)
-    after = row2 > col2
-
+    docs = block_docs(pieces, length)
+    after = triangle()
     key_t = [jnp.transpose(p[:length, :width]) for p in pieces]
-
-    started = [False] * (3 * length // TILE)
-    for i in range(tiles):
-        own_docs = docs[2 * blocks + i * per]
-        for b in range(1, per):
-            own_docs = jnp.where(lane >= b * BLOCK, docs[2 * blocks + i * per + b], own_docs)
-        bias = []
-        for c in range(chunks):
-            bias.append(
-                [jnp.where(docs[(i + c) * per + b] == own_docs, 0.0, NEG) for b in range(per)]
-            )
+    steps = [(i, h) for i in range(length // TILE) for h in range(QUERY_PER_KEY)]
+
+    def products(i, h):
         rows = pl.ds(pl.multiple_of(base + i * TILE, TILE), TILE)
-        members = []
-        for h in range(QUERY_PER_KEY):
-            cols = slice(h * HEAD_SIZE, (h + 1) * HEAD_SIZE)
-            qt = q_ref[rows, cols]
-            gt = g_ref[rows, cols]
-            scores, dweights = [], []
-            top = None
-            for c in range(chunks):
-                p, r = divmod((i + c) * TILE, length)
-                s = dot(pieces[p][r : r + TILE, :width], qt, 1, 1)
-                if c == 0:
-                    s = jnp.where(after, s, NEG)
-                if c == chunks - 1:
-                    s = jnp.where(after, NEG, s)
-                scores.append(s)
-                dweights.append(dot(pieces[p][r : r + TILE, width:], gt, 1, 1))
-                for b in range(per):
-                    t = jnp.max(s[b * BLOCK : (b + 1) * BLOCK], axis=0, keepdims=True) + bias[c][b]
-                    top = t if top is None else jnp.maximum(top, t)
-            shift = top * exponent_scale
-            total = jnp.zeros((1, TILE), jnp.float32)
-            row_dot = jnp.zeros((1, TILE), jnp.float32)
-            terms = []
-            for c in range(chunks):
-                parts = [
-                    jnp.exp2(
-                        scores[c][b * BLOCK : (b + 1) * BLOCK] * exponent_scale
-                        + (bias[c][b] - shift)
-                    )
-                    for b in range(per)
-                ]
-                e = jnp.concatenate(parts, axis=0)
-                terms.append(e)
-                total = total + jnp.sum(e, axis=0, keepdims=True)
-                row_dot = row_dot + jnp.sum(e * dweights[c], axis=0, keepdims=True)
-            inverse = 1.0 / total
-            row_dot = row_dot * inverse
-            weights, dscores = [], []
-            dq_t = jnp.zeros((width, TILE), jnp.float32)
-            for c in range(chunks):
-                w = terms[c] * inverse
-                ds = (w * (dweights[c] - row_dot)).astype(jnp.bfloat16)
-                weights.append(w.astype(jnp.bfloat16))
-                dscores.append(ds)
-                p, r = divmod((i + c) * TILE, length)
-                dq_t = dq_t + dot(key_t[p][:, r : r + TILE], ds, 1, 0)
-            dq_ref[rows, cols] = jnp.transpose(dq_t * query_scaling).astype(jnp.bfloat16)
-            members.append((qt, gt, weights, dscores))
-        q_all = jnp.concatenate([m[0] for m in members], axis=0)
-        g_all = jnp.concatenate([m[1] for m in members], axis=0)
-        for c in range(chunks):
-            w_all = jnp.concatenate([m[2][c] for m in members], axis=1)
-            d_all = jnp.concatenate([m[3][c] for m in members], axis=1)
-            dk = dot(d_all, q_all, 1, 0) * query_scaling
-            dv = dot(w_all, g_all, 1, 0)
-            slot = i + c
-            at = slice(slot * TILE, (slot + 1) * TILE)
-            if started[slot]:
-                dk = dk + acc_ref[at, :width]
-                dv = dv + acc_ref[at, width:]
-            started[slot] = True
-            acc_ref[at, :width] = dk
-            acc_ref[at, width:] = dv
-    if len(refs) == 6:
-        other = pl.ds(pl.multiple_of(length - base, length), length)
-        dq_ref[other, :] = refs[0][other, :]
+        cols = slice(h * HEAD_SIZE, (h + 1) * HEAD_SIZE)
+        qt, gt = q_ref[rows, cols], g_ref[rows, cols]
+        own_docs = tile_docs(docs, 2 * blocks + i * (TILE // BLOCK))
+        parts = []
+        for c, p, r in chunk_list(i, length, (0, 1, 2)):
+            s = masked_scores(c, pieces[p][r : r + TILE, :width], qt, after)
+            dw = dot(pieces[p][r : r + TILE, width:], gt, 1, 1)
+            parts.append((s, dw, bias_rows(docs, p * blocks + r // BLOCK, own_docs)))
+        return qt, gt, parts
+
+    def shares(i, h, parts):
+        top = None
+        for s, dw, bias in parts:
+            top = chunk_top(s, bias, top)
+        shift = top * exponent_scale
+        total = jnp.zeros((1, TILE), jnp.float32)
+        mixed = jnp.zeros((1, TILE), jnp.float32)
+        terms = []
+        for s, dw, bias in parts:
+            e = chunk_terms(s, bias, shift)
+            terms.append(e)
+            total = total + jnp.sum(e, axis=0, keepdims=True)
+            mixed = mixed + jnp.sum(e * dw, axis=0, keepdims=True)
+        inverse = 1.0 / total
+        row_dot = mixed * inverse
+        weights, dscores = [], []
+        for e, (s, dw, bias) in zip(terms, parts):
+            w = e * inverse
+            dscores.append((w * (dw - row_dot)).astype(jnp.bfloat16))
+            weights.append(w.astype(jnp.bfloat16))
+        return weights, dscores
+
+    def query_grad(i, h, dscores):
+        dq_t = jnp.zeros((width, TILE), jnp.float32)
+        for ds, (c, p, r) in zip(dscores, chunk_list(i, length, (0, 1, 2))):
+            dq_t = dq_t + dot(key_t[p][:, r : r + TILE], ds, 1, 0)
+        dq_ref[h * width : (h + 1) * width, i * TILE : (i + 1) * TILE] = dq_t
+
+    seen = set()
+    members = []
+    ready = products(*steps[0])
+    for n, (i, h) in enumerate(steps):
+        qt, gt, parts = ready
+        if n + 1 < len(steps):
+            ready = products(*steps[n + 1])
+        weights, dscores = shares(i, h, parts)
+        query_grad(i, h, dscores)
+        members.append((qt, gt, weights, dscores))
+        if h == QUERY_PER_KEY - 1:
+            slots = [p * length + r for _, p, r in chunk_list(i, length, (0, 1, 2))]
+            add_key_grads(acc_ref, members, slots, [x for x in slots if x not in seen])
+            seen.update(slots)
+            members = []
     far_out[...] = acc_ref[:length].astype(jnp.bfloat16)
     near_out[...] = acc_ref[length : 2 * length].astype(jnp.bfloat16)
     own_out[...] = acc_ref[2 * length :]
@@ -341,7 +306,7 @@
     if wanted == 2:
         dq_in, dq_ref, grad_out, acc_ref = refs
     else:
-        inner_near_ref, inner_far_ref, dq_ref, pair_out, first_out, second_out, acc_ref = refs
+        inner_far_ref, dq_ref, first_out, second_out, acc_ref = refs
     docs = block_docs((far_ref, near_ref, own_ref), length)
     after = triangle()
     piece = own_ref if wanted == 2 else far_ref
@@ -380,37 +345,51 @@
         seen.update(slots)
     if wanted == 2:
         other = pl.ds(pl.multiple_of(length - base, length), length)
-        dq_ref[other, :] = dq_in[other, :]
+        for h in range(QUERY_PER_KEY):
+            span = slice(h * width, (h + 1) * width)
+            whole = jnp.transpose(dq_in[span, :] * query_scaling)
+            dq_ref[other, span] = whole.astype(jnp.bfloat16)
         grad_out[...] = acc_ref[...]
     else:
         index = index_ref[0]
         _, _, even = halves(index)
         grad = acc_ref[...]
-        pair = inner_near_ref[...].astype(jnp.float32) + jnp.where(index == last, grad, 0.0)
-        pair_out[...] = pair.astype(jnp.bfloat16)
         grad = grad.astype(jnp.bfloat16)
         other = inner_far_ref[...]
         first_out[...] = jnp.where(even, other, grad)
         second_out[...] = jnp.where(even, grad, other)
 
 
-def early_sum_kernel(own, across, out):
-    out[...] = own[...] + across[...].astype(jnp.float32)
-
-
-def sum_kernel(index_ref, inner_own, outer_own, pair, first, second, dk_ref, dv_ref):
+def early_sum_kernel(last, index_ref, own, across, kept, out):
+    grad = jnp.where(index_ref[0] == last, kept[...], across[...])
+    out[...] = own[...] + grad.astype(jnp.float32)
+
+
+def sum_kernel(
+    index_ref, inner_own, outer_own, pair, first, second, dk_ref, dv_ref, held_ref, sems
+):
     length = inner_own.shape[0]
     width = dk_ref.shape[1]
     inner, outer, even = halves(index_ref[0])
     f32 = jnp.float32
     one, two = first[...].astype(f32), second[...].astype(f32)
-    for half, total in (
-        (inner, inner_own[...] + jnp.where(even, two, one)),
-        (outer, outer_own[...] + (pair[...].astype(f32) + jnp.where(even, one, two))),
-    ):
+    copies = []
+    for n, half in enumerate((inner, outer)):
+        if n == 0:
+            total = inner_own[...] + jnp.where(even, two, one)
+        else:
+            total = outer_own[...] + (pair[...].astype(f32) + jnp.where(even, one, two))
         rows = pl.ds(pl.multiple_of(half * length, length), length)
-        dk_ref[rows, :] = total[:, :width].astype(jnp.bfloat16)
-        dv_ref[rows, :] = total[:, width:].astype(jnp.bfloat16)
+        for m, out in enumerate((dk_ref, dv_ref)):
+            held_ref[2 * n + m] = total[:, m * width : (m + 1) * width].astype(jnp.bfloat16)
+            copies.append(
+                pltpu.make_async_copy(
+                    held_ref.at[2 * n + m], out.at[rows, :], sems.at[2 * n + m]
+                )
+            )
+            copies[-1].start()
+    for copy in copies:
+        copy.wait()
 
 
 def smem():
@@ -439,7 +418,7 @@
     pairs = [(d, d ^ 1) for d in range(count)]
     first = [(d, d ^ 2) for d in range(count)]
     second = [(d, ((d - 2) ^ 2) + 2) for d in range(2, count - 2)]
-    across = [(d, d + 1 if d % 2 else d - 1) for d in range(1, last)] + [(last, last)]
+    across = [(d, d + 1 if d % 2 else d - 1) for d in range(1, last)]
     _, _, even = halves(index[0])
 
     bf16, f32 = jnp.bfloat16, jnp.float32
@@ -473,7 +452,14 @@
     give_2 = jnp.where(even, inner, outer)
 
     take_1 = lax.ppermute(give_1, "seq", first)
-    take_2 = lax.ppermute(give_2, "seq", second + [(last - 1, last), (last, last - 1), (0, 1), (1, 0)])
+    heads = lax.axis_size("head")
+
+    def spread(links):
+        return [(a * heads + h, b * heads + h) for a, b in links for h in range(heads)]
+
+    fold = [(last - 1, last), (last, last - 1)]
+    ends = [(d * heads + h, d * heads + (h ^ 1)) for d in (0, 1) for h in range(heads)]
+    take_2 = lax.ppermute(give_2, ("seq", "head"), spread(second + fold) + ends)
     inner_near = lax.ppermute(outer, "seq", pairs)
     inner_far = jnp.where(even, take_1, take_2)
     outer_far = jnp.where(even, take_2, take_1)
@@ -490,13 +476,14 @@
         outer_stats_kernel, (rows,), (index, q, g, outer, outer_far), "outer_stats", 12
     )
     dq, inner_own, inner_g1, inner_g2 = call(
-        lambda *refs: stage_kernel("inner", *refs),
-        (like_q, wide, narrow, narrow),
+        inner_stage_kernel,
+        (dq_rows, wide, narrow, narrow),
         (index, after(q, part), g, inner, inner_near, inner_far),
         "inner_stage",
         50,
         [pltpu.VMEM((3 * length, 2 * width), f32)],
     )
+    pair_take = lax.ppermute(inner_g1, "seq", pairs)
     outer_g1, dq_part, stats = call(
         outer_near_kernel,
         (narrow, dq_rows, rows),
@@ -505,18 +492,18 @@
         20,
         [grads],
     )
-    inner_a = lax.ppermute(outer_g1, "seq", across)
-    dq_part, pair_give, give_1, give_2 = call(
+    turns = [(d * heads + h, d * heads + (h ^ 1)) for d in (0, last) for h in range(heads)]
+    inner_a = lax.ppermute(outer_g1, ("seq", "head"), spread(across) + turns)
+    dq_part, give_1, give_2 = call(
         lambda *refs: outer_share_kernel(0, last, *refs),
-        (dq_rows, narrow, narrow, narrow),
-        (index, q, g, outer, outer_near, outer_far, stats, dq_part, inner_g1, inner_g2),
+        (dq_rows, narrow, narrow),
+        (index, q, g, outer, outer_near, outer_far, stats, dq_part, inner_g2),
         "outer_far",
         15,
         [grads],
     )
-    pair_take = lax.ppermute(pair_give, "seq", pairs)
     take_1 = lax.ppermute(give_1, "seq", first)
-    take_2 = lax.ppermute(give_2, "seq", second + [(last - 1, last)])
+    take_2 = lax.ppermute(give_2, ("seq", "head"), spread(second + fold) + ends)
     dq, outer_own = call(
         lambda *refs: outer_share_kernel(2, last, *refs),
         (like_q, wide),
@@ -524,15 +511,13 @@
         "outer_own",
         15,
         [grads],
-        alias={8: 0},
     )
     (inner_own,) = call(
-        early_sum_kernel,
+        lambda *refs: early_sum_kernel(last, *refs),
         (wide,),
-        (inner_own, inner_a),
+        (index, inner_own, inner_a, outer_g1),
         "early_sum",
         0,
-        specs=[vmem(), vmem()],
         limit=SMALL,
     )
     half = jax.ShapeDtypeStruct(keys.shape, bf16)
@@ -542,7 +527,9 @@
         (index, inner_own, outer_own, pair_take, take_1, take_2),
         "sum",
         1,
+        [pltpu.VMEM((4, length, width), bf16), pltpu.SemaphoreType.DMA((4,))],
         limit=SMALL,
+        out_specs=(hbm(),) * 2,
     )
     return dq, dk, dv
 

time: 44.8 us -> 42.2 us (0.942)
  the two profiles are of different devices: /device:TPU:0 before, /device:TPU:24 now
where the time goes in v3:
time: 42.2 us; the launch traced here: 42 us
  waiting for transfers between devices  15.4 us (36%)
  Pallas kernels  14.5 us (34%)
  starting transfers between devices  9.26 us (22%)
  local copies, waits for them, and re-layouts  1.74 us (4%)
  between operations  0.78 us (2%)
    pallas_call x7, Pallas kernels, call(): pl.pallas_call(kernel, out_shape=outs, in_specs=specs or [smem()] + [vmem...  14.5 us
    ppermute x2, waiting for transfers between devices, on_device(): take_1 = lax.ppermute(give_1, 'seq', first)  5.74 us
    ppermute x2, waiting for transfers between devices, on_device(): take_2 = lax.ppermute(give_2, ('seq', 'head'), spread(second + fold) + ends)  5.44 us
    ppermute x2, starting transfers between devices, on_device(): take_2 = lax.ppermute(give_2, ('seq', 'head'), spread(second + fold) + ends)  4.95 us
    ppermute x1, waiting for transfers between devices, on_device(): inner_near = lax.ppermute(outer, 'seq', pairs)  2.86 us
    ppermute x1, starting transfers between devices, on_device(): outer_near = lax.ppermute(inner_far, 'seq', pairs)  1.56 us
    ppermute x1, starting transfers between devices, on_device(): pair_take = lax.ppermute(inner_g1, 'seq', pairs)  1.56 us
    ppermute x1, waiting for transfers between devices, on_device(): inner_a = lax.ppermute(outer_g1, ('seq', 'head'), spread(across) + turns)  1.32 us
  transfers between devices with their start and end apart: 8, of which 5 were waited for; matrix products, arithmetic and copies ran while one was open for 0% of the time, Pallas kernels for 32%

profile of v3, /device:TPU:24, one launch (start us, length us, event | category | flops | bytes accessed | tf_op | source)
XLA Modules:
  0.0 42.0 jit_solution(14642068195983610750)
XLA Ops:
  0.7 0.0 copy-start.2
  0.7 1.0 %constant_dynamic-slice_fusion = (bf16[512,128]{1,0:T(8,128)(2,1)S(1)}, bf16[512,128]{1,0:T(8,128)(2,1)S(1)}) fusion(bf16[1024,128]{1,0:T(8,128)(2,1)} %param.7, s32[]{:T(128)S(6)} %select_n.45, s32[]{:T(128)S(6)} %select_n.41), kind=kLoop, calls=%fused_computation.12 | loop fusion | bytes 524296 | tf_op jit(solution)/shard_map/dynamic_slice | solution.py:36
  1.7 0.0 copy-done.2
  1.8 0.0 copy-start.3
  1.8 0.6 %copy-done.3 = s32[8]{0:T(128)S(1)} copy-done((s32[8]{0:T(128)S(1)}, s32[8]{0:T(128)}, u32[]{:S(2)}) %copy-start.3) | copy-done | bytes 56
  2.4 0.1 fusion.2
  2.5 0.2 broadcast_select_fusion.2
  2.7 0.5 %collective-permute-start = (bf16[528,256]{1,0:T(8,128)(2,1)S(1)}, bf16[528,256]{1,0:T(8,128)(2,1)S(1)}, u32[]{:S(2)}, u32[]{:S(2)}) collective-permute-start(bf16[528,256]{1,0:T(8,128)(2,1)S(1)} %get-tuple-element.42), channel_id=1, source_target_pairs={{0,8},{4,12},{8,0},{12,4},{16,24},{20,28},{24,16},{28,20},{1,9},{5... | collective-permute-start | bytes 811016 | tf_op jit(solution)/shard_map/ppermute | solution.py:454
  3.3 1.5 %collective-permute-start.1 = (bf16[528,256]{1,0:T(8,128)(2,1)S(1)}, bf16[528,256]{1,0:T(8,128)(2,1)S(1)}, u32[]{:S(2)}, u32[]{:S(2)}) collective-permute-start(bf16[528,256]{1,0:T(8,128)(2,1)S(1)} %get-tuple-element.41), channel_id=1, source_target_pairs={{8,16},{9,17},{10,18},{11,19},{12,20},{13,21},{14,22},{15,23},{16,... | collective-permute-start | bytes 811016 | tf_op jit(solution)/shard_map/ppermute | solution.py:462
  4.8 0.5 %collective-permute-start.3 = (bf16[528,256]{1,0:T(8,128)(2,1)S(1)}, bf16[528,256]{1,0:T(8,128)(2,1)S(1)}, u32[]{:S(2)}, u32[]{:S(2)}) collective-permute-start(bf16[528,256]{1,0:T(8,128)(2,1)S(1)} %get-tuple-element.44.own_ref.refs_3_), channel_id=1, source_target_pairs={{0,4},{4,0},{8,12},{12,8},{16,20},{20,16},{24,28},{28,24},{1,5},{5... | collective-permute-start | bytes 811016 | tf_op jit(solution)/shard_map/ppermute | solution.py:463
  5.3 5.7 %collective-permute-done = bf16[528,256]{1,0:T(8,128)(2,1)S(1)} collective-permute-done((bf16[528,256]{1,0:T(8,128)(2,1)S(1)}, bf16[528,256]{1,0:T(8,128)(2,1)S(1)}, u32[]{:S(2)}, u32[]{:S(2)}) %collective-permute-start) | collective-permute-done | bytes 270368 | tf_op jit(solution)/shard_map/ppermute | solution.py:454
  11.0 1.6 %collective-permute-done.1 = bf16[528,256]{1,0:T(8,128)(2,1)S(1)} collective-permute-done((bf16[528,256]{1,0:T(8,128)(2,1)S(1)}, bf16[528,256]{1,0:T(8,128)(2,1)S(1)}, u32[]{:S(2)}, u32[]{:S(2)}) %collective-permute-start.1) | collective-permute-done | bytes 270368 | tf_op jit(solution)/shard_map/ppermute | solution.py:462
  12.7 1.6 %collective-permute-start.2 = (bf16[528,256]{1,0:T(8,128)(2,1)S(1)}, bf16[528,256]{1,0:T(8,128)(2,1)S(1)}, u32[]{:S(2)}, u32[]{:S(2)}) collective-permute-start(bf16[528,256]{1,0:T(8,128)(2,1)S(1)} %get-tuple-element.40.far_ref), channel_id=1, source_target_pairs={{0,4},{4,0},{8,12},{12,8},{16,20},{20,16},{24,28},{28,24},{1,5},{5... | collective-permute-start | bytes 811016 | tf_op jit(solution)/shard_map/ppermute | solution.py:467
  14.3 0.0 copy-done
  14.3 0.0 copy-done.1
  14.3 1.3 %outer_stats.1.part_ref = f32[16,512]{1,0:T(8,128)S(1)} custom-call(s32[1]{0:T(128)} %bitcast.index_ref.refs_0_, bf16[1024,256]{1,0:T(8,128)(2,1)S(1)} %copy-done, bf16[1024,256]{1,0:T(8,128)(2,1)S(1)} %copy-done.1, bf16[528,256]{1,0:T(8,128)(2,1)S(1)} %get-tuple-element.44.own_ref.refs_3_, bf16[528,256]{1,0:T(8,128)(2,1)S(1)} %get-tuple-element.39.far_ref.refs_5_), custom_call_target="tpu_custom_call" | custom-call | flops 402653184 | bytes 1048576 | tf_op jit(solution)/shard_map/outer_stats/pallas_call | solution.py:433
  15.6 2.9 %collective-permute-done.3.near_ref = bf16[528,256]{1,0:T(8,128)(2,1)S(1)} collective-permute-done((bf16[528,256]{1,0:T(8,128)(2,1)S(1)}, bf16[528,256]{1,0:T(8,128)(2,1)S(1)}, u32[]{:S(2)}, u32[]{:S(2)}) %collective-permute-start.3) | collective-permute-done | bytes 270368 | tf_op jit(solution)/shard_map/ppermute | solution.py:463
  18.5 4.9 %inner_stage.1 = (f32[256,512]{1,0:T(8,128)S(1)}, f32[512,256]{1,0:T(8,128)S(1)}, bf16[512,256]{1,0:T(8,128)(2,1)S(1)}, bf16[512,256]{1,0:T(8,128)(2,1)S(1)}) custom-call(s32[1]{0:T(128)} %bitcast.index_ref.refs_0_, bf16[1024,256]{1,0:T(8,128)(2,1)S(1)} %copy-done, bf16[1024,256]{1,0:T(8,128)(2,1)S(1)} %copy-done.1, ...), custom_call_target="tpu_custom_call" | custom-call | flops 1677721600 | bytes 1048576 | tf_op jit(solution)/shard_map/inner_stage/pallas_call | solution.py:433
  23.4 1.6 %collective-permute-start.5 = (bf16[512,256]{1,0:T(8,128)(2,1)S(1)}, bf16[512,256]{1,0:T(8,128)(2,1)S(1)}, u32[]{:S(2)}, u32[]{:S(2)}) collective-permute-start(bf16[512,256]{1,0:T(8,128)(2,1)S(1)} %get-tuple-element.34), channel_id=1, source_target_pairs={{0,4},{4,0},{8,12},{12,8},{16,20},{20,16},{24,28},{28,24},{1,5},{5... | collective-permute-start | bytes 786440 | tf_op jit(solution)/shard_map/ppermute | solution.py:486
  25.0 0.0 collective-permute-done.2.near_ref.refs_4_
  25.0 2.7 %outer_near.1 = (bf16[512,256]{1,0:T(8,128)(2,1)S(1)}, f32[256,512]{1,0:T(8,128)S(1)}, f32[16,512]{1,0:T(8,128)S(1)}) custom-call(s32[1]{0:T(128)} %bitcast.index_ref.refs_0_, bf16[1024,256]{1,0:T(8,128)(2,1)S(1)} %copy-done, bf16[1024,256]{1,0:T(8,128)(2,1)S(1)} %copy-done.1, bf16[528,256]{1,0:T(8,128)(2,1)S(1)} %get-tuple-element.44.own_ref.refs_3_, ...), custom_call_target="tpu_custom_call" | custom-call | flops 671088640 | bytes 1048576 | tf_op jit(solution)/shard_map/outer_near/pallas_call | solution.py:433
  27.6 0.1 collective-permute-start.4
  27.7 1.9 %outer_far.1 = (f32[256,512]{1,0:T(8,128)S(1)}, bf16[512,256]{1,0:T(8,128)(2,1)S(1)}, bf16[512,256]{1,0:T(8,128)(2,1)S(1)}) custom-call(s32[1]{0:T(128)} %bitcast.index_ref.refs_0_, bf16[1024,256]{1,0:T(8,128)(2,1)S(1)} %copy-done, bf16[1024,256]{1,0:T(8,128)(2,1)S(1)} %copy-done.1, bf16[528,256]{1,0:T(8,128)(2,1)S(1)} %get-tuple-element.44.own_ref.refs_3_, ...), custom_call_target="tpu_custom_call" | custom-call | flops 503316480 | bytes 1048576 | tf_op jit(solution)/shard_map/outer_far/pallas_call | solution.py:433
  29.7 0.1 collective-permute-start.6
  29.7 3.5 %collective-permute-start.7 = (bf16[512,256]{1,0:T(8,128)(2,1)S(1)}, bf16[512,256]{1,0:T(8,128)(2,1)S(1)}, u32[]{:S(2)}, u32[]{:S(2)}) collective-permute-start(bf16[512,256]{1,0:T(8,128)(2,1)S(1)} %get-tuple-element.36), channel_id=1, source_target_pairs={{8,16},{9,17},{10,18},{11,19},{12,20},{13,21},{14,22},{15,23},{16,... | collective-permute-start | bytes 786440 | tf_op jit(solution)/shard_map/ppermute | solution.py:506
  33.2 2.7 %outer_own.1 = (bf16[1024,256]{1,0:T(8,128)(2,1)}, f32[512,256]{1,0:T(8,128)S(1)}) custom-call(s32[1]{0:T(128)} %bitcast.index_ref.refs_0_, bf16[1024,256]{1,0:T(8,128)(2,1)S(1)} %copy-done, bf16[1024,256]{1,0:T(8,128)(2,1)S(1)} %copy-done.1, bf16[528,256]{1,0:T(8,128)(2,1)S(1)} %get-tuple-element.44.own_ref.refs_3_, ...), custom_call_target="tpu_custom_call" | custom-call | flops 503316480 | bytes 1048576 | tf_op jit(solution)/shard_map/outer_own/pallas_call | solution.py:433
  35.9 1.3 %collective-permute-done.4.refs_2_ = bf16[512,256]{1,0:T(8,128)(2,1)S(1)} collective-permute-done((bf16[512,256]{1,0:T(8,128)(2,1)S(1)}, bf16[512,256]{1,0:T(8,128)(2,1)S(1)}, u32[]{:S(2)}, u32[]{:S(2)}) %collective-permute-start.4) | collective-permute-done | bytes 262176 | tf_op jit(solution)/shard_map/ppermute | solution.py:496
  37.2 0.1 early_sum.1.inner_own
  37.3 0.0 collective-permute-done.5.pair
  37.3 0.0 collective-permute-done.6.first
  37.3 3.8 %collective-permute-done.7.second = bf16[512,256]{1,0:T(8,128)(2,1)S(1)} collective-permute-done((bf16[512,256]{1,0:T(8,128)(2,1)S(1)}, bf16[512,256]{1,0:T(8,128)(2,1)S(1)}, u32[]{:S(2)}, u32[]{:S(2)}) %collective-permute-start.7) | collective-permute-done | bytes 262176 | tf_op jit(solution)/shard_map/ppermute | solution.py:506
  41.1 1.0 %sum.1 = (bf16[1024,128]{1,0:T(8,128)(2,1)}, bf16[1024,128]{1,0:T(8,128)(2,1)}) custom-call(s32[1]{0:T(128)} %bitcast.index_ref.refs_0_, f32[512,256]{1,0:T(8,128)S(1)} %early_sum.1.inner_own, f32[512,256]{1,0:T(8,128)S(1)} %get-tuple-element.33.outer_own, bf16[512,256]{1,0:T(8,128)(2,1)S(1)} %collective-permute-done.5.pair, ...), custom_call_target="tpu_custom_call" | custom-call | flops 33554432 | bytes 1048576 | tf_op jit(solution)/shard_map/sum/pallas_call | solution.py:433
  (6 shorter events, 0.1 us)
Async XLA Ops:
  0.7 1.1 %copy-start.2 = (bf16[1024,128]{1,0:T(8,128)(2,1)S(1)}, bf16[1024,128]{1,0:T(8,128)(2,1)}, u32[]{:S(2)}) copy-start(bf16[1024,128]{1,0:T(8,128)(2,1)} %param.6) | copy-start | bytes 786436
  1.8 0.7 %copy-start.3 = (s32[8]{0:T(128)S(1)}, s32[8]{0:T(128)}, u32[]{:S(2)}) copy-start(s32[8]{0:T(128)} %param.9) | copy-start | bytes 100
  2.7 8.3 %collective-permute-start = (bf16[528,256]{1,0:T(8,128)(2,1)S(1)}, bf16[528,256]{1,0:T(8,128)(2,1)S(1)}, u32[]{:S(2)}, u32[]{:S(2)}) collective-permute-start(bf16[528,256]{1,0:T(8,128)(2,1)S(1)} %get-tuple-element.42), channel_id=1, source_target_pairs={{0,8},{4,12},{8,0},{12,4},{16,24},{20,28},{24,16},{28,20},{1,9},{5... | collective-permute-start | bytes 811016 | tf_op jit(solution)/shard_map/ppermute | solution.py:454
  3.3 9.4 %collective-permute-start.1 = (bf16[528,256]{1,0:T(8,128)(2,1)S(1)}, bf16[528,256]{1,0:T(8,128)(2,1)S(1)}, u32[]{:S(2)}, u32[]{:S(2)}) collective-permute-start(bf16[528,256]{1,0:T(8,128)(2,1)S(1)} %get-tuple-element.41), channel_id=1, source_target_pairs={{8,16},{9,17},{10,18},{11,19},{12,20},{13,21},{14,22},{15,23},{16,... | collective-permute-start | bytes 811016 | tf_op jit(solution)/shard_map/ppermute | solution.py:462
  4.8 9.5 %copy-start = (bf16[1024,256]{1,0:T(8,128)(2,1)S(1)}, bf16[1024,256]{1,0:T(8,128)(2,1)}, u32[]{:S(2)}) copy-start(bf16[1024,256]{1,0:T(8,128)(2,1)} %refs_1_.3) | copy-start | bytes 1572868
  4.8 9.5 %copy-start.1 = (bf16[1024,256]{1,0:T(8,128)(2,1)S(1)}, bf16[1024,256]{1,0:T(8,128)(2,1)}, u32[]{:S(2)}) copy-start(bf16[1024,256]{1,0:T(8,128)(2,1)} %refs_2_.3) | copy-start | bytes 1572868
  4.8 13.7 %collective-permute-start.3 = (bf16[528,256]{1,0:T(8,128)(2,1)S(1)}, bf16[528,256]{1,0:T(8,128)(2,1)S(1)}, u32[]{:S(2)}, u32[]{:S(2)}) collective-permute-start(bf16[528,256]{1,0:T(8,128)(2,1)S(1)} %get-tuple-element.44.own_ref.refs_3_), channel_id=1, source_target_pairs={{0,4},{4,0},{8,12},{12,8},{16,20},{20,16},{24,28},{28,24},{1,5},{5... | collective-permute-start | bytes 811016 | tf_op jit(solution)/shard_map/ppermute | solution.py:463
  12.7 12.3 %collective-permute-start.2 = (bf16[528,256]{1,0:T(8,128)(2,1)S(1)}, bf16[528,256]{1,0:T(8,128)(2,1)S(1)}, u32[]{:S(2)}, u32[]{:S(2)}) collective-permute-start(bf16[528,256]{1,0:T(8,128)(2,1)S(1)} %get-tuple-element.40.far_ref), channel_id=1, source_target_pairs={{0,4},{4,0},{8,12},{12,8},{16,20},{20,16},{24,28},{28,24},{1,5},{5... | collective-permute-start | bytes 811016 | tf_op jit(solution)/shard_map/ppermute | solution.py:467
  23.4 13.8 %collective-permute-start.5 = (bf16[512,256]{1,0:T(8,128)(2,1)S(1)}, bf16[512,256]{1,0:T(8,128)(2,1)S(1)}, u32[]{:S(2)}, u32[]{:S(2)}) collective-permute-start(bf16[512,256]{1,0:T(8,128)(2,1)S(1)} %get-tuple-element.34), channel_id=1, source_target_pairs={{0,4},{4,0},{8,12},{12,8},{16,20},{20,16},{24,28},{28,24},{1,5},{5... | collective-permute-start | bytes 786440 | tf_op jit(solution)/shard_map/ppermute | solution.py:486
  27.6 9.6 %collective-permute-start.4 = (bf16[512,256]{1,0:T(8,128)(2,1)S(1)}, bf16[512,256]{1,0:T(8,128)(2,1)S(1)}, u32[]{:S(2)}, u32[]{:S(2)}) collective-permute-start(bf16[512,256]{1,0:T(8,128)(2,1)S(1)} %get-tuple-element.32.refs_3_), channel_id=1, source_target_pairs={{4,8},{5,9},{6,10},{7,11},{8,4},{9,5},{10,6},{11,7},{12,16},{13,17... | collective-permute-start | bytes 786440 | tf_op jit(solution)/shard_map/ppermute | solution.py:496
  29.7 7.6 %collective-permute-start.6 = (bf16[512,256]{1,0:T(8,128)(2,1)S(1)}, bf16[512,256]{1,0:T(8,128)(2,1)S(1)}, u32[]{:S(2)}, u32[]{:S(2)}) collective-permute-start(bf16[512,256]{1,0:T(8,128)(2,1)S(1)} %get-tuple-element.35), channel_id=1, source_target_pairs={{0,8},{4,12},{8,0},{12,4},{16,24},{20,28},{24,16},{28,20},{1,9},{5... | collective-permute-start | bytes 786440 | tf_op jit(solution)/shard_map/ppermute | solution.py:505
  29.7 11.3 %collective-permute-start.7 = (bf16[512,256]{1,0:T(8,128)(2,1)S(1)}, bf16[512,256]{1,0:T(8,128)(2,1)S(1)}, u32[]{:S(2)}, u32[]{:S(2)}) collective-permute-start(bf16[512,256]{1,0:T(8,128)(2,1)S(1)} %get-tuple-element.36), channel_id=1, source_target_pairs={{8,16},{9,17},{10,18},{11,19},{12,20},{13,21},{14,22},{15,23},{16,... | collective-permute-start | bytes 786440 | tf_op jit(solution)/shard_map/ppermute | solution.py:506

commit v4 on v3

--- a/solution.py
+++ b/solution.py
@@ -40,80 +40,6 @@
     begins = jnp.pad(jnp.where(first, 1, begins).astype(jnp.bfloat16), (0, MARK - blocks))
     marks = jnp.broadcast_to(begins[:, None], (MARK, 2 * width))
     return jnp.concatenate([jnp.concatenate(both, axis=1), marks], axis=0)
-
-
-def inner_stage_kernel(
-    index_ref, q_ref, g_ref, own_ref, near_ref, far_ref,
-    dq_ref, own_out, near_out, far_out, acc_ref,
-):
-    length = q_ref.shape[0] // 2
-    width = own_ref.shape[1] // 2
-    blocks = length // BLOCK
-    base = (1 - lax.rem(index_ref[0], 2)) * length
-    pieces = (far_ref, near_ref, own_ref)
-    docs = block_docs(pieces, length)
-    after = triangle()
-    key_t = [jnp.transpose(p[:length, :width]) for p in pieces]
-    steps = [(i, h) for i in range(length // TILE) for h in range(QUERY_PER_KEY)]
-
-    def products(i, h):
-        rows = pl.ds(pl.multiple_of(base + i * TILE, TILE), TILE)
-        cols = slice(h * HEAD_SIZE, (h + 1) * HEAD_SIZE)
-        qt, gt = q_ref[rows, cols], g_ref[rows, cols]
-        own_docs = tile_docs(docs, 2 * blocks + i * (TILE // BLOCK))
-        parts = []
-        for c, p, r in chunk_list(i, length, (0, 1, 2)):
-            s = masked_scores(c, pieces[p][r : r + TILE, :width], qt, after)
-            dw = dot(pieces[p][r : r + TILE, width:], gt, 1, 1)
-            parts.append((s, dw, bias_rows(docs, p * blocks + r // BLOCK, own_docs)))
-        return qt, gt, parts
-
-    def shares(i, h, parts):
-        top = None
-        for s, dw, bias in parts:
-            top = chunk_top(s, bias, top)
-        shift = top * exponent_scale
-        total = jnp.zeros((1, TILE), jnp.float32)
-        mixed = jnp.zeros((1, TILE), jnp.float32)
-        terms = []
-        for s, dw, bias in parts:
-            e = chunk_terms(s, bias, shift)
-            terms.append(e)
-            total = total + jnp.sum(e, axis=0, keepdims=True)
-            mixed = mixed + jnp.sum(e * dw, axis=0, keepdims=True)
-        inverse = 1.0 / total
-        row_dot = mixed * inverse
-        weights, dscores = [], []
-        for e, (s, dw, bias) in zip(terms, parts):
-            w = e * inverse
-            dscores.append((w * (dw - row_dot)).astype(jnp.bfloat16))
-            weights.append(w.astype(jnp.bfloat16))
-        return weights, dscores
-
-    def query_grad(i, h, dscores):
-        dq_t = jnp.zeros((width, TILE), jnp.float32)
-        for ds, (c, p, r) in zip(dscores, chunk_list(i, length, (0, 1, 2))):
-            dq_t = dq_t + dot(key_t[p][:, r : r + TILE], ds, 1, 0)
-        dq_ref[h * width : (h + 1) * width, i * TILE : (i + 1) * TILE] = dq_t
-
-    seen = set()
-    members = []
-    ready = products(*steps[0])
-    for n, (i, h) in enumerate(steps):
-        qt, gt, parts = ready
-        if n + 1 < len(steps):
-            ready = products(*steps[n + 1])
-        weights, dscores = shares(i, h, parts)
-        query_grad(i, h, dscores)
-        members.append((qt, gt, weights, dscores))
-        if h == QUERY_PER_KEY - 1:
-            slots = [p * length + r for _, p, r in chunk_list(i, length, (0, 1, 2))]
-            add_key_grads(acc_ref, members, slots, [x for x in slots if x not in seen])
-            seen.update(slots)
-            members = []
-    far_out[...] = acc_ref[:length].astype(jnp.bfloat16)
-    near_out[...] = acc_ref[length : 2 * length].astype(jnp.bfloat16)
-    own_out[...] = acc_ref[2 * length :]
 
 
 def block_docs(pieces, length):
@@ -227,55 +153,141 @@
     docs = block_docs((near_ref, own_ref), length)
     far_bias = jnp.where(docs[blocks - 1] == 0.0, 0.0, NEG)
     key_t = jnp.transpose(near_ref[:length, :width])
-    for i in range(length // TILE):
+    steps = [(i, h) for i in range(length // TILE) for h in range(QUERY_PER_KEY)]
+
+    def products(i, h):
+        rows = pl.ds(pl.multiple_of(base + i * TILE, TILE), TILE)
+        cols = slice(h * HEAD_SIZE, (h + 1) * HEAD_SIZE)
+        qt, gt = q_ref[rows, cols], g_ref[rows, cols]
         own_docs = tile_docs(docs, blocks + i * (TILE // BLOCK))
+        parts = []
+        for c, _, r in chunk_list(i, length, (1,)):
+            s = dot(near_ref[r : r + TILE, :width], qt, 1, 1)
+            dw = dot(near_ref[r : r + TILE, width:], gt, 1, 1)
+            parts.append((s, dw, bias_rows(docs, r // BLOCK, own_docs)))
+        return qt, gt, parts
+
+    def shares(i, h, parts):
+        lanes = slice(i * TILE, (i + 1) * TILE)
+        at = h * 6
+        own_top, own_total, own_mixed = [part_ref[at + k : at + k + 1, lanes] for k in range(3)]
+        far_top, far_total, far_mixed = [part_ref[at + 3 + k : at + 4 + k, lanes] for k in range(3)]
+        top = jnp.maximum(own_top, far_top + far_bias)
+        for s, dw, bias in parts:
+            top = chunk_top(s, bias, top)
+        shift = top * exponent_scale
+        own_scale = jnp.exp2(own_top * exponent_scale - shift)
+        far_scale = jnp.exp2(far_top * exponent_scale + (far_bias - shift))
+        total = own_total * own_scale + far_total * far_scale
+        mixed = own_mixed * own_scale + far_mixed * far_scale
+        terms = []
+        for s, dw, bias in parts:
+            e = chunk_terms(s, bias, shift)
+            terms.append(e)
+            total = total + jnp.sum(e, axis=0, keepdims=True)
+            mixed = mixed + jnp.sum(e * dw, axis=0, keepdims=True)
+        inverse = 1.0 / total
+        row_dot = mixed * inverse
+        for k, value in enumerate((shift, inverse, row_dot)):
+            stats_ref[h * 3 + k : h * 3 + k + 1, lanes] = value
+        weights, dscores = [], []
+        dq_t = jnp.zeros((width, TILE), jnp.float32)
+        for e, (s, dw, bias), (c, _, r) in zip(terms, parts, chunk_list(i, length, (1,))):
+            w = e * inverse
+            ds = (w * (dw - row_dot)).astype(jnp.bfloat16)
+            weights.append(w.astype(jnp.bfloat16))
+            dscores.append(ds)
+            dq_t = dq_t + dot(key_t[:, r : r + TILE], ds, 1, 0)
+        dq_out[h * width : (h + 1) * width, lanes] = dq_t
+        return weights, dscores
+
+    members = []
+    ready = products(*steps[0])
+    for n, (i, h) in enumerate(steps):
+        qt, gt, parts = ready
+        if n + 1 < len(steps):
+            ready = products(*steps[n + 1])
+        members.append((qt, gt, *shares(i, h, parts)))
+        if h == QUERY_PER_KEY - 1:
+            slots = [r for _, _, r in chunk_list(i, length, (1,))]
+            add_key_grads(acc_ref, members, slots, slots if i == 0 else [])
+            members = []
+    near_out[...] = acc_ref[...].astype(jnp.bfloat16)
+
+
+def inner_stage_kernel(
+    last, index_ref, q_ref, g_ref, own_ref, near_ref, far_ref, fold_ref,
+    near_out, far_out, dq_out, stats_ref, acc_ref,
+):
+    length = q_ref.shape[0] // 2
+    width = own_ref.shape[1] // 2
+    blocks = length // BLOCK
+    base = (1 - lax.rem(index_ref[0], 2)) * length
+    pieces = (far_ref, near_ref, own_ref)
+    docs = block_docs(pieces, length)
+    after = triangle()
+    key_t = [jnp.transpose(pieces[p][:length, :width]) for p in (0, 1)]
+    steps = [(i, h) for i in range(length // TILE) for h in range(QUERY_PER_KEY)]
+
+    def products(i, h):
         rows = pl.ds(pl.multiple_of(base + i * TILE, TILE), TILE)
+        cols = slice(h * HEAD_SIZE, (h + 1) * HEAD_SIZE)
+        qt, gt = q_ref[rows, cols], g_ref[rows, cols]
+        own_docs = tile_docs(docs, 2 * blocks + i * (TILE // BLOCK))
+        parts = []
+        for c, p, r in chunk_list(i, length, (0, 1, 2)):
+            s = masked_scores(c, pieces[p][r : r + TILE, :width], qt, after)
+            dw = dot(pieces[p][r : r + TILE, width:], gt, 1, 1)
+            parts.append((s, dw, bias_rows(docs, p * blocks + r // BLOCK, own_docs)))
+        return qt, gt, parts
+
+    def shares(i, h, parts):
         lanes = slice(i * TILE, (i + 1) * TILE)
-        members = []
-        chunks = chunk_list(i, length, (1,))
-        for h in range(QUERY_PER_KEY):
-            cols = slice(h * HEAD_SIZE, (h + 1) * HEAD_SIZE)
-            qt, gt = q_ref[rows, cols], g_ref[rows, cols]
-            at = h * 6
-            own_top, own_total, own_mixed = [part_ref[at + k : at + k + 1, lanes] for k in range(3)]
-            far_top, far_total, far_mixed = [
-                part_ref[at + 3 + k : at + 4 + k, lanes] for k in range(3)
-            ]
-            top = jnp.maximum(own_top, far_top + far_bias)
-            parts = []
-            for c, _, r in chunks:
-                s = dot(near_ref[r : r + TILE, :width], qt, 1, 1)
-                dw = dot(near_ref[r : r + TILE, width:], gt, 1, 1)
-                bias = bias_rows(docs, r // BLOCK, own_docs)
-                top = chunk_top(s, bias, top)
-                parts.append((s, dw, bias))
-            shift = top * exponent_scale
-            own_scale = jnp.exp2(own_top * exponent_scale - shift)
-            far_scale = jnp.exp2(far_top * exponent_scale + (far_bias - shift))
-            total = own_total * own_scale + far_total * far_scale
-            mixed = own_mixed * own_scale + far_mixed * far_scale
-            terms = []
-            for s, dw, bias in parts:
-                e = chunk_terms(s, bias, shift)
-                terms.append(e)
-                total = total + jnp.sum(e, axis=0, keepdims=True)
-                mixed = mixed + jnp.sum(e * dw, axis=0, keepdims=True)
-            inverse = 1.0 / total
-            row_dot = mixed * inverse
-            for k, value in enumerate((shift, inverse, row_dot)):
-                stats_ref[h * 3 + k : h * 3 + k + 1, lanes] = value
-            weights, dscores = [], []
-            dq_t = jnp.zeros((width, TILE), jnp.float32)
-            for e, (s, dw, bias), (c, _, r) in zip(terms, parts, chunks):
-                w = e * inverse
-                ds = (w * (dw - row_dot)).astype(jnp.bfloat16)
-                weights.append(w.astype(jnp.bfloat16))
-                dscores.append(ds)
-                dq_t = dq_t + dot(key_t[:, r : r + TILE], ds, 1, 0)
-            dq_out[h * width : (h + 1) * width, lanes] = dq_t
-            members.append((qt, gt, weights, dscores))
-        add_key_grads(acc_ref, members, [r for _, _, r in chunks], i == 0)
-    near_out[...] = acc_ref[...].astype(jnp.bfloat16)
+        top = None
+        for s, dw, bias in parts:
+            top = chunk_top(s, bias, top)
+        shift = top * exponent_scale
+        total = jnp.zeros((1, TILE), jnp.float32)
+        mixed = jnp.zeros((1, TILE), jnp.float32)
+        terms = []
+        for s, dw, bias in parts:
+            e = chunk_terms(s, bias, shift)
+            terms.append(e)
+            total = total + jnp.sum(e, axis=0, keepdims=True)
+            mixed = mixed + jnp.sum(e * dw, axis=0, keepdims=True)
+        inverse = 1.0 / total
+        row_dot = mixed * inverse
+        for k, value in enumerate((shift, inverse, row_dot)):
+            stats_ref[h * 3 + k : h * 3 + k + 1, lanes] = value
+        weights, dscores = [], []
+        dq_t = jnp.zeros((width, TILE), jnp.float32)
+        for e, (s, dw, bias), (c, p, r) in zip(terms, parts, chunk_list(i, length, (0, 1, 2))):
+            if p == 2:
+                continue
+            w = e * inverse
+            ds = (w * (dw - row_dot)).astype(jnp.bfloat16)
+            weights.append(w.astype(jnp.bfloat16))
+            dscores.append(ds)
+            dq_t = dq_t + dot(key_t[p][:, r : r + TILE], ds, 1, 0)
+        dq_out[h * width : (h + 1) * width, lanes] = dq_t
+        return weights, dscores
+
+    seen = set()
+    members = []
+    ready = products(*steps[0])
+    for n, (i, h) in enumerate(steps):
+        qt, gt, parts = ready
+        if n + 1 < len(steps):
+            ready = products(*steps[n + 1])
+        members.append((qt, gt, *shares(i, h, parts)))
+        if h == QUERY_PER_KEY - 1:
+            slots = [p * length + r for _, p, r in chunk_list(i, length, (0, 1))]
+            add_key_grads(acc_ref, members, slots, [x for x in slots if x not in seen])
+            seen.update(slots)
+            members = []
+    more = jnp.where(index_ref[0] == last, fold_ref[...].astype(jnp.float32), 0.0)
+    near_out[...] = (acc_ref[length:] + more).astype(jnp.bfloat16)
+    far_out[...] = acc_ref[:length].astype(jnp.bfloat16)
 
 
 def add_key_grads(acc_ref, members, slots, first):
@@ -296,68 +308,145 @@
         acc_ref[at, width:] = dv
 
 
-def outer_share_kernel(
-    wanted, last, index_ref, q_ref, g_ref, own_ref, near_ref, far_ref, stats_ref, dq_part_ref, *refs
+def outer_far_share(
+    index_ref, q_ref, g_ref, own_ref, near_ref, far_ref, stats_ref, dq_part_ref, dq_ref, acc_ref
 ):
     length = q_ref.shape[0] // 2
     width = own_ref.shape[1] // 2
-    blocks = length // BLOCK
     base = lax.rem(index_ref[0], 2) * length
-    if wanted == 2:
-        dq_in, dq_ref, grad_out, acc_ref = refs
-    else:
-        inner_far_ref, dq_ref, first_out, second_out, acc_ref = refs
     docs = block_docs((far_ref, near_ref, own_ref), length)
+    key_t = jnp.transpose(far_ref[:length, :width])
+    piece_share(
+        0, 0, base, docs, 2 * (length // BLOCK), triangle(), key_t, q_ref, g_ref, far_ref,
+        stats_ref, dq_part_ref, dq_ref, acc_ref,
+    )
+
+
+def outer_far_kernel(
+    last, index_ref, q_ref, g_ref, own_ref, near_ref, far_ref, stats_ref, dq_part_ref,
+    inner_far_ref, dq_ref, first_out, second_out, acc_ref,
+):
+    @pl.when(index_ref[0] != last)
+    def _():
+        outer_far_share(
+            index_ref, q_ref, g_ref, own_ref, near_ref, far_ref, stats_ref, dq_part_ref, dq_ref,
+            acc_ref,
+        )
+
+    @pl.when(index_ref[0] == last)
+    def _():
+        dq_ref[...] = dq_part_ref[...]
+        acc_ref[...] = jnp.zeros_like(acc_ref)
+
+    _, _, even = halves(index_ref[0])
+    grad = acc_ref[...].astype(jnp.bfloat16)
+    other = inner_far_ref[...]
+    first_out[...] = jnp.where(even, other, grad)
+    second_out[...] = jnp.where(even, grad, other)
+
+
+def piece_share(
+    piece, first, base, docs, places, after, key_t, q_ref, g_ref, piece_ref,
+    stats_ref, dq_part_ref, dq_ref, acc_ref,
+):
+    length, width = q_ref.shape[0] // 2, piece_ref.shape[1] // 2
+    steps = [(i, h) for i in range(length // TILE) for h in range(QUERY_PER_KEY)]
+
+    def products(i, h):
+        rows = pl.ds(pl.multiple_of(base + i * TILE, TILE), TILE)
+        cols = slice(h * HEAD_SIZE, (h + 1) * HEAD_SIZE)
+        qt, gt = q_ref[rows, cols], g_ref[rows, cols]
+        own_docs = tile_docs(docs, places + i * (TILE // BLOCK))
+        parts = []
+        for c, _, r in chunk_list(i, length, (piece,)):
+            s = masked_scores(c, piece_ref[r : r + TILE, :width], qt, after)
+            dw = dot(piece_ref[r : r + TILE, width:], gt, 1, 1)
+            parts.append((s, dw, bias_rows(docs, first + r // BLOCK, own_docs), r))
+        return qt, gt, parts
+
+    seen = set()
+    members = []
+    ready = products(*steps[0])
+    for n, (i, h) in enumerate(steps):
+        qt, gt, parts = ready
+        if n + 1 < len(steps):
+            ready = products(*steps[n + 1])
+        lanes = slice(i * TILE, (i + 1) * TILE)
+        shift, inverse, row_dot = [stats_ref[h * 3 + k : h * 3 + k + 1, lanes] for k in range(3)]
+        weights, dscores = [], []
+        dq_t = dq_part_ref[h * width : (h + 1) * width, lanes]
+        for s, dw, bias, r in parts:
+            w = chunk_terms(s, bias, shift) * inverse
+            ds = (w * (dw - row_dot)).astype(jnp.bfloat16)
+            weights.append(w.astype(jnp.bfloat16))
+            dscores.append(ds)
+            dq_t = dq_t + dot(key_t[:, r : r + TILE], ds, 1, 0)
+        if piece == 2:
+            rows = pl.ds(pl.multiple_of(base + i * TILE, TILE), TILE)
+            cols = slice(h * HEAD_SIZE, (h + 1) * HEAD_SIZE)
+            dq_ref[rows, cols] = jnp.transpose(dq_t * query_scaling).astype(jnp.bfloat16)
+        else:
+            dq_ref[h * width : (h + 1) * width, lanes] = dq_t
+        members.append((qt, gt, weights, dscores))
+        if h == QUERY_PER_KEY - 1:
+            slots = [r for _, _, _, r in parts]
+            add_key_grads(acc_ref, members, slots, [x for x in slots if x not in seen])
+            seen.update(slots)
+            members = []
+
+
+def own_kernel(
+    index_ref, q_ref, g_ref, inner_ref, inner_stats, inner_dq, outer_ref, outer_stats, outer_dq,
+    dq_ref, inner_out, outer_out,
+):
+    length = q_ref.shape[0] // 2
+    width = inner_ref.shape[1] // 2
+    parity = lax.rem(index_ref[0], 2)
     after = triangle()
-    piece = own_ref if wanted == 2 else far_ref
-    key_t = jnp.transpose(piece[:length, :width])
-    seen = set()
-    for i in range(length // TILE):
-        own_docs = tile_docs(docs, 2 * blocks + i * (TILE // BLOCK))
-        rows = pl.ds(pl.multiple_of(base + i * TILE, TILE), TILE)
-        lanes = slice(i * TILE, (i + 1) * TILE)
-        members = []
-        chunks = chunk_list(i, length, (wanted,))
-        for h in range(QUERY_PER_KEY):
-            cols = slice(h * HEAD_SIZE, (h + 1) * HEAD_SIZE)
-            qt, gt = q_ref[rows, cols], g_ref[rows, cols]
-            shift, inverse, row_dot = [
-                stats_ref[h * 3 + k : h * 3 + k + 1, lanes] for k in range(3)
-            ]
-            weights, dscores = [], []
-            dq_t = dq_part_ref[h * width : (h + 1) * width, lanes]
-            for c, p, r in chunks:
-                s = masked_scores(c, piece[r : r + TILE, :width], qt, after)
-                dw = dot(piece[r : r + TILE, width:], gt, 1, 1)
-                bias = bias_rows(docs, p * blocks + r // BLOCK, own_docs)
-                w = chunk_terms(s, bias, shift) * inverse
-                ds = (w * (dw - row_dot)).astype(jnp.bfloat16)
-                weights.append(w.astype(jnp.bfloat16))
-                dscores.append(ds)
-                dq_t = dq_t + dot(key_t[:, r : r + TILE], ds, 1, 0)
-            if wanted == 2:
-                dq_ref[rows, cols] = jnp.transpose(dq_t * query_scaling).astype(jnp.bfloat16)
-            else:
-                dq_ref[h * width : (h + 1) * width, lanes] = dq_t
-            members.append((qt, gt, weights, dscores))
-        slots = [r for _, _, r in chunks]
-        add_key_grads(acc_ref, members, slots, [x for x in slots if x not in seen])
-        seen.update(slots)
-    if wanted == 2:
-        other = pl.ds(pl.multiple_of(length - base, length), length)
-        for h in range(QUERY_PER_KEY):
-            span = slice(h * width, (h + 1) * width)
-            whole = jnp.transpose(dq_in[span, :] * query_scaling)
-            dq_ref[other, span] = whole.astype(jnp.bfloat16)
-        grad_out[...] = acc_ref[...]
-    else:
-        index = index_ref[0]
-        _, _, even = halves(index)
-        grad = acc_ref[...]
-        grad = grad.astype(jnp.bfloat16)
-        other = inner_far_ref[...]
-        first_out[...] = jnp.where(even, other, grad)
-        second_out[...] = jnp.where(even, grad, other)
+    for half, own_ref, stats_ref, dq_part_ref, out_ref in (
+        (1 - parity, inner_ref, inner_stats, inner_dq, inner_out),
+        (parity, outer_ref, outer_stats, outer_dq, outer_out),
+    ):
+        docs = block_docs((own_ref,), length)
+        key_t = jnp.transpose(own_ref[:length, :width])
+        piece_share(
+            2, 0, half * length, docs, 0, after, key_t, q_ref, g_ref, own_ref,
+            stats_ref, dq_part_ref, dq_ref, out_ref,
+        )
+
+
+def fold_kernel(
+    last, index_ref, q_ref, g_ref, own_ref, near_ref, far_ref, part_ref,
+    near_out, far_out, dq_out, stats_ref, dq_ref, acc_ref,
+):
+    @pl.when(index_ref[0] == last)
+    def _():
+        outer_near_kernel(
+            index_ref, q_ref, g_ref, own_ref, near_ref, part_ref, near_out, dq_ref, stats_ref,
+            acc_ref,
+        )
+        outer_far_share(
+            index_ref, q_ref, g_ref, own_ref, near_ref, far_ref, stats_ref, dq_ref, dq_out, acc_ref
+        )
+        far_out[...] = acc_ref[...].astype(jnp.bfloat16)
+
+
+def near_kernel(
+    last, index_ref, q_ref, g_ref, own_ref, near_ref, part_ref, fold_near, fold_dq, fold_stats,
+    near_out, dq_out, stats_ref, acc_ref,
+):
+    @pl.when(index_ref[0] != last)
+    def _():
+        outer_near_kernel(
+            index_ref, q_ref, g_ref, own_ref, near_ref, part_ref, near_out, dq_out, stats_ref,
+            acc_ref,
+        )
+
+    @pl.when(index_ref[0] == last)
+    def _():
+        near_out[...] = fold_near[...]
+        dq_out[...] = fold_dq[...]
+        stats_ref[...] = fold_stats[...]
 
 
 def early_sum_kernel(last, index_ref, own, across, kept, out):
@@ -475,19 +564,27 @@
     (part,) = call(
         outer_stats_kernel, (rows,), (index, q, g, outer, outer_far), "outer_stats", 12
     )
-    dq, inner_own, inner_g1, inner_g2 = call(
-        inner_stage_kernel,
-        (dq_rows, wide, narrow, narrow),
-        (index, after(q, part), g, inner, inner_near, inner_far),
+    fold_near, fold_far, fold_dq, fold_stats = call(
+        lambda *refs: fold_kernel(last, *refs),
+        (narrow, narrow, dq_rows, rows),
+        (index, q, g, outer, inner, outer_far, part),
+        "fold",
+        1,
+        [pltpu.VMEM(dq_rows.shape, f32), grads],
+    )
+    inner_g1, inner_g2, inner_dq, inner_stats = call(
+        lambda *refs: inner_stage_kernel(last, *refs),
+        (narrow, narrow, dq_rows, rows),
+        (index, q, g, inner, inner_near, inner_far, fold_far),
         "inner_stage",
-        50,
-        [pltpu.VMEM((3 * length, 2 * width), f32)],
+        40,
+        [pltpu.VMEM((2 * length, 2 * width), f32)],
     )
     pair_take = lax.ppermute(inner_g1, "seq", pairs)
     outer_g1, dq_part, stats = call(
-        outer_near_kernel,
+        lambda *refs: near_kernel(last, *refs),
         (narrow, dq_rows, rows),
-        (index, after(q, dq), g, outer, outer_near, part),
+        (index, after(q, inner_g1), g, outer, outer_near, part, fold_near, fold_dq, fold_stats),
         "outer_near",
         20,
         [grads],
@@ -495,7 +592,7 @@
     turns = [(d * heads + h, d * heads + (h ^ 1)) for d in (0, last) for h in range(heads)]
     inner_a = lax.ppermute(outer_g1, ("seq", "head"), spread(across) + turns)
     dq_part, give_1, give_2 = call(
-        lambda *refs: outer_share_kernel(0, last, *refs),
+        lambda *refs: outer_far_kernel(last, *refs),
         (dq_rows, narrow, narrow),
         (index, q, g, outer, outer_near, outer_far, stats, dq_part, inner_g2),
         "outer_far",
@@ -503,14 +600,13 @@
         [grads],
     )
     take_1 = lax.ppermute(give_1, "seq", first)
-    take_2 = lax.ppermute(give_2, ("seq", "head"), spread(second + fold) + ends)
-    dq, outer_own = call(
-        lambda *refs: outer_share_kernel(2, last, *refs),
-        (like_q, wide),
-        (index, q, g, outer, outer_near, outer_far, stats, dq_part, dq),
-        "outer_own",
-        15,
-        [grads],
+    take_2 = lax.ppermute(give_2, ("seq", "head"), spread(second + fold[:1]) + ends)
+    dq, inner_own, outer_own = call(
+        own_kernel,
+        (like_q, wide, wide),
+        (index, q, g, inner, inner_stats, inner_dq, outer, stats, dq_part),
+        "own",
+        30,
     )
     (inner_own,) = call(
         lambda *refs: early_sum_kernel(last, *refs),

time: 42.2 us -> 39.1 us (0.927)
  the two profiles are of different devices: /device:TPU:24 before, /device:TPU:26 now
where the time goes in v4:
time: 39.1 us; the launch traced here: 38.9 us
  Pallas kernels  13.5 us (35%)
  waiting for transfers between devices  11.4 us (29%)
  starting transfers between devices  11 us (28%)
  local copies, waits for them, and re-layouts  1.74 us (4%)
  between operations  0.93 us (2%)
    pallas_call x8, Pallas kernels, call(): pl.pallas_call(kernel, out_shape=outs, in_specs=specs or [smem()] + [vmem...  13.5 us
    ppermute x1, waiting for transfers between devices, on_device(): take_2 = lax.ppermute(give_2, ('seq', 'head'), spread(second + fold) + ends)  7.33 us
    ppermute x2, starting transfers between devices, on_device(): take_1 = lax.ppermute(give_1, 'seq', first)  6.63 us
    ppermute x2, waiting for transfers between devices, on_device(): take_1 = lax.ppermute(give_1, 'seq', first)  3.7 us
    ppermute x1, starting transfers between devices, on_device(): lax.ppermute(give_2, ('seq', 'head'), spread(second + fold[:1]) + ends)  1.28 us
    ppermute x1, starting transfers between devices, on_device(): inner_near = lax.ppermute(outer, 'seq', pairs)  1.13 us
    dynamic_slice x2, local copies, waits for them, and re-layouts, pack_half(): lax.dynamic_slice_in_dim(x, half * length, length, 0)  1.05 us
  transfers between devices with their start and end apart: 8, of which 3 were waited for; matrix products, arithmetic and copies ran while one was open for 0% of the time, Pallas kernels for 32%

profile of v4, /device:TPU:26, one launch (start us, length us, event | category | flops | bytes accessed | tf_op | source)
XLA Modules:
  0.0 38.9 jit_solution(10257221550455486767)
XLA Ops:
  0.7 0.0 copy-start.2
  0.7 1.0 %constant_dynamic-slice_fusion.1 = (bf16[512,128]{1,0:T(8,128)(2,1)S(1)}, bf16[512,128]{1,0:T(8,128)(2,1)S(1)}) fusion(bf16[1024,128]{1,0:T(8,128)(2,1)} %param.6, s32[]{:T(128)S(6)} %select_n.44, s32[]{:T(128)S(6)} %select_n.41), kind=kLoop, calls=%fused_computation.13 | loop fusion | bytes 524296 | tf_op jit(solution)/shard_map/dynamic_slice | solution.py:36
  1.7 0.0 copy-done.2
  1.8 0.0 copy-start.3
  1.8 0.6 %copy-done.3 = s32[8]{0:T(128)S(1)} copy-done((s32[8]{0:T(128)S(1)}, s32[8]{0:T(128)}, u32[]{:S(2)}) %copy-start.3) | copy-done | bytes 56
  2.4 0.1 fusion.2
  2.5 0.2 broadcast_select_fusion.2
  2.7 0.6 %collective-permute-start.2 = (bf16[528,256]{1,0:T(8,128)(2,1)S(1)}, bf16[528,256]{1,0:T(8,128)(2,1)S(1)}, u32[]{:S(2)}, u32[]{:S(2)}) collective-permute-start(bf16[528,256]{1,0:T(8,128)(2,1)S(1)} %get-tuple-element.49), channel_id=1, source_target_pairs={{8,16},{9,17},{10,18},{11,19},{12,20},{13,21},{14,22},{15,23},{16,... | collective-permute-start | bytes 811016 | tf_op jit(solution)/shard_map/ppermute | solution.py:551
  3.3 0.4 collective-permute-start.1
  3.7 1.1 %collective-permute-start = (bf16[528,256]{1,0:T(8,128)(2,1)S(1)}, bf16[528,256]{1,0:T(8,128)(2,1)S(1)}, u32[]{:S(2)}, u32[]{:S(2)}) collective-permute-start(bf16[528,256]{1,0:T(8,128)(2,1)S(1)} %get-tuple-element.52.own_ref.refs_3_.outer_ref), channel_id=1, source_target_pairs={{0,4},{4,0},{8,12},{12,8},{16,20},{20,16},{24,28},{28,24},{1,5},{5... | collective-permute-start | bytes 811016 | tf_op jit(solution)/shard_map/ppermute | solution.py:552
  4.8 7.3 %collective-permute-done.2 = bf16[528,256]{1,0:T(8,128)(2,1)S(1)} collective-permute-done((bf16[528,256]{1,0:T(8,128)(2,1)S(1)}, bf16[528,256]{1,0:T(8,128)(2,1)S(1)}, u32[]{:S(2)}, u32[]{:S(2)}) %collective-permute-start.2) | collective-permute-done | bytes 270368 | tf_op jit(solution)/shard_map/ppermute | solution.py:551
  12.2 0.0 collective-permute-done.1
  12.2 0.7 %collective-permute-start.3 = (bf16[528,256]{1,0:T(8,128)(2,1)S(1)}, bf16[528,256]{1,0:T(8,128)(2,1)S(1)}, u32[]{:S(2)}, u32[]{:S(2)}) collective-permute-start(bf16[528,256]{1,0:T(8,128)(2,1)S(1)} %get-tuple-element.48.refs_5_), channel_id=1, source_target_pairs={{0,4},{4,0},{8,12},{12,8},{16,20},{20,16},{24,28},{28,24},{1,5},{5... | collective-permute-start | bytes 811016 | tf_op jit(solution)/shard_map/ppermute | solution.py:556
  12.9 0.0 copy-done
  12.9 1.3 %outer_stats.1.refs_6_.refs_5_ = f32[16,512]{1,0:T(8,128)S(1)} custom-call(s32[1]{0:T(128)} %bitcast.index_ref.refs_0_, bf16[1024,256]{1,0:T(8,128)(2,1)S(1)} %copy-done, bf16[1024,256]{1,0:T(8,128)(2,1)S(1)} %copy-done.1, bf16[528,256]{1,0:T(8,128)(2,1)S(1)} %get-tuple-element.52.own_ref.refs_3_.outer_ref, ...), custom_call_target="tpu_custom_call" | custom-call | flops 402653184 | bytes 1048576 | tf_op jit(solution)/shard_map/outer_stats/pallas_call | solution.py:522
  14.2 3.4 %fold.1 = (bf16[512,256]{1,0:T(8,128)(2,1)S(1)}, bf16[512,256]{1,0:T(8,128)(2,1)S(1)}, f32[256,512]{1,0:T(8,128)S(1)}, f32[16,512]{1,0:T(8,128)S(1)}) custom-call(s32[1]{0:T(128)} %bitcast.index_ref.refs_0_, bf16[1024,256]{1,0:T(8,128)(2,1)S(1)} %copy-done, bf16[1024,256]{1,0:T(8,128)(2,1)S(1)} %copy-done.1, ...), custom_call_target="tpu_custom_call" | custom-call | flops 33554432 | bytes 1048576 | tf_op jit(solution)/shard_map/fold/pallas_call | solution.py:522
  17.6 0.4 collective-permute-done.refs_4_
  18.0 4.2 %inner_stage.1 = (bf16[512,256]{1,0:T(8,128)(2,1)S(1)}, bf16[512,256]{1,0:T(8,128)(2,1)S(1)}, f32[256,512]{1,0:T(8,128)S(1)}, f32[16,512]{1,0:T(8,128)S(1)}) custom-call(s32[1]{0:T(128)} %bitcast.index_ref.refs_0_, bf16[1024,256]{1,0:T(8,128)(2,1)S(1)} %copy-done, bf16[1024,256]{1,0:T(8,128)(2,1)S(1)} %copy-done.1, ...), custom_call_target="tpu_custom_call" | custom-call | flops 1342177280 | bytes 1048576 | tf_op jit(solution)/shard_map/inner_stage/pallas_call | solution.py:522
  22.2 0.6 %collective-permute-start.5 = (bf16[512,256]{1,0:T(8,128)(2,1)S(1)}, bf16[512,256]{1,0:T(8,128)(2,1)S(1)}, u32[]{:S(2)}, u32[]{:S(2)}) collective-permute-start(bf16[512,256]{1,0:T(8,128)(2,1)S(1)} %get-tuple-element.30), channel_id=1, source_target_pairs={{0,4},{4,0},{8,12},{12,8},{16,20},{20,16},{24,28},{28,24},{1,5},{5... | collective-permute-start | bytes 786440 | tf_op jit(solution)/shard_map/ppermute | solution.py:583
  22.8 0.0 collective-permute-done.3.refs_4_
  22.8 0.1 outer_near.1
  22.9 0.1 collective-permute-start.4
  22.9 0.4 outer_far.1
  23.3 6.3 %collective-permute-start.6 = (bf16[512,256]{1,0:T(8,128)(2,1)S(1)}, bf16[512,256]{1,0:T(8,128)(2,1)S(1)}, u32[]{:S(2)}, u32[]{:S(2)}) collective-permute-start(bf16[512,256]{1,0:T(8,128)(2,1)S(1)} %get-tuple-element.43), channel_id=1, source_target_pairs={{0,8},{4,12},{8,0},{12,4},{16,24},{20,28},{24,16},{28,20},{1,9},{5... | collective-permute-start | bytes 786440 | tf_op jit(solution)/shard_map/ppermute | solution.py:602
  29.6 1.3 %collective-permute-start.7 = (bf16[512,256]{1,0:T(8,128)(2,1)S(1)}, bf16[512,256]{1,0:T(8,128)(2,1)S(1)}, u32[]{:S(2)}, u32[]{:S(2)}) collective-permute-start(bf16[512,256]{1,0:T(8,128)(2,1)S(1)} %get-tuple-element.44), channel_id=1, source_target_pairs={{8,16},{9,17},{10,18},{11,19},{12,20},{13,21},{14,22},{15,23},{16,... | collective-permute-start | bytes 786440 | tf_op jit(solution)/shard_map/ppermute | solution.py:603
  30.9 3.2 %own.1 = (bf16[1024,256]{1,0:T(8,128)(2,1)}, f32[512,256]{1,0:T(8,128)S(1)}, f32[512,256]{1,0:T(8,128)S(1)}) custom-call(s32[1]{0:T(128)} %bitcast.index_ref.refs_0_, bf16[1024,256]{1,0:T(8,128)(2,1)S(1)} %copy-done, bf16[1024,256]{1,0:T(8,128)(2,1)S(1)} %copy-done.1, bf16[528,256]{1,0:T(8,128)(2,1)S(1)} %get-tuple-element.51.refs_4_.refs_3_.inner_ref, ...), custom_call_target="tpu_custom_call" | custom-call | flops 1006632960 | bytes 1048576 | tf_op jit(solution)/shard_map/own/pallas_call | solution.py:522
  34.0 0.0 collective-permute-done.4.refs_2_
  34.0 0.1 early_sum.1.inner_own
  34.1 0.0 collective-permute-done.5.pair
  34.1 3.7 %collective-permute-done.6.first = bf16[512,256]{1,0:T(8,128)(2,1)S(1)} collective-permute-done((bf16[512,256]{1,0:T(8,128)(2,1)S(1)}, bf16[512,256]{1,0:T(8,128)(2,1)S(1)}, u32[]{:S(2)}, u32[]{:S(2)}) %collective-permute-start.6) | collective-permute-done | bytes 262176 | tf_op jit(solution)/shard_map/ppermute | solution.py:602
  37.8 0.0 collective-permute-done.7.second
  37.8 1.0 %sum.1 = (bf16[1024,128]{1,0:T(8,128)(2,1)}, bf16[1024,128]{1,0:T(8,128)(2,1)}) custom-call(s32[1]{0:T(128)} %bitcast.index_ref.refs_0_, f32[512,256]{1,0:T(8,128)S(1)} %early_sum.1.inner_own, f32[512,256]{1,0:T(8,128)S(1)} %get-tuple-element.42.outer_own, bf16[512,256]{1,0:T(8,128)(2,1)S(1)} %collective-permute-done.5.pair, ...), custom_call_target="tpu_custom_call" | custom-call | flops 33554432 | bytes 1048576 | tf_op jit(solution)/shard_map/sum/pallas_call | solution.py:522
  (7 shorter events, 0.1 us)
Async XLA Ops:
  0.7 1.1 %copy-start.2 = (bf16[1024,128]{1,0:T(8,128)(2,1)S(1)}, bf16[1024,128]{1,0:T(8,128)(2,1)}, u32[]{:S(2)}) copy-start(bf16[1024,128]{1,0:T(8,128)(2,1)} %param.7) | copy-start | bytes 786436
  1.8 0.7 %copy-start.3 = (s32[8]{0:T(128)S(1)}, s32[8]{0:T(128)}, u32[]{:S(2)}) copy-start(s32[8]{0:T(128)} %param.9) | copy-start | bytes 100
  2.7 9.4 %collective-permute-start.2 = (bf16[528,256]{1,0:T(8,128)(2,1)S(1)}, bf16[528,256]{1,0:T(8,128)(2,1)S(1)}, u32[]{:S(2)}, u32[]{:S(2)}) collective-permute-start(bf16[528,256]{1,0:T(8,128)(2,1)S(1)} %get-tuple-element.49), channel_id=1, source_target_pairs={{8,16},{9,17},{10,18},{11,19},{12,20},{13,21},{14,22},{15,23},{16,... | collective-permute-start | bytes 811016 | tf_op jit(solution)/shard_map/ppermute | solution.py:551
  3.3 8.8 %collective-permute-start.1 = (bf16[528,256]{1,0:T(8,128)(2,1)S(1)}, bf16[528,256]{1,0:T(8,128)(2,1)S(1)}, u32[]{:S(2)}, u32[]{:S(2)}) collective-permute-start(bf16[528,256]{1,0:T(8,128)(2,1)S(1)} %get-tuple-element.50), channel_id=1, source_target_pairs={{0,8},{4,12},{8,0},{12,4},{16,24},{20,28},{24,16},{28,20},{1,9},{5... | collective-permute-start | bytes 811016 | tf_op jit(solution)/shard_map/ppermute | solution.py:543
  3.7 9.2 %copy-start = (bf16[1024,256]{1,0:T(8,128)(2,1)S(1)}, bf16[1024,256]{1,0:T(8,128)(2,1)}, u32[]{:S(2)}) copy-start(bf16[1024,256]{1,0:T(8,128)(2,1)} %q_ref.3) | copy-start | bytes 1572868
  3.7 9.2 %copy-start.1 = (bf16[1024,256]{1,0:T(8,128)(2,1)S(1)}, bf16[1024,256]{1,0:T(8,128)(2,1)}, u32[]{:S(2)}) copy-start(bf16[1024,256]{1,0:T(8,128)(2,1)} %g_ref.3) | copy-start | bytes 1572868
  3.7 14.3 %collective-permute-start = (bf16[528,256]{1,0:T(8,128)(2,1)S(1)}, bf16[528,256]{1,0:T(8,128)(2,1)S(1)}, u32[]{:S(2)}, u32[]{:S(2)}) collective-permute-start(bf16[528,256]{1,0:T(8,128)(2,1)S(1)} %get-tuple-element.52.own_ref.refs_3_.outer_ref), channel_id=1, source_target_pairs={{0,4},{4,0},{8,12},{12,8},{16,20},{20,16},{24,28},{28,24},{1,5},{5... | collective-permute-start | bytes 811016 | tf_op jit(solution)/shard_map/ppermute | solution.py:552
  12.2 10.6 %collective-permute-start.3 = (bf16[528,256]{1,0:T(8,128)(2,1)S(1)}, bf16[528,256]{1,0:T(8,128)(2,1)S(1)}, u32[]{:S(2)}, u32[]{:S(2)}) collective-permute-start(bf16[528,256]{1,0:T(8,128)(2,1)S(1)} %get-tuple-element.48.refs_5_), channel_id=1, source_target_pairs={{0,4},{4,0},{8,12},{12,8},{16,20},{20,16},{24,28},{28,24},{1,5},{5... | collective-permute-start | bytes 811016 | tf_op jit(solution)/shard_map/ppermute | solution.py:556
  22.2 11.9 %collective-permute-start.5 = (bf16[512,256]{1,0:T(8,128)(2,1)S(1)}, bf16[512,256]{1,0:T(8,128)(2,1)S(1)}, u32[]{:S(2)}, u32[]{:S(2)}) collective-permute-start(bf16[512,256]{1,0:T(8,128)(2,1)S(1)} %get-tuple-element.30), channel_id=1, source_target_pairs={{0,4},{4,0},{8,12},{12,8},{16,20},{20,16},{24,28},{28,24},{1,5},{5... | collective-permute-start | bytes 786440 | tf_op jit(solution)/shard_map/ppermute | solution.py:583
  22.9 11.2 %collective-permute-start.4 = (bf16[512,256]{1,0:T(8,128)(2,1)S(1)}, bf16[512,256]{1,0:T(8,128)(2,1)S(1)}, u32[]{:S(2)}, u32[]{:S(2)}) collective-permute-start(bf16[512,256]{1,0:T(8,128)(2,1)S(1)} %get-tuple-element.41.refs_3_), channel_id=1, source_target_pairs={{4,8},{5,9},{6,10},{7,11},{8,4},{9,5},{10,6},{11,7},{12,16},{13,17... | collective-permute-start | bytes 786440 | tf_op jit(solution)/shard_map/ppermute | solution.py:593
  23.3 14.5 %collective-permute-start.6 = (bf16[512,256]{1,0:T(8,128)(2,1)S(1)}, bf16[512,256]{1,0:T(8,128)(2,1)S(1)}, u32[]{:S(2)}, u32[]{:S(2)}) collective-permute-start(bf16[512,256]{1,0:T(8,128)(2,1)S(1)} %get-tuple-element.43), channel_id=1, source_target_pairs={{0,8},{4,12},{8,0},{12,4},{16,24},{20,28},{24,16},{28,20},{1,9},{5... | collective-permute-start | bytes 786440 | tf_op jit(solution)/shard_map/ppermute | solution.py:602
  29.6 8.3 %collective-permute-start.7 = (bf16[512,256]{1,0:T(8,128)(2,1)S(1)}, bf16[512,256]{1,0:T(8,128)(2,1)S(1)}, u32[]{:S(2)}, u32[]{:S(2)}) collective-permute-start(bf16[512,256]{1,0:T(8,128)(2,1)S(1)} %get-tuple-element.44), channel_id=1, source_target_pairs={{8,16},{9,17},{10,18},{11,19},{12,20},{13,21},{14,22},{15,23},{16,... | collective-permute-start | bytes 786440 | tf_op jit(solution)/shard_map/ppermute | solution.py:603

commit v5 on v4

--- a/solution.py
+++ b/solution.py
@@ -29,17 +29,26 @@
     return 1 - parity, parity, even
 
 
-def pack_half(keys, values, starts, half, place):
+def pack_halves(keys, values, starts, parity, place):
     length = keys.shape[0] // 2
-    width = keys.shape[1]
     blocks = length // BLOCK
-    both = [lax.dynamic_slice_in_dim(x, half * length, length, 0) for x in (keys, values)]
-    starts = lax.optimization_barrier((starts, *both))[0]
-    begins = lax.dynamic_slice_in_dim(starts, half * blocks, blocks, 0)
-    first = (lax.iota(jnp.int32, blocks) == 0) & (place == 0) & (half == 0)
-    begins = jnp.pad(jnp.where(first, 1, begins).astype(jnp.bfloat16), (0, MARK - blocks))
-    marks = jnp.broadcast_to(begins[:, None], (MARK, 2 * width))
-    return jnp.concatenate([jnp.concatenate(both, axis=1), marks], axis=0)
+    halves = (1 - parity, parity)
+    parts = [
+        lax.dynamic_slice_in_dim(x, half * length, length, 0)
+        for half in halves
+        for x in (keys, values)
+    ]
+    begins = [starts[:blocks], starts[blocks:]]
+    first = (lax.iota(jnp.int32, blocks) == 0) & (place == 0)
+    begins[0] = jnp.where(first, 1, begins[0])
+    packs = []
+    for n, half in enumerate(halves):
+        rows = jnp.where(half == 0, begins[0], begins[1]).astype(jnp.bfloat16)
+        rows = jnp.pad(rows, (0, MARK - blocks))
+        marks = jnp.broadcast_to(rows[:, None], (MARK, 2 * keys.shape[1]))
+        both = jnp.concatenate(parts[2 * n : 2 * n + 2], axis=1)
+        packs.append(jnp.concatenate([both, marks], axis=0))
+    return packs
 
 
 def block_docs(pieces, length):
@@ -75,13 +84,42 @@
     return row > lax.broadcasted_iota(jnp.int32, (TILE, TILE), 1)
 
 
-def masked_scores(c, keys, qt, after):
-    s = dot(keys, qt, 1, 1)
-    if c == 0:
-        s = jnp.where(after, s, NEG)
-    if c == WINDOW // TILE:
-        s = jnp.where(after, NEG, s)
-    return s
+def spans(chunks):
+    runs = []
+    for chunk in chunks:
+        if runs and runs[-1][-1][1] == chunk[1]:
+            runs[-1].append(chunk)
+        else:
+            runs.append([chunk])
+    return runs
+
+
+def run_products(run, piece_ref, qt, gt, after):
+    width = piece_ref.shape[1] // 2
+    rows = slice(run[0][2], run[0][2] + len(run) * TILE)
+    scores = dot(piece_ref[rows, :width], qt, 1, 1)
+    dweights = dot(piece_ref[rows, width:], gt, 1, 1)
+    found = []
+    for n, (c, _, _) in enumerate(run):
+        s = scores[n * TILE : (n + 1) * TILE]
+        if c == 0:
+            s = jnp.where(after, s, NEG)
+        if c == WINDOW // TILE:
+            s = jnp.where(after, NEG, s)
+        found.append((s, dweights[n * TILE : (n + 1) * TILE]))
+    return found
+
+
+def query_share(key_t, runs, dscores):
+    total = None
+    n = 0
+    for run in runs:
+        p, r = run[0][1:]
+        ds = jnp.concatenate(dscores[n : n + len(run)], axis=0)
+        n += len(run)
+        part = dot(key_t[p][:, r : r + ds.shape[0]], ds, 1, 0)
+        total = part if total is None else total + part
+    return total
 
 
 def bias_rows(docs, first, own):
@@ -134,10 +172,9 @@
             qt, gt = q_ref[rows, cols], g_ref[rows, cols]
             for n, (piece, ref, first) in enumerate(((2, own_ref, blocks), (0, far_ref, 0))):
                 parts = []
-                for c, _, r in chunk_list(i, length, (piece,)):
-                    s = masked_scores(c, ref[r : r + TILE, :width], qt, after)
-                    dw = dot(ref[r : r + TILE, width:], gt, 1, 1)
-                    parts.append((s, dw, bias_rows(docs, first + r // BLOCK, own_docs)))
+                for run in spans(chunk_list(i, length, (piece,))):
+                    for (_, _, r), (s, dw) in zip(run, run_products(run, ref, qt, gt, after)):
+                        parts.append((s, dw, bias_rows(docs, first + r // BLOCK, own_docs)))
                 for k, value in enumerate(softmax_part(parts)):
                     at = (h * 2 + n) * 3 + k
                     stats_ref[at : at + 1, i * TILE : (i + 1) * TILE] = value
@@ -161,10 +198,9 @@
         qt, gt = q_ref[rows, cols], g_ref[rows, cols]
         own_docs = tile_docs(docs, blocks + i * (TILE // BLOCK))
         parts = []
-        for c, _, r in chunk_list(i, length, (1,)):
-            s = dot(near_ref[r : r + TILE, :width], qt, 1, 1)
-            dw = dot(near_ref[r : r + TILE, width:], gt, 1, 1)
-            parts.append((s, dw, bias_rows(docs, r // BLOCK, own_docs)))
+        for run in spans(chunk_list(i, length, (1,))):
+            for (_, _, r), (s, dw) in zip(run, run_products(run, near_ref, qt, gt, None)):
+                parts.append((s, dw, bias_rows(docs, r // BLOCK, own_docs)))
         return qt, gt, parts
 
     def shares(i, h, parts):
@@ -191,14 +227,13 @@
         for k, value in enumerate((shift, inverse, row_dot)):
             stats_ref[h * 3 + k : h * 3 + k + 1, lanes] = value
         weights, dscores = [], []
-        dq_t = jnp.zeros((width, TILE), jnp.float32)
-        for e, (s, dw, bias), (c, _, r) in zip(terms, parts, chunk_list(i, length, (1,))):
+        for e, (s, dw, bias) in zip(terms, parts):
             w = e * inverse
-            ds = (w * (dw - row_dot)).astype(jnp.bfloat16)
+            dscores.append((w * (dw - row_dot)).astype(jnp.bfloat16))
             weights.append(w.astype(jnp.bfloat16))
-            dscores.append(ds)
-            dq_t = dq_t + dot(key_t[:, r : r + TILE], ds, 1, 0)
-        dq_out[h * width : (h + 1) * width, lanes] = dq_t
+        dq_out[h * width : (h + 1) * width, lanes] = query_share(
+            {1: key_t}, spans(chunk_list(i, length, (1,))), dscores
+        )
         return weights, dscores
 
     members = []
@@ -235,10 +270,10 @@
         qt, gt = q_ref[rows, cols], g_ref[rows, cols]
         own_docs = tile_docs(docs, 2 * blocks + i * (TILE // BLOCK))
         parts = []
-        for c, p, r in chunk_list(i, length, (0, 1, 2)):
-            s = masked_scores(c, pieces[p][r : r + TILE, :width], qt, after)
-            dw = dot(pieces[p][r : r + TILE, width:], gt, 1, 1)
-            parts.append((s, dw, bias_rows(docs, p * blocks + r // BLOCK, own_docs)))
+        for run in spans(chunk_list(i, length, (0, 1, 2))):
+            found = run_products(run, pieces[run[0][1]], qt, gt, after)
+            for (_, p, r), (s, dw) in zip(run, found):
+                parts.append((s, dw, bias_rows(docs, p * blocks + r // BLOCK, own_docs)))
         return qt, gt, parts
 
     def shares(i, h, parts):
@@ -260,16 +295,15 @@
         for k, value in enumerate((shift, inverse, row_dot)):
             stats_ref[h * 3 + k : h * 3 + k + 1, lanes] = value
         weights, dscores = [], []
-        dq_t = jnp.zeros((width, TILE), jnp.float32)
         for e, (s, dw, bias), (c, p, r) in zip(terms, parts, chunk_list(i, length, (0, 1, 2))):
             if p == 2:
                 continue
             w = e * inverse
-            ds = (w * (dw - row_dot)).astype(jnp.bfloat16)
+            dscores.append((w * (dw - row_dot)).astype(jnp.bfloat16))
             weights.append(w.astype(jnp.bfloat16))
-            dscores.append(ds)
-            dq_t = dq_t + dot(key_t[p][:, r : r + TILE], ds, 1, 0)
-        dq_out[h * width : (h + 1) * width, lanes] = dq_t
+        dq_out[h * width : (h + 1) * width, lanes] = query_share(
+            key_t, spans(chunk_list(i, length, (0, 1))), dscores
+        )
         return weights, dscores
 
     seen = set()
@@ -294,18 +328,29 @@
     width = acc_ref.shape[1] // 2
     q_all = jnp.concatenate([m[0] for m in members], axis=0)
     g_all = jnp.concatenate([m[1] for m in members], axis=0)
-    for n, slot in enumerate(slots):
-        w_all = jnp.concatenate([m[2][n] for m in members], axis=1)
-        d_all = jnp.concatenate([m[3][n] for m in members], axis=1)
+    n = 0
+    while n < len(slots):
+        m = n + 1
+        while m < len(slots) and slots[m] == slots[m - 1] + TILE and m - n < 2:
+            m += 1
+        w_all, d_all = [
+            jnp.concatenate(
+                [jnp.concatenate([x[k][c] for x in members], axis=1) for c in range(n, m)], axis=0
+            )
+            for k in (2, 3)
+        ]
         dk = dot(d_all, q_all, 1, 0) * query_scaling
         dv = dot(w_all, g_all, 1, 0)
-        at = slice(slot, slot + TILE)
-        fresh = first if isinstance(first, bool) else slot in first
-        if not fresh:
-            dk = dk + acc_ref[at, :width]
-            dv = dv + acc_ref[at, width:]
-        acc_ref[at, :width] = dk
-        acc_ref[at, width:] = dv
+        for c in range(n, m):
+            at = slice(slots[c], slots[c] + TILE)
+            own = slice((c - n) * TILE, (c - n + 1) * TILE)
+            if (first is True) or (first is not False and slots[c] in first):
+                acc_ref[at, :width] = dk[own]
+                acc_ref[at, width:] = dv[own]
+            else:
+                acc_ref[at, :width] = acc_ref[at, :width] + dk[own]
+                acc_ref[at, width:] = acc_ref[at, width:] + dv[own]
+        n = m
 
 
 def outer_far_share(
@@ -358,10 +403,9 @@
         qt, gt = q_ref[rows, cols], g_ref[rows, cols]
         own_docs = tile_docs(docs, places + i * (TILE // BLOCK))
         parts = []
-        for c, _, r in chunk_list(i, length, (piece,)):
-            s = masked_scores(c, piece_ref[r : r + TILE, :width], qt, after)
-            dw = dot(piece_ref[r : r + TILE, width:], gt, 1, 1)
-            parts.append((s, dw, bias_rows(docs, first + r // BLOCK, own_docs), r))
+        for run in spans(chunk_list(i, length, (piece,))):
+            for (_, _, r), (s, dw) in zip(run, run_products(run, piece_ref, qt, gt, after)):
+                parts.append((s, dw, bias_rows(docs, first + r // BLOCK, own_docs), r))
         return qt, gt, parts
 
     seen = set()
@@ -374,13 +418,13 @@
         lanes = slice(i * TILE, (i + 1) * TILE)
         shift, inverse, row_dot = [stats_ref[h * 3 + k : h * 3 + k + 1, lanes] for k in range(3)]
         weights, dscores = [], []
-        dq_t = dq_part_ref[h * width : (h + 1) * width, lanes]
         for s, dw, bias, r in parts:
             w = chunk_terms(s, bias, shift) * inverse
-            ds = (w * (dw - row_dot)).astype(jnp.bfloat16)
+            dscores.append((w * (dw - row_dot)).astype(jnp.bfloat16))
             weights.append(w.astype(jnp.bfloat16))
-            dscores.append(ds)
-            dq_t = dq_t + dot(key_t[:, r : r + TILE], ds, 1, 0)
+        dq_t = dq_part_ref[h * width : (h + 1) * width, lanes] + query_share(
+            {piece: key_t}, spans(chunk_list(i, length, (piece,))), dscores
+        )
         if piece == 2:
             rows = pl.ds(pl.multiple_of(base + i * TILE, TILE), TILE)
             cols = slice(h * HEAD_SIZE, (h + 1) * HEAD_SIZE)
@@ -535,8 +579,7 @@
 
     place = index[0]
     parity = lax.rem(place, 2)
-    inner = pack_half(keys, values, starts, 1 - parity, place)
-    outer = pack_half(keys, values, starts, parity, place)
+    inner, outer = pack_halves(keys, values, starts, parity, place)
     give_1 = jnp.where(even, outer, inner)
     give_2 = jnp.where(even, inner, outer)
 

time: 39.1 us -> 39.1 us (level)
  waiting for transfers between devices: 11.4 us -> 12.1 us
  Pallas kernels: 13.5 us -> 13.1 us
  starting transfers between devices: 11 us -> 10.6 us
    pallas_call x8, Pallas kernels: 13.5 us -> 13.1 us  [call(): pl.pallas_call(kernel, out_shape=outs, in_specs=specs or [smem()] + [vmem...]
    dynamic_slice x2 -> x1, local copies, waits for them, and re-layouts: 1.05 us -> 1.13 us  [pack_halves(): lax.dynamic_slice_in_dim(x, half * length, length, 0)]
  transfers between devices with their start and end apart: 8 -> 8, of which waited for: 3 -> 4; matrix products, arithmetic and copies ran while one was open for 0% -> 0% of each run, Pallas kernels for 32% -> 31%
where the time goes in v5:
time: 39.1 us; the launch traced here: 38.9 us
  Pallas kernels  13.1 us (34%)
  waiting for transfers between devices  12.1 us (31%)
  starting transfers between devices  10.6 us (27%)
  local copies, waits for them, and re-layouts  1.79 us (5%)
  between operations  0.9 us (2%)
    pallas_call x8, Pallas kernels, call(): pl.pallas_call(kernel, out_shape=outs, in_specs=specs or [smem()] + [vmem...  13.1 us
    ppermute x1, waiting for transfers between devices, on_device(): take_2 = lax.ppermute(give_2, ('seq', 'head'), spread(second + fold) + ends)  7.33 us
    ppermute x2, starting transfers between devices, on_device(): take_1 = lax.ppermute(give_1, 'seq', first)  6.28 us
    ppermute x2, waiting for transfers between devices, on_device(): take_1 = lax.ppermute(give_1, 'seq', first)  4.07 us
    ppermute x1, starting transfers between devices, on_device(): lax.ppermute(give_2, ('seq', 'head'), spread(second + fold[:1]) + ends)  1.28 us
    dynamic_slice x1, local copies, waits for them, and re-layouts, pack_halves(): lax.dynamic_slice_in_dim(x, half * length, length, 0)  1.13 us
    ppermute x1, starting transfers between devices, on_device(): inner_near = lax.ppermute(outer, 'seq', pairs)  1.13 us
  transfers between devices with their start and end apart: 8, of which 4 were waited for; matrix products, arithmetic and copies ran while one was open for 0% of the time, Pallas kernels for 31%

profile of v5, /device:TPU:26, one launch (start us, length us, event | category | flops | bytes accessed | tf_op | source)
XLA Modules:
  0.0 38.9 jit_solution(7311536516580480554)
XLA Ops:
  0.7 0.0 copy-start.2
  0.7 0.6 %copy-done.2 = s32[8]{0:T(128)S(1)} copy-done((s32[8]{0:T(128)S(1)}, s32[8]{0:T(128)}, u32[]{:S(2)}) %copy-start.2) | copy-done | bytes 56
  1.3 0.1 fusion.3
  1.4 1.1 %constant_dynamic-slice_fusion = (bf16[512,128]{1,0:T(8,128)(2,1)S(1)}, bf16[512,128]{1,0:T(8,128)(2,1)S(1)}, bf16[512,128]{1,0:T(8,128)(2,1)S(1)}, bf16[512,128]{1,0:T(8,128)(2,1)S(1)}) fusion(bf16[1024,128]{1,0:T(8,128)(2,1)} %param.7, s32[]{:T(128)S(6)} %select_n.50, s32[]{:T(128)S(6)} %select_n.46, bf16[1024,128]{1,0:T(8,128)(2,1)} %param.6), kind=kLoop, calls=%fused_computation.10 | loop fusion | bytes 1048584 | tf_op jit(solution)/shard_map/dynamic_slice | solution.py:37
  2.5 0.2 broadcast_select_fusion.2
  2.8 0.6 %collective-permute-start.2 = (bf16[528,256]{1,0:T(8,128)(2,1)S(1)}, bf16[528,256]{1,0:T(8,128)(2,1)S(1)}, u32[]{:S(2)}, u32[]{:S(2)}) collective-permute-start(bf16[528,256]{1,0:T(8,128)(2,1)S(1)} %get-tuple-element.45), channel_id=1, source_target_pairs={{8,16},{9,17},{10,18},{11,19},{12,20},{13,21},{14,22},{15,23},{16,... | collective-permute-start | bytes 811016 | tf_op jit(solution)/shard_map/ppermute | solution.py:594
  3.4 0.4 collective-permute-start.1
  3.7 0.0 copy-start
  3.7 1.1 %collective-permute-start = (bf16[528,256]{1,0:T(8,128)(2,1)S(1)}, bf16[528,256]{1,0:T(8,128)(2,1)S(1)}, u32[]{:S(2)}, u32[]{:S(2)}) collective-permute-start(bf16[528,256]{1,0:T(8,128)(2,1)S(1)} %get-tuple-element.48.own_ref.refs_3_.outer_ref), channel_id=1, source_target_pairs={{0,4},{4,0},{8,12},{12,8},{16,20},{20,16},{24,28},{28,24},{1,5},{5... | collective-permute-start | bytes 811016 | tf_op jit(solution)/shard_map/ppermute | solution.py:595
  4.8 7.3 %collective-permute-done.2 = bf16[528,256]{1,0:T(8,128)(2,1)S(1)} collective-permute-done((bf16[528,256]{1,0:T(8,128)(2,1)S(1)}, bf16[528,256]{1,0:T(8,128)(2,1)S(1)}, u32[]{:S(2)}, u32[]{:S(2)}) %collective-permute-start.2) | collective-permute-done | bytes 270368 | tf_op jit(solution)/shard_map/ppermute | solution.py:594
  12.2 0.0 collective-permute-done.1
  12.2 0.7 %collective-permute-start.3 = (bf16[528,256]{1,0:T(8,128)(2,1)S(1)}, bf16[528,256]{1,0:T(8,128)(2,1)S(1)}, u32[]{:S(2)}, u32[]{:S(2)}) collective-permute-start(bf16[528,256]{1,0:T(8,128)(2,1)S(1)} %get-tuple-element.44.refs_5_), channel_id=1, source_target_pairs={{0,4},{4,0},{8,12},{12,8},{16,20},{20,16},{24,28},{28,24},{1,5},{5... | collective-permute-start | bytes 811016 | tf_op jit(solution)/shard_map/ppermute | solution.py:599
  12.9 0.0 copy-done
  12.9 0.0 copy-done.1
  12.9 1.3 %outer_stats.1.refs_6_.refs_5_ = f32[16,512]{1,0:T(8,128)S(1)} custom-call(s32[1]{0:T(128)} %bitcast.index_ref.refs_0_, bf16[1024,256]{1,0:T(8,128)(2,1)S(1)} %copy-done, bf16[1024,256]{1,0:T(8,128)(2,1)S(1)} %copy-done.1, bf16[528,256]{1,0:T(8,128)(2,1)S(1)} %get-tuple-element.48.own_ref.refs_3_.outer_ref, ...), custom_call_target="tpu_custom_call" | custom-call | flops 402653184 | bytes 1048576 | tf_op jit(solution)/shard_map/outer_stats/pallas_call | solution.py:566
  14.2 3.4 %fold.1 = (bf16[512,256]{1,0:T(8,128)(2,1)S(1)}, bf16[512,256]{1,0:T(8,128)(2,1)S(1)}, f32[256,512]{1,0:T(8,128)S(1)}, f32[16,512]{1,0:T(8,128)S(1)}) custom-call(s32[1]{0:T(128)} %bitcast.index_ref.refs_0_, bf16[1024,256]{1,0:T(8,128)(2,1)S(1)} %copy-done, bf16[1024,256]{1,0:T(8,128)(2,1)S(1)} %copy-done.1, ...), custom_call_target="tpu_custom_call" | custom-call | flops 33554432 | bytes 1048576 | tf_op jit(solution)/shard_map/fold/pallas_call | solution.py:566
  17.6 0.4 collective-permute-done.refs_4_
  18.0 3.8 %inner_stage.1 = (bf16[512,256]{1,0:T(8,128)(2,1)S(1)}, bf16[512,256]{1,0:T(8,128)(2,1)S(1)}, f32[256,512]{1,0:T(8,128)S(1)}, f32[16,512]{1,0:T(8,128)S(1)}) custom-call(s32[1]{0:T(128)} %bitcast.index_ref.refs_0_, bf16[1024,256]{1,0:T(8,128)(2,1)S(1)} %copy-done, bf16[1024,256]{1,0:T(8,128)(2,1)S(1)} %copy-done.1, ...), custom_call_target="tpu_custom_call" | custom-call | flops 1342177280 | bytes 1048576 | tf_op jit(solution)/shard_map/inner_stage/pallas_call | solution.py:566
  21.8 0.6 %collective-permute-start.5 = (bf16[512,256]{1,0:T(8,128)(2,1)S(1)}, bf16[512,256]{1,0:T(8,128)(2,1)S(1)}, u32[]{:S(2)}, u32[]{:S(2)}) collective-permute-start(bf16[512,256]{1,0:T(8,128)(2,1)S(1)} %get-tuple-element.26), channel_id=1, source_target_pairs={{0,4},{4,0},{8,12},{12,8},{16,20},{20,16},{24,28},{28,24},{1,5},{5... | collective-permute-start | bytes 786440 | tf_op jit(solution)/shard_map/ppermute | solution.py:626
  22.4 0.3 collective-permute-done.3.refs_4_
  22.7 0.1 outer_near.1
  22.8 0.1 collective-permute-start.4
  22.8 0.4 outer_far.1
  23.2 5.9 %collective-permute-start.6 = (bf16[512,256]{1,0:T(8,128)(2,1)S(1)}, bf16[512,256]{1,0:T(8,128)(2,1)S(1)}, u32[]{:S(2)}, u32[]{:S(2)}) collective-permute-start(bf16[512,256]{1,0:T(8,128)(2,1)S(1)} %get-tuple-element.39), channel_id=1, source_target_pairs={{0,8},{4,12},{8,0},{12,4},{16,24},{20,28},{24,16},{28,20},{1,9},{5... | collective-permute-start | bytes 786440 | tf_op jit(solution)/shard_map/ppermute | solution.py:645
  29.1 1.3 %collective-permute-start.7 = (bf16[512,256]{1,0:T(8,128)(2,1)S(1)}, bf16[512,256]{1,0:T(8,128)(2,1)S(1)}, u32[]{:S(2)}, u32[]{:S(2)}) collective-permute-start(bf16[512,256]{1,0:T(8,128)(2,1)S(1)} %get-tuple-element.40), channel_id=1, source_target_pairs={{8,16},{9,17},{10,18},{11,19},{12,20},{13,21},{14,22},{15,23},{16,... | collective-permute-start | bytes 786440 | tf_op jit(solution)/shard_map/ppermute | solution.py:646
  30.4 3.2 %own.1 = (bf16[1024,256]{1,0:T(8,128)(2,1)}, f32[512,256]{1,0:T(8,128)S(1)}, f32[512,256]{1,0:T(8,128)S(1)}) custom-call(s32[1]{0:T(128)} %bitcast.index_ref.refs_0_, bf16[1024,256]{1,0:T(8,128)(2,1)S(1)} %copy-done, bf16[1024,256]{1,0:T(8,128)(2,1)S(1)} %copy-done.1, bf16[528,256]{1,0:T(8,128)(2,1)S(1)} %get-tuple-element.47.refs_4_.refs_3_.inner_ref, ...), custom_call_target="tpu_custom_call" | custom-call | flops 1006632960 | bytes 1048576 | tf_op jit(solution)/shard_map/own/pallas_call | solution.py:566
  33.6 0.0 collective-permute-done.4.refs_2_
  33.6 0.1 early_sum.1.inner_own
  33.7 0.0 collective-permute-done.5.pair
  33.7 4.1 %collective-permute-done.6.first = bf16[512,256]{1,0:T(8,128)(2,1)S(1)} collective-permute-done((bf16[512,256]{1,0:T(8,128)(2,1)S(1)}, bf16[512,256]{1,0:T(8,128)(2,1)S(1)}, u32[]{:S(2)}, u32[]{:S(2)}) %collective-permute-start.6) | collective-permute-done | bytes 262176 | tf_op jit(solution)/shard_map/ppermute | solution.py:645
  37.8 0.0 collective-permute-done.7.second
  37.8 1.0 %sum.1 = (bf16[1024,128]{1,0:T(8,128)(2,1)}, bf16[1024,128]{1,0:T(8,128)(2,1)}) custom-call(s32[1]{0:T(128)} %bitcast.index_ref.refs_0_, f32[512,256]{1,0:T(8,128)S(1)} %early_sum.1.inner_own, f32[512,256]{1,0:T(8,128)S(1)} %get-tuple-element.38.outer_own, bf16[512,256]{1,0:T(8,128)(2,1)S(1)} %collective-permute-done.5.pair, ...), custom_call_target="tpu_custom_call" | custom-call | flops 33554432 | bytes 1048576 | tf_op jit(solution)/shard_map/sum/pallas_call | solution.py:566
  (3 shorter events, 0.1 us)
Async XLA Ops:
  0.7 0.7 %copy-start.2 = (s32[8]{0:T(128)S(1)}, s32[8]{0:T(128)}, u32[]{:S(2)}) copy-start(s32[8]{0:T(128)} %param.9) | copy-start | bytes 100
  2.8 9.4 %collective-permute-start.2 = (bf16[528,256]{1,0:T(8,128)(2,1)S(1)}, bf16[528,256]{1,0:T(8,128)(2,1)S(1)}, u32[]{:S(2)}, u32[]{:S(2)}) collective-permute-start(bf16[528,256]{1,0:T(8,128)(2,1)S(1)} %get-tuple-element.45), channel_id=1, source_target_pairs={{8,16},{9,17},{10,18},{11,19},{12,20},{13,21},{14,22},{15,23},{16,... | collective-permute-start | bytes 811016 | tf_op jit(solution)/shard_map/ppermute | solution.py:594
  3.4 8.8 %collective-permute-start.1 = (bf16[528,256]{1,0:T(8,128)(2,1)S(1)}, bf16[528,256]{1,0:T(8,128)(2,1)S(1)}, u32[]{:S(2)}, u32[]{:S(2)}) collective-permute-start(bf16[528,256]{1,0:T(8,128)(2,1)S(1)} %get-tuple-element.46), channel_id=1, source_target_pairs={{0,8},{4,12},{8,0},{12,4},{16,24},{20,28},{24,16},{28,20},{1,9},{5... | collective-permute-start | bytes 811016 | tf_op jit(solution)/shard_map/ppermute | solution.py:586
  3.7 9.2 %copy-start = (bf16[1024,256]{1,0:T(8,128)(2,1)S(1)}, bf16[1024,256]{1,0:T(8,128)(2,1)}, u32[]{:S(2)}) copy-start(bf16[1024,256]{1,0:T(8,128)(2,1)} %q_ref.3) | copy-start | bytes 1572868
  3.7 9.2 %copy-start.1 = (bf16[1024,256]{1,0:T(8,128)(2,1)S(1)}, bf16[1024,256]{1,0:T(8,128)(2,1)}, u32[]{:S(2)}) copy-start(bf16[1024,256]{1,0:T(8,128)(2,1)} %g_ref.3) | copy-start | bytes 1572868
  3.7 14.3 %collective-permute-start = (bf16[528,256]{1,0:T(8,128)(2,1)S(1)}, bf16[528,256]{1,0:T(8,128)(2,1)S(1)}, u32[]{:S(2)}, u32[]{:S(2)}) collective-permute-start(bf16[528,256]{1,0:T(8,128)(2,1)S(1)} %get-tuple-element.48.own_ref.refs_3_.outer_ref), channel_id=1, source_target_pairs={{0,4},{4,0},{8,12},{12,8},{16,20},{20,16},{24,28},{28,24},{1,5},{5... | collective-permute-start | bytes 811016 | tf_op jit(solution)/shard_map/ppermute | solution.py:595
  12.2 10.5 %collective-permute-start.3 = (bf16[528,256]{1,0:T(8,128)(2,1)S(1)}, bf16[528,256]{1,0:T(8,128)(2,1)S(1)}, u32[]{:S(2)}, u32[]{:S(2)}) collective-permute-start(bf16[528,256]{1,0:T(8,128)(2,1)S(1)} %get-tuple-element.44.refs_5_), channel_id=1, source_target_pairs={{0,4},{4,0},{8,12},{12,8},{16,20},{20,16},{24,28},{28,24},{1,5},{5... | collective-permute-start | bytes 811016 | tf_op jit(solution)/shard_map/ppermute | solution.py:599
  21.8 11.9 %collective-permute-start.5 = (bf16[512,256]{1,0:T(8,128)(2,1)S(1)}, bf16[512,256]{1,0:T(8,128)(2,1)S(1)}, u32[]{:S(2)}, u32[]{:S(2)}) collective-permute-start(bf16[512,256]{1,0:T(8,128)(2,1)S(1)} %get-tuple-element.26), channel_id=1, source_target_pairs={{0,4},{4,0},{8,12},{12,8},{16,20},{20,16},{24,28},{28,24},{1,5},{5... | collective-permute-start | bytes 786440 | tf_op jit(solution)/shard_map/ppermute | solution.py:626
  22.8 10.8 %collective-permute-start.4 = (bf16[512,256]{1,0:T(8,128)(2,1)S(1)}, bf16[512,256]{1,0:T(8,128)(2,1)S(1)}, u32[]{:S(2)}, u32[]{:S(2)}) collective-permute-start(bf16[512,256]{1,0:T(8,128)(2,1)S(1)} %get-tuple-element.37.refs_3_), channel_id=1, source_target_pairs={{4,8},{5,9},{6,10},{7,11},{8,4},{9,5},{10,6},{11,7},{12,16},{13,17... | collective-permute-start | bytes 786440 | tf_op jit(solution)/shard_map/ppermute | solution.py:636
  23.2 14.6 %collective-permute-start.6 = (bf16[512,256]{1,0:T(8,128)(2,1)S(1)}, bf16[512,256]{1,0:T(8,128)(2,1)S(1)}, u32[]{:S(2)}, u32[]{:S(2)}) collective-permute-start(bf16[512,256]{1,0:T(8,128)(2,1)S(1)} %get-tuple-element.39), channel_id=1, source_target_pairs={{0,8},{4,12},{8,0},{12,4},{16,24},{20,28},{24,16},{28,20},{1,9},{5... | collective-permute-start | bytes 786440 | tf_op jit(solution)/shard_map/ppermute | solution.py:645
  29.1 8.6 %collective-permute-start.7 = (bf16[512,256]{1,0:T(8,128)(2,1)S(1)}, bf16[512,256]{1,0:T(8,128)(2,1)S(1)}, u32[]{:S(2)}, u32[]{:S(2)}) collective-permute-start(bf16[512,256]{1,0:T(8,128)(2,1)S(1)} %get-tuple-element.40), channel_id=1, source_target_pairs={{8,16},{9,17},{10,18},{11,19},{12,20},{13,21},{14,22},{15,23},{16,... | collective-permute-start | bytes 786440 | tf_op jit(solution)/shard_map/ppermute | solution.py:646

commit v6 on v5

--- a/solution.py
+++ b/solution.py
@@ -157,9 +157,13 @@
     return top, total, mixed
 
 
-def outer_stats_kernel(index_ref, q_ref, g_ref, own_ref, far_ref, stats_ref):
+def outer_stats_kernel(
+    index_ref, q_ref, g_ref, own_ref, far_ref, inner_far_ref, stats_ref, far_t_ref, inner_far_t_ref
+):
     length = q_ref.shape[0] // 2
     width = own_ref.shape[1] // 2
+    far_t_ref[...] = jnp.transpose(far_ref[:length, :width])
+    inner_far_t_ref[...] = jnp.transpose(inner_far_ref[:length, :width])
     blocks = length // BLOCK
     base = lax.rem(index_ref[0], 2) * length
     docs = block_docs((far_ref, own_ref), length)
@@ -251,7 +255,7 @@
 
 
 def inner_stage_kernel(
-    last, index_ref, q_ref, g_ref, own_ref, near_ref, far_ref, fold_ref,
+    last, index_ref, q_ref, g_ref, own_ref, near_ref, far_ref, fold_ref, far_t_ref,
     near_out, far_out, dq_out, stats_ref, acc_ref,
 ):
     length = q_ref.shape[0] // 2
@@ -261,7 +265,7 @@
     pieces = (far_ref, near_ref, own_ref)
     docs = block_docs(pieces, length)
     after = triangle()
-    key_t = [jnp.transpose(pieces[p][:length, :width]) for p in (0, 1)]
+    key_t = [far_t_ref, jnp.transpose(near_ref[:length, :width])]
     steps = [(i, h) for i in range(length // TILE) for h in range(QUERY_PER_KEY)]
 
     def products(i, h):
@@ -354,13 +358,13 @@
 
 
 def outer_far_share(
-    index_ref, q_ref, g_ref, own_ref, near_ref, far_ref, stats_ref, dq_part_ref, dq_ref, acc_ref
+    index_ref, q_ref, g_ref, own_ref, near_ref, far_ref, stats_ref, dq_part_ref, dq_ref, acc_ref,
+    key_t,
 ):
     length = q_ref.shape[0] // 2
     width = own_ref.shape[1] // 2
     base = lax.rem(index_ref[0], 2) * length
     docs = block_docs((far_ref, near_ref, own_ref), length)
-    key_t = jnp.transpose(far_ref[:length, :width])
     piece_share(
         0, 0, base, docs, 2 * (length // BLOCK), triangle(), key_t, q_ref, g_ref, far_ref,
         stats_ref, dq_part_ref, dq_ref, acc_ref,
@@ -369,13 +373,13 @@
 
 def outer_far_kernel(
     last, index_ref, q_ref, g_ref, own_ref, near_ref, far_ref, stats_ref, dq_part_ref,
-    inner_far_ref, dq_ref, first_out, second_out, acc_ref,
+    inner_far_ref, far_t_ref, dq_ref, first_out, second_out, acc_ref,
 ):
     @pl.when(index_ref[0] != last)
     def _():
         outer_far_share(
             index_ref, q_ref, g_ref, own_ref, near_ref, far_ref, stats_ref, dq_part_ref, dq_ref,
-            acc_ref,
+            acc_ref, far_t_ref,
         )
 
     @pl.when(index_ref[0] == last)
@@ -460,7 +464,7 @@
 
 
 def fold_kernel(
-    last, index_ref, q_ref, g_ref, own_ref, near_ref, far_ref, part_ref,
+    last, index_ref, q_ref, g_ref, own_ref, near_ref, far_ref, part_ref, far_t_ref,
     near_out, far_out, dq_out, stats_ref, dq_ref, acc_ref,
 ):
     @pl.when(index_ref[0] == last)
@@ -470,7 +474,8 @@
             acc_ref,
         )
         outer_far_share(
-            index_ref, q_ref, g_ref, own_ref, near_ref, far_ref, stats_ref, dq_ref, dq_out, acc_ref
+            index_ref, q_ref, g_ref, own_ref, near_ref, far_ref, stats_ref, dq_ref, dq_out, acc_ref,
+            far_t_ref,
         )
         far_out[...] = acc_ref[...].astype(jnp.bfloat16)
 
@@ -604,13 +609,18 @@
     grads = pltpu.VMEM((length, 2 * width), f32)
     dq_rows = jax.ShapeDtypeStruct((QUERY_PER_KEY * width, length), f32)
 
-    (part,) = call(
-        outer_stats_kernel, (rows,), (index, q, g, outer, outer_far), "outer_stats", 12
+    turned = jax.ShapeDtypeStruct((width, length), bf16)
+    part, far_t, inner_far_t = call(
+        outer_stats_kernel,
+        (rows, turned, turned),
+        (index, q, g, outer, outer_far, inner_far),
+        "outer_stats",
+        12,
     )
     fold_near, fold_far, fold_dq, fold_stats = call(
         lambda *refs: fold_kernel(last, *refs),
         (narrow, narrow, dq_rows, rows),
-        (index, q, g, outer, inner, outer_far, part),
+        (index, q, g, outer, inner, outer_far, part, far_t),
         "fold",
         1,
         [pltpu.VMEM(dq_rows.shape, f32), grads],
@@ -618,7 +628,7 @@
     inner_g1, inner_g2, inner_dq, inner_stats = call(
         lambda *refs: inner_stage_kernel(last, *refs),
         (narrow, narrow, dq_rows, rows),
-        (index, q, g, inner, inner_near, inner_far, fold_far),
+        (index, q, g, inner, inner_near, inner_far, fold_far, inner_far_t),
         "inner_stage",
         40,
         [pltpu.VMEM((2 * length, 2 * width), f32)],
@@ -637,7 +647,7 @@
     dq_part, give_1, give_2 = call(
         lambda *refs: outer_far_kernel(last, *refs),
         (dq_rows, narrow, narrow),
-        (index, q, g, outer, outer_near, outer_far, stats, dq_part, inner_g2),
+        (index, q, g, outer, outer_near, outer_far, stats, dq_part, inner_g2, far_t),
         "outer_far",
         15,
         [grads],

time: 39.1 us -> 39.1 us (level)
  the two profiles are of different devices: /device:TPU:26 before, /device:TPU:30 now
where the time goes in v6:
time: 39.1 us; the launch traced here: 38.9 us
  Pallas kernels  13.2 us (34%)
  waiting for transfers between devices  11.9 us (30%)
  starting transfers between devices  10.7 us (27%)
  local copies, waits for them, and re-layouts  1.79 us (5%)
  between operations  0.9 us (2%)
    pallas_call x8, Pallas kernels, call(): pl.pallas_call(kernel, out_shape=outs, in_specs=specs or [smem()] + [vmem...  13.2 us
    ppermute x1, waiting for transfers between devices, on_device(): take_2 = lax.ppermute(give_2, ('seq', 'head'), spread(second + fold) + ends)  7.33 us
    ppermute x2, starting transfers between devices, on_device(): take_1 = lax.ppermute(give_1, 'seq', first)  6.37 us
    ppermute x2, waiting for transfers between devices, on_device(): take_1 = lax.ppermute(give_1, 'seq', first)  4.03 us
    ppermute x1, starting transfers between devices, on_device(): lax.ppermute(give_2, ('seq', 'head'), spread(second + fold[:1]) + ends)  1.28 us
    dynamic_slice x1, local copies, waits for them, and re-layouts, pack_halves(): lax.dynamic_slice_in_dim(x, half * length, length, 0)  1.13 us
    ppermute x1, starting transfers between devices, on_device(): inner_near = lax.ppermute(outer, 'seq', pairs)  1.13 us
  transfers between devices with their start and end apart: 8, of which 4 were waited for; matrix products, arithmetic and copies ran while one was open for 0% of the time, Pallas kernels for 31%

profile of v6, /device:TPU:30, one launch (start us, length us, event | category | flops | bytes accessed | tf_op | source)
XLA Modules:
  0.0 38.9 jit_solution(16961134694168623010)
XLA Ops:
  0.7 0.0 copy-start.2
  0.7 0.6 %copy-done.2 = s32[8]{0:T(128)S(1)} copy-done((s32[8]{0:T(128)S(1)}, s32[8]{0:T(128)}, u32[]{:S(2)}) %copy-start.2) | copy-done | bytes 56
  1.3 0.1 fusion.3
  1.4 1.1 %constant_dynamic-slice_fusion = (bf16[512,128]{1,0:T(8,128)(2,1)S(1)}, bf16[512,128]{1,0:T(8,128)(2,1)S(1)}, bf16[512,128]{1,0:T(8,128)(2,1)S(1)}, bf16[512,128]{1,0:T(8,128)(2,1)S(1)}) fusion(bf16[1024,128]{1,0:T(8,128)(2,1)} %param.7, s32[]{:T(128)S(6)} %select_n.50, s32[]{:T(128)S(6)} %select_n.46, bf16[1024,128]{1,0:T(8,128)(2,1)} %param.6), kind=kLoop, calls=%fused_computation.10 | loop fusion | bytes 1048584 | tf_op jit(solution)/shard_map/dynamic_slice | solution.py:37
  2.5 0.2 broadcast_select_fusion.2
  2.8 0.6 %collective-permute-start.2 = (bf16[528,256]{1,0:T(8,128)(2,1)S(1)}, bf16[528,256]{1,0:T(8,128)(2,1)S(1)}, u32[]{:S(2)}, u32[]{:S(2)}) collective-permute-start(bf16[528,256]{1,0:T(8,128)(2,1)S(1)} %get-tuple-element.51), channel_id=1, source_target_pairs={{8,16},{9,17},{10,18},{11,19},{12,20},{13,21},{14,22},{15,23},{16,... | collective-permute-start | bytes 811016 | tf_op jit(solution)/shard_map/ppermute | solution.py:599
  3.4 0.4 collective-permute-start.1
  3.7 0.0 copy-start.1
  3.7 1.1 %collective-permute-start = (bf16[528,256]{1,0:T(8,128)(2,1)S(1)}, bf16[528,256]{1,0:T(8,128)(2,1)S(1)}, u32[]{:S(2)}, u32[]{:S(2)}) collective-permute-start(bf16[528,256]{1,0:T(8,128)(2,1)S(1)} %get-tuple-element.54.own_ref.refs_3_.outer_ref), channel_id=1, source_target_pairs={{0,4},{4,0},{8,12},{12,8},{16,20},{20,16},{24,28},{28,24},{1,5},{5... | collective-permute-start | bytes 811016 | tf_op jit(solution)/shard_map/ppermute | solution.py:600
  4.8 7.3 %collective-permute-done.2 = bf16[528,256]{1,0:T(8,128)(2,1)S(1)} collective-permute-done((bf16[528,256]{1,0:T(8,128)(2,1)S(1)}, bf16[528,256]{1,0:T(8,128)(2,1)S(1)}, u32[]{:S(2)}, u32[]{:S(2)}) %collective-permute-start.2) | collective-permute-done | bytes 270368 | tf_op jit(solution)/shard_map/ppermute | solution.py:599
  12.2 0.0 collective-permute-done.1
  12.2 0.7 %collective-permute-start.3 = (bf16[528,256]{1,0:T(8,128)(2,1)S(1)}, bf16[528,256]{1,0:T(8,128)(2,1)S(1)}, u32[]{:S(2)}, u32[]{:S(2)}) collective-permute-start(bf16[528,256]{1,0:T(8,128)(2,1)S(1)} %get-tuple-element.50.inner_far_ref.refs_5_), channel_id=1, source_target_pairs={{0,4},{4,0},{8,12},{12,8},{16,20},{20,16},{24,28},{28,24},{1,5},{5... | collective-permute-start | bytes 811016 | tf_op jit(solution)/shard_map/ppermute | solution.py:604
  12.9 0.0 copy-done
  12.9 0.0 copy-done.1
  12.9 1.3 %outer_stats.1 = (f32[16,512]{1,0:T(8,128)S(1)}, bf16[128,512]{1,0:T(8,128)(2,1)S(1)}, bf16[128,512]{1,0:T(8,128)(2,1)S(1)}) custom-call(s32[1]{0:T(128)} %bitcast.index_ref.refs_0_, bf16[1024,256]{1,0:T(8,128)(2,1)S(1)} %copy-done, bf16[1024,256]{1,0:T(8,128)(2,1)S(1)} %copy-done.1, bf16[528,256]{1,0:T(8,128)(2,1)S(1)} %get-tuple-element.54.own_ref.refs_3_.outer_ref, ...), custom_call_target="tpu_custom_call" | custom-call | flops 402653184 | bytes 1048576 | tf_op jit(solution)/shard_map/outer_stats/pallas_call | solution.py:571
  14.2 3.4 %fold.1 = (bf16[512,256]{1,0:T(8,128)(2,1)S(1)}, bf16[512,256]{1,0:T(8,128)(2,1)S(1)}, f32[256,512]{1,0:T(8,128)S(1)}, f32[16,512]{1,0:T(8,128)S(1)}) custom-call(s32[1]{0:T(128)} %bitcast.index_ref.refs_0_, bf16[1024,256]{1,0:T(8,128)(2,1)S(1)} %copy-done, bf16[1024,256]{1,0:T(8,128)(2,1)S(1)} %copy-done.1, ...), custom_call_target="tpu_custom_call" | custom-call | flops 33554432 | bytes 1048576 | tf_op jit(solution)/shard_map/fold/pallas_call | solution.py:571
  17.6 0.4 collective-permute-done.refs_4_
  18.0 3.9 %inner_stage.1 = (bf16[512,256]{1,0:T(8,128)(2,1)S(1)}, bf16[512,256]{1,0:T(8,128)(2,1)S(1)}, f32[256,512]{1,0:T(8,128)S(1)}, f32[16,512]{1,0:T(8,128)S(1)}) custom-call(s32[1]{0:T(128)} %bitcast.index_ref.refs_0_, bf16[1024,256]{1,0:T(8,128)(2,1)S(1)} %copy-done, bf16[1024,256]{1,0:T(8,128)(2,1)S(1)} %copy-done.1, ...), custom_call_target="tpu_custom_call" | custom-call | flops 1342177280 | bytes 1048576 | tf_op jit(solution)/shard_map/inner_stage/pallas_call | solution.py:571
  21.9 0.6 %collective-permute-start.5 = (bf16[512,256]{1,0:T(8,128)(2,1)S(1)}, bf16[512,256]{1,0:T(8,128)(2,1)S(1)}, u32[]{:S(2)}, u32[]{:S(2)}) collective-permute-start(bf16[512,256]{1,0:T(8,128)(2,1)S(1)} %get-tuple-element.32), channel_id=1, source_target_pairs={{0,4},{4,0},{8,12},{12,8},{16,20},{20,16},{24,28},{28,24},{1,5},{5... | collective-permute-start | bytes 786440 | tf_op jit(solution)/shard_map/ppermute | solution.py:636
  22.5 0.2 collective-permute-done.3.refs_4_
  22.7 0.1 outer_near.1
  22.7 0.1 collective-permute-start.4
  22.8 0.4 outer_far.1
  23.2 6.0 %collective-permute-start.6 = (bf16[512,256]{1,0:T(8,128)(2,1)S(1)}, bf16[512,256]{1,0:T(8,128)(2,1)S(1)}, u32[]{:S(2)}, u32[]{:S(2)}) collective-permute-start(bf16[512,256]{1,0:T(8,128)(2,1)S(1)} %get-tuple-element.45), channel_id=1, source_target_pairs={{0,8},{4,12},{8,0},{12,4},{16,24},{20,28},{24,16},{28,20},{1,9},{5... | collective-permute-start | bytes 786440 | tf_op jit(solution)/shard_map/ppermute | solution.py:655
  29.2 1.3 %collective-permute-start.7 = (bf16[512,256]{1,0:T(8,128)(2,1)S(1)}, bf16[512,256]{1,0:T(8,128)(2,1)S(1)}, u32[]{:S(2)}, u32[]{:S(2)}) collective-permute-start(bf16[512,256]{1,0:T(8,128)(2,1)S(1)} %get-tuple-element.46), channel_id=1, source_target_pairs={{8,16},{9,17},{10,18},{11,19},{12,20},{13,21},{14,22},{15,23},{16,... | collective-permute-start | bytes 786440 | tf_op jit(solution)/shard_map/ppermute | solution.py:656
  30.5 3.2 %own.1 = (bf16[1024,256]{1,0:T(8,128)(2,1)}, f32[512,256]{1,0:T(8,128)S(1)}, f32[512,256]{1,0:T(8,128)S(1)}) custom-call(s32[1]{0:T(128)} %bitcast.index_ref.refs_0_, bf16[1024,256]{1,0:T(8,128)(2,1)S(1)} %copy-done, bf16[1024,256]{1,0:T(8,128)(2,1)S(1)} %copy-done.1, bf16[528,256]{1,0:T(8,128)(2,1)S(1)} %get-tuple-element.53.refs_4_.refs_3_.inner_ref, ...), custom_call_target="tpu_custom_call" | custom-call | flops 1006632960 | bytes 1048576 | tf_op jit(solution)/shard_map/own/pallas_call | solution.py:571
  33.6 0.0 collective-permute-done.4.refs_2_
  33.6 0.1 early_sum.1.inner_own
  33.7 0.0 collective-permute-done.5.pair
  33.7 4.0 %collective-permute-done.6.first = bf16[512,256]{1,0:T(8,128)(2,1)S(1)} collective-permute-done((bf16[512,256]{1,0:T(8,128)(2,1)S(1)}, bf16[512,256]{1,0:T(8,128)(2,1)S(1)}, u32[]{:S(2)}, u32[]{:S(2)}) %collective-permute-start.6) | collective-permute-done | bytes 262176 | tf_op jit(solution)/shard_map/ppermute | solution.py:655
  37.8 0.0 collective-permute-done.7.second
  37.8 1.0 %sum.1 = (bf16[1024,128]{1,0:T(8,128)(2,1)}, bf16[1024,128]{1,0:T(8,128)(2,1)}) custom-call(s32[1]{0:T(128)} %bitcast.index_ref.refs_0_, f32[512,256]{1,0:T(8,128)S(1)} %early_sum.1.inner_own, f32[512,256]{1,0:T(8,128)S(1)} %get-tuple-element.44.outer_own, bf16[512,256]{1,0:T(8,128)(2,1)S(1)} %collective-permute-done.5.pair, ...), custom_call_target="tpu_custom_call" | custom-call | flops 33554432 | bytes 1048576 | tf_op jit(solution)/shard_map/sum/pallas_call | solution.py:571
  (3 shorter events, 0.1 us)
Async XLA Ops:
  0.7 0.7 %copy-start.2 = (s32[8]{0:T(128)S(1)}, s32[8]{0:T(128)}, u32[]{:S(2)}) copy-start(s32[8]{0:T(128)} %param.9) | copy-start | bytes 100
  2.8 9.4 %collective-permute-start.2 = (bf16[528,256]{1,0:T(8,128)(2,1)S(1)}, bf16[528,256]{1,0:T(8,128)(2,1)S(1)}, u32[]{:S(2)}, u32[]{:S(2)}) collective-permute-start(bf16[528,256]{1,0:T(8,128)(2,1)S(1)} %get-tuple-element.51), channel_id=1, source_target_pairs={{8,16},{9,17},{10,18},{11,19},{12,20},{13,21},{14,22},{15,23},{16,... | collective-permute-start | bytes 811016 | tf_op jit(solution)/shard_map/ppermute | solution.py:599
  3.4 8.8 %collective-permute-start.1 = (bf16[528,256]{1,0:T(8,128)(2,1)S(1)}, bf16[528,256]{1,0:T(8,128)(2,1)S(1)}, u32[]{:S(2)}, u32[]{:S(2)}) collective-permute-start(bf16[528,256]{1,0:T(8,128)(2,1)S(1)} %get-tuple-element.52), channel_id=1, source_target_pairs={{0,8},{4,12},{8,0},{12,4},{16,24},{20,28},{24,16},{28,20},{1,9},{5... | collective-permute-start | bytes 811016 | tf_op jit(solution)/shard_map/ppermute | solution.py:591
  3.7 9.2 %copy-start = (bf16[1024,256]{1,0:T(8,128)(2,1)S(1)}, bf16[1024,256]{1,0:T(8,128)(2,1)}, u32[]{:S(2)}) copy-start(bf16[1024,256]{1,0:T(8,128)(2,1)} %q_ref.3) | copy-start | bytes 1572868
  3.7 9.2 %copy-start.1 = (bf16[1024,256]{1,0:T(8,128)(2,1)S(1)}, bf16[1024,256]{1,0:T(8,128)(2,1)}, u32[]{:S(2)}) copy-start(bf16[1024,256]{1,0:T(8,128)(2,1)} %g_ref.3) | copy-start | bytes 1572868
  3.7 14.3 %collective-permute-start = (bf16[528,256]{1,0:T(8,128)(2,1)S(1)}, bf16[528,256]{1,0:T(8,128)(2,1)S(1)}, u32[]{:S(2)}, u32[]{:S(2)}) collective-permute-start(bf16[528,256]{1,0:T(8,128)(2,1)S(1)} %get-tuple-element.54.own_ref.refs_3_.outer_ref), channel_id=1, source_target_pairs={{0,4},{4,0},{8,12},{12,8},{16,20},{20,16},{24,28},{28,24},{1,5},{5... | collective-permute-start | bytes 811016 | tf_op jit(solution)/shard_map/ppermute | solution.py:600
  12.2 10.4 %collective-permute-start.3 = (bf16[528,256]{1,0:T(8,128)(2,1)S(1)}, bf16[528,256]{1,0:T(8,128)(2,1)S(1)}, u32[]{:S(2)}, u32[]{:S(2)}) collective-permute-start(bf16[528,256]{1,0:T(8,128)(2,1)S(1)} %get-tuple-element.50.inner_far_ref.refs_5_), channel_id=1, source_target_pairs={{0,4},{4,0},{8,12},{12,8},{16,20},{20,16},{24,28},{28,24},{1,5},{5... | collective-permute-start | bytes 811016 | tf_op jit(solution)/shard_map/ppermute | solution.py:604
  21.9 11.9 %collective-permute-start.5 = (bf16[512,256]{1,0:T(8,128)(2,1)S(1)}, bf16[512,256]{1,0:T(8,128)(2,1)S(1)}, u32[]{:S(2)}, u32[]{:S(2)}) collective-permute-start(bf16[512,256]{1,0:T(8,128)(2,1)S(1)} %get-tuple-element.32), channel_id=1, source_target_pairs={{0,4},{4,0},{8,12},{12,8},{16,20},{20,16},{24,28},{28,24},{1,5},{5... | collective-permute-start | bytes 786440 | tf_op jit(solution)/shard_map/ppermute | solution.py:636
  22.7 10.9 %collective-permute-start.4 = (bf16[512,256]{1,0:T(8,128)(2,1)S(1)}, bf16[512,256]{1,0:T(8,128)(2,1)S(1)}, u32[]{:S(2)}, u32[]{:S(2)}) collective-permute-start(bf16[512,256]{1,0:T(8,128)(2,1)S(1)} %get-tuple-element.43.refs_3_), channel_id=1, source_target_pairs={{4,8},{5,9},{6,10},{7,11},{8,4},{9,5},{10,6},{11,7},{12,16},{13,17... | collective-permute-start | bytes 786440 | tf_op jit(solution)/shard_map/ppermute | solution.py:646
  23.2 14.6 %collective-permute-start.6 = (bf16[512,256]{1,0:T(8,128)(2,1)S(1)}, bf16[512,256]{1,0:T(8,128)(2,1)S(1)}, u32[]{:S(2)}, u32[]{:S(2)}) collective-permute-start(bf16[512,256]{1,0:T(8,128)(2,1)S(1)} %get-tuple-element.45), channel_id=1, source_target_pairs={{0,8},{4,12},{8,0},{12,4},{16,24},{20,28},{24,16},{28,20},{1,9},{5... | collective-permute-start | bytes 786440 | tf_op jit(solution)/shard_map/ppermute | solution.py:655
  29.2 8.6 %collective-permute-start.7 = (bf16[512,256]{1,0:T(8,128)(2,1)S(1)}, bf16[512,256]{1,0:T(8,128)(2,1)S(1)}, u32[]{:S(2)}, u32[]{:S(2)}) collective-permute-start(bf16[512,256]{1,0:T(8,128)(2,1)S(1)} %get-tuple-element.46), channel_id=1, source_target_pairs={{8,16},{9,17},{10,18},{11,19},{12,20},{13,21},{14,22},{15,23},{16,... | collective-permute-start | bytes 786440 | tf_op jit(solution)/shard_map/ppermute | solution.py:656
